TPU v7x, 256 devices: a whole 4x4x8 slice. The times are simulated.
256 devices in a mesh: island: 8 (over z), fsdp: 8 (over y, x_hi), dp: 4 (over x_lo, core).
Axes of the slice: x: 4 (x_hi: 2, x_lo: 2; x = x_hi * 2 + x_lo), y: 4, z: 8, core: 2. Of those that a mesh axis runs over, the one named last changes fastest.
Arguments:
- tokens: bfloat16 [196608, 4096], P(('island', 'fsdp', 'dp')), may hold values from -24 to 24
- targets: bfloat16 [196608, 1024], P(('island', 'fsdp', 'dp')), may hold values from -6 to 6
- kv_weight: float32 [4096, 1024], P(('fsdp', 'dp')), may hold values from -6 to 6
- momentum: float32 [4096, 1024], P(('fsdp', 'dp')), may hold values from -1.5 to 1.5
- first_moment: float32 [8, 4096, 1024], P('island', ('fsdp', 'dp')), may hold values from -4 to 4
- second_moment: float32 [8, 4096, 1024], P('island', ('fsdp', 'dp')), may hold values from 0.05 to 2
- step: int32 [], replicated, may hold values from 1 to 63
Outputs:
- new_weight: float32 [4096, 1024], P(('fsdp', 'dp'))
- new_momentum: float32 [4096, 1024], P(('fsdp', 'dp'))
- new_first: float32 [8, 4096, 1024], P('island', ('fsdp', 'dp'))
- new_second: float32 [8, 4096, 1024], P('island', ('fsdp', 'dp'))
All inputs are finite; a program needn't handle non-finite values.
Results may differ from a plain program's by a relative error of at most 0.024.
Values may be sent and summed in bfloat16 or wider, within the bound.
No kernel may reach another device: no remote copies, remote signals or barrier semaphores. Data moves between devices by JAX's collectives and lax.ppermute only.
A program may use at most 128 MiB of HBM per device.

v0:
```python
import jax
import jax.numpy as jnp
from jax import lax
from jax.sharding import PartitionSpec as P

WARM = 32


def outer_update(weight, momentum, mean_pseudo):
    new_momentum = 0.9 * momentum + mean_pseudo
    new_weight = weight - 0.7 * (mean_pseudo + 0.9 * new_momentum)
    return (new_weight, new_momentum)


def per_device(tokens, targets, kv_weight, momentum, first_moment, second_moment, step):
    group = lax.axis_size("fsdp") * lax.axis_size("dp")
    islands = lax.axis_size("island")
    width = tokens.shape[1]
    inv_width = 1.0 / jnp.sqrt(jnp.float32(width))
    inv_count = 1.0 / jnp.sqrt(jnp.float32(tokens.shape[0] * group))
    weight_half = kv_weight.astype(jnp.bfloat16)
    block = tokens
    proj = jnp.dot(
        block,
        lax.all_gather(weight_half, ("fsdp", "dp"), axis=0, tiled=True),
        preferred_element_type=jnp.float32,
    )
    scaled = ((proj * inv_width - targets.astype(jnp.float32)) * inv_count).astype(jnp.bfloat16)
    block = tokens
    grad = lax.psum_scatter(
        lax.dot_general(
            block, scaled, (((0,), (0,)), ((), ())), preferred_element_type=jnp.float32
        ).astype(jnp.bfloat16),
        ("fsdp", "dp"),
        scatter_dimension=0,
        tiled=True,
    ).astype(jnp.float32)
    first = first_moment[0]
    second = second_moment[0]
    new_first = 0.9 * first + 0.1 * grad
    new_second = 0.95 * second + 0.05 * grad * grad
    count = step.astype(jnp.float32)
    rate = 0.1 * jnp.minimum(count, jnp.float32(WARM)) / jnp.float32(WARM)
    first_hat = new_first / (1.0 - jnp.power(jnp.float32(0.9), count))
    second_hat = new_second / (1.0 - jnp.power(jnp.float32(0.95), count))
    update = first_hat / (jnp.sqrt(second_hat) + 1e-08)
    pseudo = rate * (update + 0.1 * kv_weight)
    total = lax.psum(pseudo.astype(jnp.bfloat16), "island").astype(jnp.float32)
    new_weight, new_momentum = outer_update(kv_weight, momentum, total / jnp.float32(islands))
    return (new_weight, new_momentum, new_first[None], new_second[None])


def solution(mesh):
    placed = (
        P(("island", "fsdp", "dp"), None),
        P(("island", "fsdp", "dp"), None),
        P(("fsdp", "dp"), None),
        P(("fsdp", "dp"), None),
        P("island", ("fsdp", "dp"), None),
        P("island", ("fsdp", "dp"), None),
        P(),
    )
    return jax.shard_map(
        per_device,
        mesh=mesh,
        in_specs=placed,
        out_specs=(
            P(("fsdp", "dp"), None),
            P(("fsdp", "dp"), None),
            P("island", ("fsdp", "dp"), None),
            P("island", ("fsdp", "dp"), None),
        ),
        check_vma=False,
    )
```

profile of v0, /device:TPU:2, one launch (start us, length us, event | category | flops | bytes accessed | tf_op | source)
XLA Modules:
  0.0 291.5 jit_solution(6245917664255193553)
XLA Ops:
  7.2 0.0 all-gather.2.cloned.1.call-start
  7.2 1.8 convert_element_type.28
  9.0 0.0 all-gather.2.cloned.1.call-update
  9.0 0.0 reduce-scatter.4.cloned.1.call-start
  9.1 62.9 %all-gather.2.cloned.1.call-done = bf16[4096,1024]{1,0:T(8,128)(2,1)} async-done(((bf16[128,1024]{1,0:T(8,128)(2,1)}), bf16[4096,1024]{1,0:T(8,128)(2,1)}) %all-gather.2.cloned.1.call-update) | async-done | bytes 8388624 | tf_op jit(solution)/shard_map/all_gather | solution.py:25
  72.0 22.8 %convert_bitcast_fusion = bf16[4096,1024]{0,1:T(8,128)(2,1)} fusion(bf16[768,4096]{1,0:T(8,128)(2,1)} %param.7, bf16[768,1024]{1,0:T(8,128)(2,1)} %param.8, bf16[4096,1024]{1,0:T(8,128)(2,1)} %all-gather.2.cloned.1.call-done), kind=kOutput, calls=%fused_computation | convolution fusion | flops 12893028352 | bytes 24641536 | tf_op jit(solution)/shard_map/dot_general | solution.py:31
  94.9 12.0 %copy.29 = bf16[4096,1024]{1,0:T(8,128)(2,1)} copy(bf16[4096,1024]{0,1:T(8,128)(2,1)} %convert_bitcast_fusion) | data formatting | bytes 16777216
  106.8 0.0 copy-start
  106.8 0.0 copy-start.1
  106.8 0.0 copy-start.2
  106.8 0.0 copy-start.3
  106.8 0.0 reduce-scatter.4.cloned.1.call-update
  106.9 0.0 all-reduce.2.cloned.1.call-start
  106.9 1.0 copy-done
  107.9 0.2 copy.24
  108.8 0.0 copy-done.1
  108.8 0.2 copy.20
  109.0 0.0 copy-done.2
  109.0 0.2 copy.21
  109.2 97.5 %reduce-scatter.4.cloned.1.call-done = bf16[128,1024]{1,0:T(8,128)(2,1)} async-done(((bf16[4096,1024]{1,0:T(8,128)(2,1)}), bf16[128,1024]{1,0:T(8,128)(2,1)}) %reduce-scatter.4.cloned.1.call-update) | async-done | bytes 262160
  206.7 1.1 copy.30
  207.8 1.1 fusion.5
  208.9 0.0 all-reduce.2.cloned.1.call-update
  209.0 0.0 copy-done.3
  209.0 0.2 copy.23
  209.2 1.0 copy.28
  210.2 1.0 copy.27
  211.2 70.7 %all-reduce.2.cloned.1.call-done = bf16[128,1024]{0,1:T(8,128)(2,1)} async-done(((bf16[128,1024]{0,1:T(8,128)(2,1)}), bf16[128,1024]{0,1:T(8,128)(2,1)}) %all-reduce.2.cloned.1.call-update) | async-done | bytes 262160 | tf_op jit(solution)/shard_map/psum | solution.py:48
  281.9 1.1 multiply_add_fusion
  283.0 1.0 copy.26
  284.0 1.0 copy.25
Async XLA Ops:
  7.2 64.8 %all-gather.2.cloned.1.call-start = ((), (), s32[]{:S(2)}) async-start(), calls=%async_computation.1 | async-start | bytes 8650752 | tf_op jit(solution)/shard_map/all_gather | solution.py:25
  9.0 197.7 %reduce-scatter.4.cloned.1.call-start = ((), (), s32[]{:S(2)}) async-start(), calls=%async_computation.3 | async-start | bytes 8650752
  106.8 1.0 copy-start
  106.8 2.0 copy-start.1
  106.8 2.2 copy-start.2
  106.8 102.1 %copy-start.3 = (f32[128,1024]{1,0:T(8,128)S(1)}, f32[128,1024]{1,0:T(8,128)}, u32[]{:S(2)}) copy-start(f32[128,1024]{1,0:T(8,128)} %param.10) | copy-start | bytes 1572868
  106.9 175.0 %all-reduce.2.cloned.1.call-start = ((), (), s32[]{:S(2)}) async-start(), calls=%async_computation.2 | async-start | bytes 524288 | tf_op jit(solution)/shard_map/psum | solution.py:48
Sparse Core Ops, SparseCore 0:
  11.1 60.8 all-gather.1
  107.0 99.6 reduce-scatter.3
  209.7 72.1 all-reduce.1
where the time goes:
time: 292 us; the launch traced here: 291 us
  waiting for transfers between devices  231 us (79%)
  matrix products  22.8 us (8%)
  local copies, waits for them, and re-layouts  18.8 us (6%)
  between operations  14.6 us (5%)
  other arithmetic  4 us (1%)
    unnamed x4, waiting for transfers between devices  97.5 us
    psum x1, waiting for transfers between devices, per_device(): total = lax.psum(pseudo.astype(jnp.bfloat16), 'island').astype(jnp.float32)  70.7 us
    all_gather x1, waiting for transfers between devices, per_device(): lax.all_gather(weight_half, ('fsdp', 'dp'), axis=0, tiled=True)  62.9 us
    dot_general x1, matrix products, per_device(): lax.dot_general(block, scaled, (((0,), (0,)), ((), ())), preferred_elemen...  22.8 us
    unnamed x18, local copies, waits for them, and re-layouts  18.8 us
  transfers between devices with their start and end apart: 3, of which 3 were waited for; matrix products, arithmetic and copies ran while one was open for 1% of the time, Pallas kernels for 0%

commit v1 on v0

v1 whole, which is shorter than its diff:
```python
import functools
import jax
import jax.numpy as jnp
from jax import lax
from jax.experimental import pallas as pl
from jax.experimental.pallas import tpu as pltpu
from jax.sharding import PartitionSpec as P

WARM = 32
NX = NY = 4
NZ = 8
NC = 1
AXES = ("island", "fsdp", "dp")
MIB = 1024 * 1024
VM = pl.BlockSpec(memory_space=pltpu.VMEM)
SM = pl.BlockSpec(memory_space=pltpu.SMEM)


def flat(z, y, x, c):
    return (z % NZ) * 32 + (y % NY) * 8 + (x % NX) * 2 + c


def send(value, where):
    pairs = [
        (flat(z, y, x, c), flat(*where(z, y, x, c)))
        for z in range(NZ)
        for y in range(NY)
        for x in range(NX)
        for c in range(2)
    ]
    return lax.ppermute(value, AXES, pairs)


def near(k):
    return lambda z, y, x, c: (z, y, x + k, c) if c == 0 else (z, y + k, x, c)


def far(k):
    return lambda z, y, x, c: (z, y + k, x, c) if c == 0 else (z, y, x + k, c)


def partner(z, y, x, c):
    return (z, y, x, 1 - c)


def shifted(z, y, x, c):
    return far(2 * (z % 2))(z, y, x, c)


def shifted_partner(z, y, x, c):
    return shifted(z, y, x, 1 - c)


def params(limit):
    return pltpu.CompilerParams(vmem_limit_bytes=limit * MIB)


def project_kernel(scales, width, at_ref, v0, vp, vm, va, vb, x, xo, t, to, s_ref, so_ref, w_ref):
    piece = width and v0.shape[0] // 8
    spans = [(v0, 0, 8), (vp, 8, 8), (vm, 16, 8), (va, 24, 4), (vb, 28, 4)]
    for ref, first, count in spans:
        for k in range(count):
            row = pl.multiple_of(at_ref[first + k] * piece, piece)
            w_ref[pl.ds(row, piece), :] = ref[k * piece : (k + 1) * piece, :]
    inv_width, inv_count = scales
    column = pl.multiple_of(at_ref[32] * width, width)

    def emit(tokens, goals, out):
        proj = jnp.dot(tokens[...], w_ref[...], preferred_element_type=jnp.float32)
        scaled = (proj * inv_width - goals.astype(jnp.float32)) * inv_count
        out[...] = scaled.T.astype(jnp.bfloat16)

    emit(x, t[:, pl.ds(column, width)], s_ref)
    emit(xo, to[...], so_ref)


def term_kernel(first, count, at_ref, s, so, x, xo, out):
    side = 256

    def step(k, carry):
        column = pl.multiple_of(at_ref[first + k] * side, side)
        total = jnp.dot(s[...], x[:, pl.ds(column, side)], preferred_element_type=jnp.float32)
        total += jnp.dot(so[...], xo[:, pl.ds(column, side)], preferred_element_type=jnp.float32)
        out[:, pl.ds(pl.multiple_of(k * side, side), side)] = total.astype(out.dtype)
        return carry

    lax.fori_loop(0, count, step, 0)


def split_kernel(core_ref, own, a, b, c, mine, theirs):
    total = own[...] + a[...].astype(jnp.float32) + b[...].astype(jnp.float32) + c[...].astype(jnp.float32)
    core = core_ref[0]
    low, high = total[:, :128], total[:, 128:]
    mine[...] = jnp.where(core == 0, low, high)
    theirs[...] = jnp.where(core == 0, high, low).astype(theirs.dtype)


def inner_kernel(core_ref, rate_ref, mine, theirs, first, second, weight, new_first, new_second, pseudo):
    core = core_ref[0]
    width = mine.shape[0]
    for grads, side in ((mine, core), (theirs, 1 - core)):
        columns = pl.ds(pl.multiple_of(side * width, width), width)
        grad = grads[...].astype(jnp.float32).T
        one = 0.9 * first[:, columns] + 0.1 * grad
        two = 0.95 * second[:, columns] + 0.05 * grad * grad
        update = (one * rate_ref[1]) / (jnp.sqrt(two * rate_ref[2]) + 1e-08)
        new_first[:, columns] = one
        new_second[:, columns] = two
        pseudo[:, columns] = (rate_ref[0] * (update + 0.1 * weight[:, columns])).astype(pseudo.dtype)


def per_device(tokens, targets, kv_weight, momentum, first_moment, second_moment, step):
    f32, bf16 = jnp.float32, jnp.bfloat16
    features = tokens.shape[1]
    columns = kv_weight.shape[1]
    half = columns // 2
    width = half // NC
    z = lax.axis_index("island")
    plane = lax.axis_index("fsdp") * 4 + lax.axis_index("dp")
    core = plane % 2
    x, y = (plane // 2) % NX, plane // 8
    odd = z % 2
    scales = (1.0 / float(features) ** 0.5, 1.0 / float(tokens.shape[0] * 32) ** 0.5)

    def chip(g, m):
        outer, inner = jnp.where(core == 0, y, x) + g, jnp.where(core == 0, x, y) + m
        outer, inner = outer % 4, inner % 4
        return jnp.where(core == 0, outer * NX + inner, inner * NX + outer)

    rows_at = [
        chip(2 * odd + g, m) * 2 + (h + core) % 2 for g in (0, 1, 3, 2) for m in range(4) for h in range(2)
    ]
    rows_at = jnp.stack(rows_at + [core]).astype(jnp.int32)
    chips_at = jnp.stack([chip(g, m) for g in (2, 1, 3, 0) for m in range(4)]).astype(jnp.int32)
    core_at = core.astype(jnp.int32).reshape(1)

    whole = kv_weight.astype(bf16)
    own_half = lax.dynamic_slice_in_dim(whole, core * half, half, 1)
    other_half = lax.dynamic_slice_in_dim(whole, (1 - core) * half, half, 1)
    back = shifted
    shard = jnp.concatenate([send(own_half, back), send(other_half, shifted_partner)], axis=0)
    tokens_other = send(tokens, partner)
    goals_other = send(lax.dynamic_slice_in_dim(targets, (1 - core) * half, half, 1), partner)

    inner = [shard] + [send(shard, near(-k)) for k in (1, 2, 3)]
    block = jnp.concatenate(inner, axis=0)
    cut = block.shape[0] // 2
    vp, vm = send(block, far(-1)), send(block, far(1))
    va = send(block[:cut], lambda z, y, x, c: (z + 1, y, x, c))
    vb = send(block[cut:], lambda z, y, x, c: (z - 1, y, x, c))

    count = tokens.shape[0]
    s, so = pl.pallas_call(
        functools.partial(project_kernel, scales, width),
        out_shape=[jax.ShapeDtypeStruct((width, count), bf16)] * 2,
        in_specs=[SM] + [VM] * 9,
        out_specs=[VM] * 2,
        scratch_shapes=[pltpu.VMEM((features, width), bf16)],
        compiler_params=params(24),
        name="project",
    )(rows_at, block, vp, vm, va, vb, tokens, tokens_other, targets, goals_other)

    def terms(first, count, dtype, name):
        return pl.pallas_call(
            functools.partial(term_kernel, first, count),
            out_shape=jax.ShapeDtypeStruct((width, count * 256), dtype),
            in_specs=[SM] + [VM] * 4,
            out_specs=VM,
            compiler_params=params(24),
            name=name,
        )(chips_at, s, so, tokens, tokens_other)

    relay = terms(0, 4, bf16, "terms_relay")
    up = terms(4, 4, bf16, "terms_up")
    down = terms(8, 4, bf16, "terms_down")
    kept = terms(12, 4, f32, "terms_kept")
    mid = relay.shape[1] // 2
    from_low = send(relay[:, :mid], far(1))
    from_high = send(relay[:, mid:], far(-1))
    up_b = send(up[:, mid:], far(1))
    down_a = send(down[:, :mid], far(-1))
    up_a = send((up[:, :mid].astype(f32) + from_low.astype(f32)).astype(bf16), far(1))
    down_b = send((down[:, mid:].astype(f32) + from_high.astype(f32)).astype(bf16), far(-1))
    low = kept[:, :mid] + up_a.astype(f32) + down_a.astype(f32)
    high = kept[:, mid:] + up_b.astype(f32) + down_b.astype(f32)
    parts = [low[:, :256], low[:, 256:], high[:, :256], high[:, 256:]]
    arrived = [send(parts[k].astype(bf16), near(k)) for k in (1, 2, 3)]
    mine, theirs = pl.pallas_call(
        split_kernel,
        out_shape=[jax.ShapeDtypeStruct((width, 128), f32), jax.ShapeDtypeStruct((width, 128), bf16)],
        in_specs=[SM] + [VM] * 4,
        out_specs=[VM] * 2,
        compiler_params=params(16),
        name="split",
    )(core_at, parts[0], *arrived)
    theirs = send(theirs, partner)

    tally = step.astype(f32)
    rate = 0.1 * jnp.minimum(tally, f32(WARM)) / f32(WARM)
    rates = jnp.stack(
        [rate, 1.0 / (1.0 - jnp.power(f32(0.9), tally)), 1.0 / (1.0 - jnp.power(f32(0.95), tally))]
    )
    state = jax.ShapeDtypeStruct(kv_weight.shape, f32)
    new_first, new_second, pseudo = pl.pallas_call(
        inner_kernel,
        out_shape=[state, state, jax.ShapeDtypeStruct(kv_weight.shape, bf16)],
        in_specs=[SM] * 2 + [VM] * 5,
        out_specs=[VM] * 3,
        compiler_params=params(16),
        name="inner_step",
    )(core_at, rates, mine, theirs, first_moment[0], second_moment[0], kv_weight)

    rows = pseudo.shape[0]
    split = lax.all_to_all(pseudo.reshape(NZ, rows // NZ, columns), "island", 0, 0, tiled=True)
    share = jnp.sum(split.astype(f32), axis=0) / f32(NZ)
    spread = jnp.broadcast_to(share.astype(bf16)[None], (NZ, rows // NZ, columns))
    mean = lax.all_to_all(spread, "island", 0, 0, tiled=True).reshape(rows, columns).astype(f32)
    new_momentum = 0.9 * momentum + mean
    new_weight = kv_weight - 0.7 * (mean + 0.9 * new_momentum)
    return (new_weight, new_momentum, new_first[None], new_second[None])


def solution(mesh):
    placed = (
        P(("island", "fsdp", "dp"), None),
        P(("island", "fsdp", "dp"), None),
        P(("fsdp", "dp"), None),
        P(("fsdp", "dp"), None),
        P("island", ("fsdp", "dp"), None),
        P("island", ("fsdp", "dp"), None),
        P(),
    )
    return jax.shard_map(
        per_device,
        mesh=mesh,
        in_specs=placed,
        out_specs=(
            P(("fsdp", "dp"), None),
            P(("fsdp", "dp"), None),
            P("island", ("fsdp", "dp"), None),
            P("island", ("fsdp", "dp"), None),
        ),
        check_vma=False,
    )
```

time: 292 us -> 151 us (0.52)
  waiting for transfers between devices: 231 us -> 44.2 us
  Pallas kernels: 0 us -> 33.8 us
  starting transfers between devices: 0.12 us -> 30.4 us
  blocking collectives: 0 us -> 29.6 us
  matrix products: 22.8 us -> 0 us
  local copies, waits for them, and re-layouts: 18.8 us -> 3.47 us
  between operations: 14.6 us -> 1.85 us
    unnamed x4 -> x0, waiting for transfers between devices: 97.5 us -> none
    psum x1 -> x0, waiting for transfers between devices: 70.7 us -> none  [per_device(): total = lax.psum(pseudo.astype(jnp.bfloat16), 'island').astype(jnp.float32)]
    all_gather x1 -> x0, waiting for transfers between devices: 62.9 us -> none  [per_device(): lax.all_gather(weight_half, ('fsdp', 'dp'), axis=0, tiled=True)]
    ppermute x0 -> x21, waiting for transfers between devices: none -> 44.2 us  [send(): return lax.ppermute(value, AXES, pairs)]
    pallas_call x0 -> x7, Pallas kernels: none -> 33.8 us  [the longest x4 20.7 us: terms(): pl.pallas_call(functools.partial(term_kernel, first, count), out_shape=ja...]
    ppermute x0 -> x21, starting transfers between devices: none -> 30.4 us  [send(): return lax.ppermute(value, AXES, pairs)]
    all_to_all x0 -> x2, blocking collectives: none -> 29.6 us  [the longest x1 14.9 us: per_device(): lax.all_to_all(pseudo.reshape(NZ, rows // NZ, columns), 'island', 0, 0, t...]
    dot_general x1 -> x0, matrix products: 22.8 us -> none  [per_device(): lax.dot_general(block, scaled, (((0,), (0,)), ((), ())), preferred_elemen...]
  transfers between devices with their start and end apart: 3 -> 21, of which waited for: 3 -> 11; matrix products, arithmetic and copies ran while one was open for 1% -> 3% of each run, Pallas kernels for 0% -> 10%
where the time goes in v1:
time: 151 us; the launch traced here: 148 us
  waiting for transfers between devices  44.2 us (29%)
  Pallas kernels  33.8 us (22%)
  starting transfers between devices  30.4 us (20%)
  blocking collectives  29.6 us (20%)
  other arithmetic  4.91 us (3%)
  local copies, waits for them, and re-layouts  3.47 us (2%)
  between operations  1.85 us (1%)
    ppermute x21, waiting for transfers between devices, send(): return lax.ppermute(value, AXES, pairs)  44.2 us
    ppermute x21, starting transfers between devices, send(): return lax.ppermute(value, AXES, pairs)  30.4 us
    pallas_call x4, Pallas kernels, terms(): pl.pallas_call(functools.partial(term_kernel, first, count), out_shape=ja...  20.7 us
    all_to_all x1, blocking collectives, per_device(): lax.all_to_all(pseudo.reshape(NZ, rows // NZ, columns), 'island', 0, 0, t...  14.9 us
    all_to_all x1, blocking collectives, per_device(): lax.all_to_all(spread, 'island', 0, 0, tiled=True).reshape(rows, columns)  14.8 us
    pallas_call x1, Pallas kernels, per_device(): pl.pallas_call(functools.partial(project_kernel, scales, width), out_shap...  11.1 us
  transfers between devices with their start and end apart: 21, of which 11 were waited for; matrix products, arithmetic and copies ran while one was open for 3% of the time, Pallas kernels for 10%

profile of v1, /device:TPU:2, one launch (start us, length us, event | category | flops | bytes accessed | tf_op | source)
XLA Modules:
  0.0 148.2 jit_solution(16070106060138064855)
XLA Ops:
  0.6 0.1 collective-permute-start.9
  0.8 1.2 convert_element_type.56
  2.0 0.7 collective-permute-start
  2.7 0.5 collective-permute-start.1
  3.1 7.9 %collective-permute-done.1 = bf16[128,512]{1,0:T(8,128)(2,1)S(1)} collective-permute-done((bf16[128,512]{1,0:T(8,128)(2,1)S(1)}, bf16[128,512]{1,0:T(8,128)(2,1)S(1)}, u32[]{:S(2)}, u32[]{:S(2)}) %collective-permute-start.1) | collective-permute-done | bytes 131104 | tf_op jit(solution)/shard_map/ppermute | solution.py:31
  11.1 2.3 %collective-permute-start.2 = (bf16[256,512]{1,0:T(8,128)(2,1)S(1)}, bf16[256,512]{1,0:T(8,128)(2,1)S(1)}, u32[]{:S(2)}, u32[]{:S(2)}) collective-permute-start(bf16[256,512]{1,0:T(8,128)(2,1)S(1)} %get-tuple-element.28), channel_id=1, source_target_pairs={{0,6},{1,25},{2,0},{3,27},{4,2},{5,29},{6,4},{7,31},{8,14},{9,1},{... | collective-permute-start | bytes 786440 | tf_op jit(solution)/shard_map/ppermute | solution.py:31
  13.4 0.7 collective-permute-start.3
  14.1 1.8 %collective-permute-start.4 = (bf16[256,512]{1,0:T(8,128)(2,1)S(1)}, bf16[256,512]{1,0:T(8,128)(2,1)S(1)}, u32[]{:S(2)}, u32[]{:S(2)}) collective-permute-start(bf16[256,512]{1,0:T(8,128)(2,1)S(1)} %get-tuple-element.28), channel_id=1, source_target_pairs={{0,2},{1,9},{2,4},{3,11},{4,6},{5,13},{6,0},{7,15},{8,10},{9,17},{... | collective-permute-start | bytes 786440 | tf_op jit(solution)/shard_map/ppermute | solution.py:31
  16.0 0.1 collective-permute-start.10
  16.1 1.4 collective-permute-done.2
  17.6 3.8 %collective-permute-done.3 = bf16[256,512]{1,0:T(8,128)(2,1)S(1)} collective-permute-done((bf16[256,512]{1,0:T(8,128)(2,1)S(1)}, bf16[256,512]{1,0:T(8,128)(2,1)S(1)}, u32[]{:S(2)}, u32[]{:S(2)}) %collective-permute-start.3) | collective-permute-done | bytes 262176 | tf_op jit(solution)/shard_map/ppermute | solution.py:31
  21.3 1.1 collective-permute-done.4
  22.5 3.1 %collective-permute-start.5 = (bf16[1024,512]{1,0:T(8,128)(2,1)S(1)}, bf16[1024,512]{1,0:T(8,128)(2,1)}, u32[]{:S(2)}, u32[]{:S(2)}) collective-permute-start(bf16[1024,512]{1,0:T(8,128)(2,1)S(1)} %constant_dynamic-update-slice_fusion.2.v0), channel_id=1, source_target_pairs={{0,24},{1,7},{2,26},{3,1},{4,28},{5,3},{6,30},{7,5},{8,0},{9,15},{... | collective-permute-start | bytes 3145736 | tf_op jit(solution)/shard_map/ppermute | solution.py:31
  25.6 0.8 pad_maximum_fusion.1
  26.4 6.9 %collective-permute-start.8 = (bf16[512,512]{1,0:T(8,128)(2,1)}, bf16[512,512]{1,0:T(8,128)(2,1)}, u32[]{:S(2)}, u32[]{:S(2)}) collective-permute-start(bf16[512,512]{1,0:T(8,128)(2,1)} %pad_maximum_fusion.1), channel_id=1, source_target_pairs={{0,224},{1,225},{2,226},{3,227},{4,228},{5,229},{6,230},{7,231},{8... | collective-permute-start | bytes 1572872 | tf_op jit(solution)/shard_map/ppermute | solution.py:31
  33.2 0.8 pad_maximum_fusion
  34.1 0.1 stack.183.at_ref
  34.2 0.1 stack.216.at_ref
  34.3 10.1 %collective-permute-done.8.vb = bf16[512,512]{1,0:T(8,128)(2,1)} collective-permute-done((bf16[512,512]{1,0:T(8,128)(2,1)}, bf16[512,512]{1,0:T(8,128)(2,1)}, u32[]{:S(2)}, u32[]{:S(2)}) %collective-permute-start.8) | collective-permute-done | bytes 524320 | tf_op jit(solution)/shard_map/ppermute | solution.py:31
  44.4 4.2 %collective-permute-done.7.va = bf16[512,512]{1,0:T(8,128)(2,1)} collective-permute-done((bf16[512,512]{1,0:T(8,128)(2,1)}, bf16[512,512]{1,0:T(8,128)(2,1)}, u32[]{:S(2)}, u32[]{:S(2)}) %collective-permute-start.7) | collective-permute-done | bytes 524320 | tf_op jit(solution)/shard_map/ppermute | solution.py:31
  48.6 2.8 %copy-done = bf16[768,4096]{1,0:T(8,128)(2,1)S(1)} copy-done((bf16[768,4096]{1,0:T(8,128)(2,1)S(1)}, bf16[768,4096]{1,0:T(8,128)(2,1)}, u32[]{:S(2)}) %copy-start) | copy-done | bytes 6291480
  51.4 11.1 %project.1 = (bf16[512,768]{1,0:T(8,128)(2,1)S(1)}, bf16[512,768]{1,0:T(8,128)(2,1)S(1)}) custom-call(s32[33]{0:T(128)S(1)} %stack.216.at_ref, bf16[1024,512]{1,0:T(8,128)(2,1)S(1)} %constant_dynamic-update-slice_fusion.2.v0, bf16[1024,512]{1,0:T(8,128)(2,1)} %collective-permute-done.5.vp, bf16[1024,512]{1,0:T(8,128)(2,1)} %collective-permute-done.6.vm, ...), custom_call_target="tpu_custom_call" | custom-call | tf_op jit(solution)/shard_map/project/pallas_call | solution.py:153
  62.5 5.2 %terms_relay.1 = bf16[512,1024]{1,0:T(8,128)(2,1)S(1)} custom-call(s32[16]{0:T(128)S(1)} %stack.183.at_ref, bf16[512,768]{1,0:T(8,128)(2,1)S(1)} %get-tuple-element.11.s, bf16[512,768]{1,0:T(8,128)(2,1)S(1)} %get-tuple-element.12.so, bf16[768,4096]{1,0:T(8,128)(2,1)S(1)} %copy-done.1, bf16[768,4096]{1,0:T(8,128)(2,1)} %collective-permute-done.9.xo), custom_call_target="tpu_custom_call" | custom-call | tf_op jit(solution)/shard_map/terms_relay/pallas_call | solution.py:164
  67.9 3.2 %collective-permute-start.16 = (bf16[512,512]{1,0:T(8,128)(2,1)S(1)}, bf16[512,512]{1,0:T(8,128)(2,1)S(1)}, u32[]{:S(2)}, u32[]{:S(2)}) collective-permute-start(bf16[512,512]{1,0:T(8,128)(2,1)S(1)} %get-tuple-element.22), channel_id=1, source_target_pairs={{0,24},{1,7},{2,26},{3,1},{4,28},{5,3},{6,30},{7,5},{8,0},{9,15},{... | collective-permute-start | bytes 1572872 | tf_op jit(solution)/shard_map/ppermute | solution.py:31
  71.1 5.2 %terms_up.1 = bf16[512,1024]{1,0:T(8,128)(2,1)S(1)} custom-call(s32[16]{0:T(128)S(1)} %stack.183.at_ref, bf16[512,768]{1,0:T(8,128)(2,1)S(1)} %get-tuple-element.11.s, bf16[512,768]{1,0:T(8,128)(2,1)S(1)} %get-tuple-element.12.so, bf16[768,4096]{1,0:T(8,128)(2,1)S(1)} %copy-done.1, bf16[768,4096]{1,0:T(8,128)(2,1)} %collective-permute-done.9.xo), custom_call_target="tpu_custom_call" | custom-call | tf_op jit(solution)/shard_map/terms_up/pallas_call | solution.py:164
  76.3 0.1 collective-permute-start.15
  76.4 5.2 %terms_down.1 = bf16[512,1024]{1,0:T(8,128)(2,1)S(1)} custom-call(s32[16]{0:T(128)S(1)} %stack.183.at_ref, bf16[512,768]{1,0:T(8,128)(2,1)S(1)} %get-tuple-element.11.s, bf16[512,768]{1,0:T(8,128)(2,1)S(1)} %get-tuple-element.12.so, bf16[768,4096]{1,0:T(8,128)(2,1)S(1)} %copy-done.1, bf16[768,4096]{1,0:T(8,128)(2,1)} %collective-permute-done.9.xo), custom_call_target="tpu_custom_call" | custom-call | tf_op jit(solution)/shard_map/terms_down/pallas_call | solution.py:164
  81.6 3.3 %collective-permute-start.13 = (bf16[512,512]{1,0:T(8,128)(2,1)S(1)}, bf16[512,512]{1,0:T(8,128)(2,1)S(1)}, u32[]{:S(2)}, u32[]{:S(2)}) collective-permute-start(bf16[512,512]{1,0:T(8,128)(2,1)S(1)} %slice.58), channel_id=1, source_target_pairs={{0,24},{1,7},{2,26},{3,1},{4,28},{5,3},{6,30},{7,5},{8,0},{9,15},{... | collective-permute-start | bytes 1572872 | tf_op jit(solution)/shard_map/ppermute | solution.py:31
  84.9 0.2 add_convert_fusion.1
  85.1 0.1 collective-permute-start.12
  85.2 0.2 add_convert_fusion
  85.4 3.3 %collective-permute-start.17 = (bf16[512,512]{1,0:T(8,128)(2,1)S(1)}, bf16[512,512]{1,0:T(8,128)(2,1)S(1)}, u32[]{:S(2)}, u32[]{:S(2)}) collective-permute-start(bf16[512,512]{1,0:T(8,128)(2,1)S(1)} %add_convert_fusion), channel_id=1, source_target_pairs={{0,24},{1,7},{2,26},{3,1},{4,28},{5,3},{6,30},{7,5},{8,0},{9,15},{... | collective-permute-start | bytes 1572872 | tf_op jit(solution)/shard_map/ppermute | solution.py:31
  88.7 5.2 %terms_kept.1 = f32[512,1024]{1,0:T(8,128)S(1)} custom-call(s32[16]{0:T(128)S(1)} %stack.183.at_ref, bf16[512,768]{1,0:T(8,128)(2,1)S(1)} %get-tuple-element.11.s, bf16[512,768]{1,0:T(8,128)(2,1)S(1)} %get-tuple-element.12.so, bf16[768,4096]{1,0:T(8,128)(2,1)S(1)} %copy-done.1, bf16[768,4096]{1,0:T(8,128)(2,1)} %collective-permute-done.9.xo), custom_call_target="tpu_custom_call" | custom-call | tf_op jit(solution)/shard_map/terms_kept/pallas_call | solution.py:164
  93.9 1.7 %collective-permute-done.12 = bf16[512,512]{1,0:T(8,128)(2,1)S(1)} collective-permute-done((bf16[512,512]{1,0:T(8,128)(2,1)S(1)}, bf16[512,512]{1,0:T(8,128)(2,1)S(1)}, u32[]{:S(2)}, u32[]{:S(2)}) %collective-permute-start.12) | collective-permute-done | bytes 524320 | tf_op jit(solution)/shard_map/ppermute | solution.py:31
  95.6 6.7 %collective-permute-done.17 = bf16[512,512]{1,0:T(8,128)(2,1)S(1)} collective-permute-done((bf16[512,512]{1,0:T(8,128)(2,1)S(1)}, bf16[512,512]{1,0:T(8,128)(2,1)S(1)}, u32[]{:S(2)}, u32[]{:S(2)}) %collective-permute-start.17) | collective-permute-done | bytes 524320 | tf_op jit(solution)/shard_map/ppermute | solution.py:31
  102.3 0.5 fusion.1
  102.9 2.0 %collective-permute-start.18 = (bf16[512,256]{1,0:T(8,128)(2,1)S(1)}, bf16[512,256]{1,0:T(8,128)(2,1)S(1)}, u32[]{:S(2)}, u32[]{:S(2)}) collective-permute-start(bf16[512,256]{1,0:T(8,128)(2,1)S(1)} %get-tuple-element.25), channel_id=1, source_target_pairs={{0,4},{1,17},{2,6},{3,19},{4,0},{5,21},{6,2},{7,23},{8,12},{9,25},... | collective-permute-start | bytes 786440 | tf_op jit(solution)/shard_map/ppermute | solution.py:31
  104.9 0.4 collective-permute-start.19
  105.3 1.7 %collective-permute-start.14 = (bf16[512,256]{1,0:T(8,128)(2,1)S(1)}, bf16[512,256]{1,0:T(8,128)(2,1)S(1)}, u32[]{:S(2)}, u32[]{:S(2)}) collective-permute-start(bf16[512,256]{1,0:T(8,128)(2,1)S(1)} %slice.78), channel_id=1, source_target_pairs={{0,2},{1,9},{2,4},{3,11},{4,6},{5,13},{6,0},{7,15},{8,10},{9,17},{... | collective-permute-start | bytes 786440 | tf_op jit(solution)/shard_map/ppermute | solution.py:31
  107.1 4.1 %collective-permute-done.18.b = bf16[512,256]{1,0:T(8,128)(2,1)S(1)} collective-permute-done((bf16[512,256]{1,0:T(8,128)(2,1)S(1)}, bf16[512,256]{1,0:T(8,128)(2,1)S(1)}, u32[]{:S(2)}, u32[]{:S(2)}) %collective-permute-start.18) | collective-permute-done | bytes 262176 | tf_op jit(solution)/shard_map/ppermute | solution.py:31
  111.2 2.7 %collective-permute-done.19.c = bf16[512,256]{1,0:T(8,128)(2,1)S(1)} collective-permute-done((bf16[512,256]{1,0:T(8,128)(2,1)S(1)}, bf16[512,256]{1,0:T(8,128)(2,1)S(1)}, u32[]{:S(2)}, u32[]{:S(2)}) %collective-permute-start.19) | collective-permute-done | bytes 262176 | tf_op jit(solution)/shard_map/ppermute | solution.py:31
  113.9 0.1 split.1
  114.0 0.1 collective-permute-start.20
  115.0 0.4 collective-permute-done.20.theirs
  115.5 2.0 %inner_step.1 = (f32[128,1024]{1,0:T(8,128)}, f32[128,1024]{1,0:T(8,128)}, bf16[128,1024]{1,0:T(8,128)(2,1)S(1)}) custom-call(s32[1]{0:T(128)} %bitcast.core_ref, f32[3]{0:T(128)S(1)} %pad_maximum_fusion.2.rate_ref, f32[512,128]{1,0:T(8,128)S(1)} %get-tuple-element.13.mine, bf16[512,128]{1,0:T(8,128)(2,1)S(1)} %collective-permute-done.20.theirs, ...), custom_call_target="tpu_custom_call" | custom-call | tf_op jit(solution)/shard_map/inner_step/pallas_call | solution.py:204
  117.4 14.9 %all_to_all.10 = bf16[8,16,1024]{2,1,0:T(8,128)(2,1)S(1)} all-to-all(bf16[8,16,1024]{2,1,0:T(8,128)(2,1)S(1)} %bitcast.64), channel_id=1, replica_groups=mesh['island'=8,'fsdp'=8,'dp'=4] {'island'}, dimensions={0} | all-to-all | bytes 524288 | tf_op jit(solution)/shard_map/all_to_all | solution.py:214
  132.4 14.8 %all_to_all.11 = bf16[8,16,1024]{2,1,0:T(8,128)(2,1)S(1)} all-to-all(bf16[8,16,1024]{2,1,0:T(8,128)(2,1)S(1)} %broadcast_in_dim.12), channel_id=1, replica_groups=mesh['island'=8,'fsdp'=8,'dp'=4] {'island'}, dimensions={0} | all-to-all | bytes 524288 | tf_op jit(solution)/shard_map/all_to_all | solution.py:217
  147.1 1.1 fusion.4
  (43 shorter events, 0.7 us)
Async XLA Ops:
  0.6 15.3 %copy-start.3 = (bf16[768,1024]{1,0:T(8,128)(2,1)S(1)}, bf16[768,1024]{1,0:T(8,128)(2,1)}, u32[]{:S(2)}) copy-start(bf16[768,1024]{1,0:T(8,128)(2,1)} %t.1) | copy-start | bytes 4718596
  0.6 48.0 %collective-permute-start.9 = (bf16[768,4096]{1,0:T(8,128)(2,1)}, bf16[768,4096]{1,0:T(8,128)(2,1)}, u32[]{:S(2)}, u32[]{:S(2)}) collective-permute-start(bf16[768,4096]{1,0:T(8,128)(2,1)} %x.9), channel_id=1, source_target_pairs={{0,1},{1,0},{2,3},{3,2},{4,5},{5,4},{6,7},{7,6},{8,9},{9,8},{10,11... | collective-permute-start | bytes 18874376 | tf_op jit(solution)/shard_map/ppermute | solution.py:31
  2.0 1.1 collective-permute-start
  2.7 8.4 %collective-permute-start.1 = (bf16[128,512]{1,0:T(8,128)(2,1)S(1)}, bf16[128,512]{1,0:T(8,128)(2,1)S(1)}, u32[]{:S(2)}, u32[]{:S(2)}) collective-permute-start(bf16[128,512]{1,0:T(8,128)(2,1)S(1)} %get-tuple-element.26), channel_id=1, source_target_pairs={{0,1},{1,0},{2,3},{3,2},{4,5},{5,4},{6,7},{7,6},{8,9},{9,8},{10,11... | collective-permute-start | bytes 393224 | tf_op jit(solution)/shard_map/ppermute | solution.py:31
  11.1 6.4 %collective-permute-start.2 = (bf16[256,512]{1,0:T(8,128)(2,1)S(1)}, bf16[256,512]{1,0:T(8,128)(2,1)S(1)}, u32[]{:S(2)}, u32[]{:S(2)}) collective-permute-start(bf16[256,512]{1,0:T(8,128)(2,1)S(1)} %get-tuple-element.28), channel_id=1, source_target_pairs={{0,6},{1,25},{2,0},{3,27},{4,2},{5,29},{6,4},{7,31},{8,14},{9,1},{... | collective-permute-start | bytes 786440 | tf_op jit(solution)/shard_map/ppermute | solution.py:31
  13.4 7.9 %collective-permute-start.3 = (bf16[256,512]{1,0:T(8,128)(2,1)S(1)}, bf16[256,512]{1,0:T(8,128)(2,1)S(1)}, u32[]{:S(2)}, u32[]{:S(2)}) collective-permute-start(bf16[256,512]{1,0:T(8,128)(2,1)S(1)} %get-tuple-element.28), channel_id=1, source_target_pairs={{0,4},{1,17},{2,6},{3,19},{4,0},{5,21},{6,2},{7,23},{8,12},{9,25},... | collective-permute-start | bytes 786440 | tf_op jit(solution)/shard_map/ppermute | solution.py:31
  14.1 8.3 %collective-permute-start.4 = (bf16[256,512]{1,0:T(8,128)(2,1)S(1)}, bf16[256,512]{1,0:T(8,128)(2,1)S(1)}, u32[]{:S(2)}, u32[]{:S(2)}) collective-permute-start(bf16[256,512]{1,0:T(8,128)(2,1)S(1)} %get-tuple-element.28), channel_id=1, source_target_pairs={{0,2},{1,9},{2,4},{3,11},{4,6},{5,13},{6,0},{7,15},{8,10},{9,17},{... | collective-permute-start | bytes 786440 | tf_op jit(solution)/shard_map/ppermute | solution.py:31
  16.0 18.1 %collective-permute-start.10 = (bf16[768,512]{1,0:T(8,128)(2,1)S(1)}, bf16[768,512]{1,0:T(8,128)(2,1)S(1)}, u32[]{:S(2)}, u32[]{:S(2)}) collective-permute-start(bf16[768,512]{1,0:T(8,128)(2,1)S(1)} %constant_dynamic-slice_fusion), channel_id=1, source_target_pairs={{0,1},{1,0},{2,3},{3,2},{4,5},{5,4},{6,7},{7,6},{8,9},{9,8},{10,11... | collective-permute-start | bytes 2359304 | tf_op jit(solution)/shard_map/ppermute | solution.py:31
  22.5 26.2 %collective-permute-start.5 = (bf16[1024,512]{1,0:T(8,128)(2,1)S(1)}, bf16[1024,512]{1,0:T(8,128)(2,1)}, u32[]{:S(2)}, u32[]{:S(2)}) collective-permute-start(bf16[1024,512]{1,0:T(8,128)(2,1)S(1)} %constant_dynamic-update-slice_fusion.2.v0), channel_id=1, source_target_pairs={{0,24},{1,7},{2,26},{3,1},{4,28},{5,3},{6,30},{7,5},{8,0},{9,15},{... | collective-permute-start | bytes 3145736 | tf_op jit(solution)/shard_map/ppermute | solution.py:31
  25.5 23.1 %collective-permute-start.6 = (bf16[1024,512]{1,0:T(8,128)(2,1)S(1)}, bf16[1024,512]{1,0:T(8,128)(2,1)}, u32[]{:S(2)}, u32[]{:S(2)}) collective-permute-start(bf16[1024,512]{1,0:T(8,128)(2,1)S(1)} %constant_dynamic-update-slice_fusion.2.v0), channel_id=1, source_target_pairs={{0,8},{1,3},{2,10},{3,5},{4,12},{5,7},{6,14},{7,1},{8,16},{9,11},{... | collective-permute-start | bytes 3145736 | tf_op jit(solution)/shard_map/ppermute | solution.py:31
  26.4 18.0 %collective-permute-start.8 = (bf16[512,512]{1,0:T(8,128)(2,1)}, bf16[512,512]{1,0:T(8,128)(2,1)}, u32[]{:S(2)}, u32[]{:S(2)}) collective-permute-start(bf16[512,512]{1,0:T(8,128)(2,1)} %pad_maximum_fusion.1), channel_id=1, source_target_pairs={{0,224},{1,225},{2,226},{3,227},{4,228},{5,229},{6,230},{7,231},{8... | collective-permute-start | bytes 1572872 | tf_op jit(solution)/shard_map/ppermute | solution.py:31
  34.1 14.6 %collective-permute-start.7 = (bf16[512,512]{1,0:T(8,128)(2,1)}, bf16[512,512]{1,0:T(8,128)(2,1)}, u32[]{:S(2)}, u32[]{:S(2)}) collective-permute-start(bf16[512,512]{1,0:T(8,128)(2,1)} %pad_maximum_fusion), channel_id=1, source_target_pairs={{0,32},{1,33},{2,34},{3,35},{4,36},{5,37},{6,38},{7,39},{8,40},{9,... | collective-permute-start | bytes 1572872 | tf_op jit(solution)/shard_map/ppermute | solution.py:31
  48.6 2.8 %copy-start = (bf16[768,4096]{1,0:T(8,128)(2,1)S(1)}, bf16[768,4096]{1,0:T(8,128)(2,1)}, u32[]{:S(2)}) copy-start(bf16[768,4096]{1,0:T(8,128)(2,1)} %x.9) | copy-start | bytes 18874372
  51.4 11.1 %copy-start.1 = (bf16[768,4096]{1,0:T(8,128)(2,1)S(1)}, bf16[768,4096]{1,0:T(8,128)(2,1)}, u32[]{:S(2)}) copy-start(bf16[768,4096]{1,0:T(8,128)(2,1)} %x.9) | copy-start | bytes 18874372
  67.8 17.2 %collective-permute-start.11 = (bf16[512,512]{1,0:T(8,128)(2,1)S(1)}, bf16[512,512]{1,0:T(8,128)(2,1)S(1)}, u32[]{:S(2)}, u32[]{:S(2)}) collective-permute-start(bf16[512,512]{1,0:T(8,128)(2,1)S(1)} %get-tuple-element.23), channel_id=1, source_target_pairs={{0,8},{1,3},{2,10},{3,5},{4,12},{5,7},{6,14},{7,1},{8,16},{9,11},{... | collective-permute-start | bytes 1572872 | tf_op jit(solution)/shard_map/ppermute | solution.py:31
  67.9 17.3 %collective-permute-start.16 = (bf16[512,512]{1,0:T(8,128)(2,1)S(1)}, bf16[512,512]{1,0:T(8,128)(2,1)S(1)}, u32[]{:S(2)}, u32[]{:S(2)}) collective-permute-start(bf16[512,512]{1,0:T(8,128)(2,1)S(1)} %get-tuple-element.22), channel_id=1, source_target_pairs={{0,24},{1,7},{2,26},{3,1},{4,28},{5,3},{6,30},{7,5},{8,0},{9,15},{... | collective-permute-start | bytes 1572872 | tf_op jit(solution)/shard_map/ppermute | solution.py:31
  76.3 17.6 %collective-permute-start.15 = (bf16[512,512]{1,0:T(8,128)(2,1)S(1)}, bf16[512,512]{1,0:T(8,128)(2,1)S(1)}, u32[]{:S(2)}, u32[]{:S(2)}) collective-permute-start(bf16[512,512]{1,0:T(8,128)(2,1)S(1)} %slice.62), channel_id=1, source_target_pairs={{0,8},{1,3},{2,10},{3,5},{4,12},{5,7},{6,14},{7,1},{8,16},{9,11},{... | collective-permute-start | bytes 1572872 | tf_op jit(solution)/shard_map/ppermute | solution.py:31
  81.6 12.2 %collective-permute-start.13 = (bf16[512,512]{1,0:T(8,128)(2,1)S(1)}, bf16[512,512]{1,0:T(8,128)(2,1)S(1)}, u32[]{:S(2)}, u32[]{:S(2)}) collective-permute-start(bf16[512,512]{1,0:T(8,128)(2,1)S(1)} %slice.58), channel_id=1, source_target_pairs={{0,24},{1,7},{2,26},{3,1},{4,28},{5,3},{6,30},{7,5},{8,0},{9,15},{... | collective-permute-start | bytes 1572872 | tf_op jit(solution)/shard_map/ppermute | solution.py:31
  85.1 10.5 %collective-permute-start.12 = (bf16[512,512]{1,0:T(8,128)(2,1)S(1)}, bf16[512,512]{1,0:T(8,128)(2,1)S(1)}, u32[]{:S(2)}, u32[]{:S(2)}) collective-permute-start(bf16[512,512]{1,0:T(8,128)(2,1)S(1)} %add_convert_fusion.1), channel_id=1, source_target_pairs={{0,8},{1,3},{2,10},{3,5},{4,12},{5,7},{6,14},{7,1},{8,16},{9,11},{... | collective-permute-start | bytes 1572872 | tf_op jit(solution)/shard_map/ppermute | solution.py:31
  85.4 16.9 %collective-permute-start.17 = (bf16[512,512]{1,0:T(8,128)(2,1)S(1)}, bf16[512,512]{1,0:T(8,128)(2,1)S(1)}, u32[]{:S(2)}, u32[]{:S(2)}) collective-permute-start(bf16[512,512]{1,0:T(8,128)(2,1)S(1)} %add_convert_fusion), channel_id=1, source_target_pairs={{0,24},{1,7},{2,26},{3,1},{4,28},{5,3},{6,30},{7,5},{8,0},{9,15},{... | collective-permute-start | bytes 1572872 | tf_op jit(solution)/shard_map/ppermute | solution.py:31
  102.8 12.7 %copy-start.2 = (f32[128,1024]{1,0:T(8,128)S(1)}, f32[128,1024]{1,0:T(8,128)}, u32[]{:S(2)}) copy-start(f32[128,1024]{1,0:T(8,128)} %weight.1) | copy-start | bytes 1572868
  102.8 12.7 %copy-start.4 = (f32[1,128,1024]{2,1,0:T(8,128)S(1)}, f32[1,128,1024]{2,1,0:T(8,128)}, u32[]{:S(2)}) copy-start(f32[1,128,1024]{2,1,0:T(8,128)} %param.11) | copy-start | bytes 1572868
  102.8 12.6 %copy-start.5 = (f32[1,128,1024]{2,1,0:T(8,128)S(1)}, f32[1,128,1024]{2,1,0:T(8,128)}, u32[]{:S(2)}) copy-start(f32[1,128,1024]{2,1,0:T(8,128)} %param.12) | copy-start | bytes 1572868
  102.9 8.3 %collective-permute-start.18 = (bf16[512,256]{1,0:T(8,128)(2,1)S(1)}, bf16[512,256]{1,0:T(8,128)(2,1)S(1)}, u32[]{:S(2)}, u32[]{:S(2)}) collective-permute-start(bf16[512,256]{1,0:T(8,128)(2,1)S(1)} %get-tuple-element.25), channel_id=1, source_target_pairs={{0,4},{1,17},{2,6},{3,19},{4,0},{5,21},{6,2},{7,23},{8,12},{9,25},... | collective-permute-start | bytes 786440 | tf_op jit(solution)/shard_map/ppermute | solution.py:31
  104.9 9.0 %collective-permute-start.19 = (bf16[512,256]{1,0:T(8,128)(2,1)S(1)}, bf16[512,256]{1,0:T(8,128)(2,1)S(1)}, u32[]{:S(2)}, u32[]{:S(2)}) collective-permute-start(bf16[512,256]{1,0:T(8,128)(2,1)S(1)} %get-tuple-element.24), channel_id=1, source_target_pairs={{0,6},{1,25},{2,0},{3,27},{4,2},{5,29},{6,4},{7,31},{8,14},{9,1},{... | collective-permute-start | bytes 786440 | tf_op jit(solution)/shard_map/ppermute | solution.py:31
  105.3 8.5 %collective-permute-start.14 = (bf16[512,256]{1,0:T(8,128)(2,1)S(1)}, bf16[512,256]{1,0:T(8,128)(2,1)S(1)}, u32[]{:S(2)}, u32[]{:S(2)}) collective-permute-start(bf16[512,256]{1,0:T(8,128)(2,1)S(1)} %slice.78), channel_id=1, source_target_pairs={{0,2},{1,9},{2,4},{3,11},{4,6},{5,13},{6,0},{7,15},{8,10},{9,17},{... | collective-permute-start | bytes 786440 | tf_op jit(solution)/shard_map/ppermute | solution.py:31
  114.0 33.1 %copy-start.6 = (f32[128,1024]{1,0:T(8,128)S(1)}, f32[128,1024]{1,0:T(8,128)}, u32[]{:S(2)}) copy-start(f32[128,1024]{1,0:T(8,128)} %param.10) | copy-start | bytes 1572868
  114.0 1.4 collective-permute-start.20

commit v2 on v1

v2 whole, which is shorter than its diff:
```python
import functools
import jax
import jax.numpy as jnp
from jax import lax
from jax.experimental import pallas as pl
from jax.experimental.pallas import tpu as pltpu
from jax.sharding import PartitionSpec as P

WARM = 32
NX = NY = 4
NZ = 8
NC = 2
BIG = (768, 4096)
SIDE = 256
LIMIT_A = 10
LIMIT_B = 8
AXES = ("island", "fsdp", "dp")
MIB = 1024 * 1024
VM = pl.BlockSpec(memory_space=pltpu.VMEM)
SM = pl.BlockSpec(memory_space=pltpu.SMEM)


def flat(z, y, x, c):
    return (z % NZ) * 32 + (y % NY) * 8 + (x % NX) * 2 + c


def send(value, where):
    pairs = [
        (flat(z, y, x, c), flat(*where(z, y, x, c)))
        for z in range(NZ)
        for y in range(NY)
        for x in range(NX)
        for c in range(2)
    ]
    return lax.ppermute(value, AXES, pairs)


def near(k):
    return lambda z, y, x, c: (z, y, x + k, c) if c == 0 else (z, y + k, x, c)


def far(k):
    return lambda z, y, x, c: (z, y + k, x, c) if c == 0 else (z, y, x + k, c)


def partner(z, y, x, c):
    return (z, y, x, 1 - c)


def params(limit):
    return pltpu.CompilerParams(vmem_limit_bytes=limit * MIB)


def here():
    fsdp, dp = lax.axis_index("fsdp"), lax.axis_index("dp")
    return lax.div(fsdp, 2), lax.rem(fsdp, 2) * 2 + lax.div(dp, 2), lax.rem(dp, 2)


def chip(place, g, m):
    y, x, core = place
    outer = lax.rem(jnp.where(core == 0, y, x) + g, 4)
    inner = lax.rem(jnp.where(core == 0, x, y) + m, 4)
    return jnp.where(core == 0, outer * NX + inner, inner * NX + outer)


def term(place, g, m, s, so, x, xo):
    columns = pl.ds(pl.multiple_of(chip(place, g, m) * SIDE, SIDE), SIDE)
    total = jnp.dot(s[...], x[:, columns], preferred_element_type=jnp.float32)
    return total + jnp.dot(so[...], xo[:, columns], preferred_element_type=jnp.float32)


def project_kernel(scales, j, v0, v1, v3, v2, x, xo, t, to, s_ref, so_ref, relay, w_ref):
    place = here()
    core = place[2]
    width = v0.shape[1]
    piece = SIDE // 2
    for g, ref in ((0, v0), (1, v1), (3, v3), (2, v2)):
        for m in range(4):
            for h in range(2):
                row = chip(place, g, m) * SIDE + lax.rem(core + h, 2) * piece
                first = m * SIDE + h * piece
                w_ref[pl.ds(pl.multiple_of(row, piece), piece), :] = ref[first : first + piece, :]
    inv_width, inv_count = scales
    column = pl.multiple_of((core * NC + j) * width, width)

    def emit(tokens, goals, out):
        proj = jnp.dot(tokens[...], w_ref[...], preferred_element_type=jnp.float32)
        scaled = (proj * inv_width - goals.astype(jnp.float32)) * inv_count
        out[...] = scaled.T.astype(jnp.bfloat16)

    emit(xo, to[:, j * width : (j + 1) * width], so_ref)
    emit(x, t[:, pl.ds(column, width)], s_ref)
    for m in range(4):
        relay[:, m * SIDE : (m + 1) * SIDE] = term(place, 2, m, s_ref, so_ref, x, xo).astype(relay.dtype)


def sides_kernel(s, so, x, xo, up, down):
    place = here()
    for g, out in ((1, up), (3, down)):
        for m in range(4):
            out[:, m * SIDE : (m + 1) * SIDE] = term(place, g, m, s, so, x, xo).astype(out.dtype)


def kept_kernel(*refs):
    x, xo, out = refs[-3:]
    place = here()
    for j in range(NC):
        s, so = refs[2 * j : 2 * j + 2]
        width = s.shape[0]
        for m in range(4):
            out[j * width : (j + 1) * width, m * SIDE : (m + 1) * SIDE] = term(place, 0, m, s, so, x, xo)


def fold_kernel(*refs):
    kept, arrived, outs = refs[0], refs[1 : 1 + 3 * NC], refs[1 + 3 * NC :]
    width = arrived[0].shape[0]
    for j in range(NC):
        rows = slice(j * width, (j + 1) * width)
        for m in range(4):
            columns = slice(m * SIDE, (m + 1) * SIDE)
            total = kept[rows, columns]
            for ref in arrived[3 * j : 3 * j + 3]:
                total += ref[:, columns].astype(jnp.float32)
            outs[m][rows, :] = total.astype(outs[m].dtype)


def split_kernel(own, a, b, c, mine, theirs):
    total = own[...] + a[...].astype(jnp.float32) + b[...].astype(jnp.float32) + c[...].astype(jnp.float32)
    core = here()[2]
    low, high = total[:, : SIDE // 2], total[:, SIDE // 2 :]
    mine[...] = jnp.where(core == 0, low, high)
    theirs[...] = jnp.where(core == 0, high, low).astype(theirs.dtype)


def inner_kernel(rate_ref, mine, theirs, first, second, weight, new_first, new_second, pseudo):
    core = here()[2]
    width = mine.shape[0]
    for grads, side in ((mine, core), (theirs, 1 - core)):
        columns = pl.ds(pl.multiple_of(side * width, width), width)
        grad = grads[...].astype(jnp.float32).T
        one = 0.9 * first[:, columns] + 0.1 * grad
        two = 0.95 * second[:, columns] + 0.05 * grad * grad
        update = (one * rate_ref[1]) / (jnp.sqrt(two * rate_ref[2]) + 1e-08)
        new_first[:, columns] = one
        new_second[:, columns] = two
        pseudo[:, columns] = (rate_ref[0] * (update + 0.1 * weight[:, columns])).astype(pseudo.dtype)


def local(kernel, shapes, limit, name, *operands, scratch=(), scalars=0):
    operands = [
        pltpu.with_memory_space_constraint(o, pltpu.VMEM) if o.shape == BIG else o for o in operands
    ]
    return pl.pallas_call(
        kernel,
        out_shape=[jax.ShapeDtypeStruct(*s) for s in shapes],
        in_specs=[SM] * scalars + [VM] * (len(operands) - scalars),
        out_specs=[VM] * len(shapes),
        scratch_shapes=list(scratch),
        compiler_params=params(limit),
        name=name,
    )(*operands)


def per_device(tokens, targets, kv_weight, momentum, first_moment, second_moment, step):
    f32, bf16 = jnp.float32, jnp.bfloat16
    count, features = tokens.shape
    rows, columns = kv_weight.shape
    half = columns // 2
    width = half // NC
    core = here()[2]
    scales = (1.0 / float(features) ** 0.5, 1.0 / float(count * 32) ** 0.5)

    whole = kv_weight.astype(bf16)
    own_half = lax.dynamic_slice_in_dim(whole, core * half, half, 1)
    other_half = lax.dynamic_slice_in_dim(whole, (1 - core) * half, half, 1)
    crossed = send(other_half, partner)
    crossed, tokens_now = lax.optimization_barrier((crossed, tokens))
    tokens_other = send(tokens_now, partner)
    shard = jnp.concatenate([own_half, crossed], axis=0)
    goals_other = send(lax.dynamic_slice_in_dim(targets, (1 - core) * half, half, 1), partner)

    inner = [shard] + [send(shard, near(-k)) for k in (1, 2, 3)]
    scaled, arrived = [], []
    for j in range(NC):
        block = jnp.concatenate([p[:, j * width : (j + 1) * width] for p in inner], axis=0)
        if j > 0:
            block, v1, v3, v2 = lax.optimization_barrier((block, v1, v3, v2))
        v1, v3, v2 = send(block, far(-1)), send(block, far(1)), send(block, far(2))
        s, so, relay = local(
            functools.partial(project_kernel, scales, j),
            [((width, count), bf16)] * 2 + [((width, 4 * SIDE), bf16)],
            LIMIT_A,
            "project",
            block, v1, v3, v2, tokens, tokens_other, targets, goals_other,
            scratch=[pltpu.VMEM((features, width), bf16)],
        )
        up, down = local(
            sides_kernel, [((width, 4 * SIDE), bf16)] * 2, LIMIT_B, "sides", s, so, tokens, tokens_other
        )
        scaled += [s, so]
        arrived += [send(relay, far(2)), send(up, far(1)), send(down, far(-1))]

    (kept,) = local(
        kept_kernel, [((half, 4 * SIDE), f32)], LIMIT_B, "kept", *scaled, tokens, tokens_other
    )
    parts = local(
        fold_kernel, [((half, SIDE), f32)] + [((half, SIDE), bf16)] * 3, LIMIT_B, "fold", kept, *arrived
    )
    mine, theirs = local(
        split_kernel,
        [((half, SIDE // 2), f32), ((half, SIDE // 2), bf16)],
        LIMIT_B,
        "split",
        parts[0], *[send(parts[k], near(k)) for k in (1, 2, 3)],
    )
    theirs = send(theirs, partner)

    tally = step.astype(f32)
    rate = 0.1 * jnp.minimum(tally, f32(WARM)) / f32(WARM)
    rates = jnp.stack(
        [rate, 1.0 / (1.0 - jnp.power(f32(0.9), tally)), 1.0 / (1.0 - jnp.power(f32(0.95), tally))]
    )
    state = (kv_weight.shape, f32)
    new_first, new_second, pseudo = local(
        inner_kernel,
        [state, state, (kv_weight.shape, bf16)],
        LIMIT_B,
        "inner_step",
        rates, mine, theirs, first_moment[0], second_moment[0], kv_weight,
        scalars=1,
    )

    split = lax.all_to_all(pseudo.reshape(NZ, rows // NZ, columns), "island", 0, 0, tiled=True)
    share = jnp.sum(split.astype(f32), axis=0) / f32(NZ)
    spread = jnp.broadcast_to(share.astype(bf16)[None], (NZ, rows // NZ, columns))
    mean = lax.all_to_all(spread, "island", 0, 0, tiled=True).reshape(rows, columns).astype(f32)
    new_momentum = 0.9 * momentum + mean
    new_weight = kv_weight - 0.7 * (mean + 0.9 * new_momentum)
    return (new_weight, new_momentum, new_first[None], new_second[None])


def solution(mesh):
    placed = (
        P(("island", "fsdp", "dp"), None),
        P(("island", "fsdp", "dp"), None),
        P(("fsdp", "dp"), None),
        P(("fsdp", "dp"), None),
        P("island", ("fsdp", "dp"), None),
        P("island", ("fsdp", "dp"), None),
        P(),
    )
    return jax.shard_map(
        per_device,
        mesh=mesh,
        in_specs=placed,
        out_specs=(
            P(("fsdp", "dp"), None),
            P(("fsdp", "dp"), None),
            P("island", ("fsdp", "dp"), None),
            P("island", ("fsdp", "dp"), None),
        ),
        check_vma=False,
    )
```

time: 151 us -> 131 us (0.87); the launches traced: 148 us -> 131 us
  Pallas kernels: 33.8 us -> 17.2 us
  blocking collectives: 29.6 us -> 33.9 us
  starting transfers between devices: 30.4 us -> 26.8 us
  other arithmetic: 4.91 us -> 2.43 us
    pallas_call x7 -> x8, Pallas kernels: 33.8 us -> 17.2 us  [local(): pl.pallas_call(kernel, out_shape=[jax.ShapeDtypeStruct(*s) for s in shape...]
    all_to_all x1, blocking collectives: 14.9 us -> 20.4 us  [per_device(): lax.all_to_all(pseudo.reshape(NZ, rows // NZ, columns), 'island', 0, 0, t...]
    ppermute x21 -> x22, starting transfers between devices: 30.4 us -> 26.8 us  [send(): return lax.ppermute(value, AXES, pairs)]
    concatenate x2 -> x4, other arithmetic: 1.65 us -> 0.11 us  [the longest x2 0.07 us: per_device(): jnp.concatenate([p[:, j * width:(j + 1) * width] for p in inner], axis=0)]
    ppermute x21 -> x22, waiting for transfers between devices: 44.2 us -> 45.4 us  [send(): return lax.ppermute(value, AXES, pairs)]
  transfers between devices with their start and end apart: 21 -> 22, of which waited for: 11 -> 12; matrix products, arithmetic and copies ran while one was open for 3% -> 1% of each run, Pallas kernels for 10% -> 11%
where the time goes in v2:
time: 131 us
  waiting for transfers between devices  45.4 us (35%)
  blocking collectives  33.9 us (26%)
  starting transfers between devices  26.8 us (20%)
  Pallas kernels  17.2 us (13%)
  local copies, waits for them, and re-layouts  2.94 us (2%)
  other arithmetic  2.43 us (2%)
  between operations  1.75 us (1%)
    ppermute x22, waiting for transfers between devices, send(): return lax.ppermute(value, AXES, pairs)  45.4 us
    ppermute x22, starting transfers between devices, send(): return lax.ppermute(value, AXES, pairs)  26.8 us
    all_to_all x1, blocking collectives, per_device(): lax.all_to_all(pseudo.reshape(NZ, rows // NZ, columns), 'island', 0, 0, t...  20.4 us
    pallas_call x8, Pallas kernels, local(): pl.pallas_call(kernel, out_shape=[jax.ShapeDtypeStruct(*s) for s in shape...  17.2 us
    all_to_all x1, blocking collectives, per_device(): lax.all_to_all(spread, 'island', 0, 0, tiled=True).reshape(rows, columns)  13.5 us
  transfers between devices with their start and end apart: 22, of which 12 were waited for; matrix products, arithmetic and copies ran while one was open for 1% of the time, Pallas kernels for 11%

profile of v2, /device:TPU:2, one launch (start us, length us, event | category | flops | bytes accessed | tf_op | source)
XLA Modules:
  0.0 130.5 jit_solution(288625954196639368)
XLA Ops:
  0.6 1.1 convert_element_type.23
  1.8 0.1 collective-permute-start
  1.9 1.3 %collective-permute-done = bf16[128,512]{1,0:T(8,128)(2,1)S(1)} collective-permute-done((bf16[128,512]{1,0:T(8,128)(2,1)S(1)}, bf16[128,512]{1,0:T(8,128)(2,1)S(1)}, u32[]{:S(2)}, u32[]{:S(2)}) %collective-permute-start) | collective-permute-done | bytes 131104 | tf_op jit(solution)/shard_map/ppermute | solution.py:35
  3.2 0.1 collective-permute-start.7
  3.4 1.6 %collective-permute-start.3 = (bf16[256,512]{1,0:T(8,128)(2,1)S(1)}, bf16[256,512]{1,0:T(8,128)(2,1)S(1)}, u32[]{:S(2)}, u32[]{:S(2)}) collective-permute-start(bf16[256,512]{1,0:T(8,128)(2,1)S(1)} %pad_maximum_fusion.2), channel_id=1, source_target_pairs={{0,2},{1,9},{2,4},{3,11},{4,6},{5,13},{6,0},{7,15},{8,10},{9,17},{... | collective-permute-start | bytes 786440 | tf_op jit(solution)/shard_map/ppermute | solution.py:35
  4.9 1.4 %constant_dynamic-slice_fusion = bf16[768,512]{1,0:T(8,128)(2,1)S(1)} fusion(bf16[768,1024]{1,0:T(8,128)(2,1)} %t.3, s32[]{:T(128)S(6)} %select_n.8), kind=kLoop, calls=%fused_computation.15 | loop fusion | bytes 1572868 | tf_op jit(solution)/shard_map/dynamic_slice | solution.py:180
  6.3 0.4 collective-permute-start.8
  6.8 2.4 %collective-permute-start.2 = (bf16[256,512]{1,0:T(8,128)(2,1)S(1)}, bf16[256,512]{1,0:T(8,128)(2,1)S(1)}, u32[]{:S(2)}, u32[]{:S(2)}) collective-permute-start(bf16[256,512]{1,0:T(8,128)(2,1)S(1)} %pad_maximum_fusion.2), channel_id=1, source_target_pairs={{0,4},{1,17},{2,6},{3,19},{4,0},{5,21},{6,2},{7,23},{8,12},{9,25},... | collective-permute-start | bytes 786440 | tf_op jit(solution)/shard_map/ppermute | solution.py:35
  9.2 1.2 collective-permute-start.1
  10.4 4.4 %collective-permute-done.2 = bf16[256,512]{1,0:T(8,128)(2,1)S(1)} collective-permute-done((bf16[256,512]{1,0:T(8,128)(2,1)S(1)}, bf16[256,512]{1,0:T(8,128)(2,1)S(1)}, u32[]{:S(2)}, u32[]{:S(2)}) %collective-permute-start.2) | collective-permute-done | bytes 262176 | tf_op jit(solution)/shard_map/ppermute | solution.py:35
  14.8 2.7 %collective-permute-done.1 = bf16[256,512]{1,0:T(8,128)(2,1)S(1)} collective-permute-done((bf16[256,512]{1,0:T(8,128)(2,1)S(1)}, bf16[256,512]{1,0:T(8,128)(2,1)S(1)}, u32[]{:S(2)}, u32[]{:S(2)}) %collective-permute-start.1) | collective-permute-done | bytes 262176 | tf_op jit(solution)/shard_map/ppermute | solution.py:35
  17.5 2.5 %collective-permute-start.4 = (bf16[1024,256]{1,0:T(8,128)(2,1)S(1)}, bf16[1024,256]{1,0:T(8,128)(2,1)S(1)}, u32[]{:S(2)}, u32[]{:S(2)}) collective-permute-start(bf16[1024,256]{1,0:T(8,128)(2,1)S(1)} %pad_maximum_fusion.v0), channel_id=1, source_target_pairs={{0,24},{1,7},{2,26},{3,1},{4,28},{5,3},{6,30},{7,5},{8,0},{9,15},{... | collective-permute-start | bytes 1572872 | tf_op jit(solution)/shard_map/ppermute | solution.py:35
  20.0 2.6 %collective-permute-start.6 = (bf16[1024,256]{1,0:T(8,128)(2,1)S(1)}, bf16[1024,256]{1,0:T(8,128)(2,1)S(1)}, u32[]{:S(2)}, u32[]{:S(2)}) collective-permute-start(bf16[1024,256]{1,0:T(8,128)(2,1)S(1)} %pad_maximum_fusion.v0), channel_id=1, source_target_pairs={{0,16},{1,5},{2,18},{3,7},{4,20},{5,1},{6,22},{7,3},{8,24},{9,13},... | collective-permute-start | bytes 1572872 | tf_op jit(solution)/shard_map/ppermute | solution.py:35
  22.6 9.7 %collective-permute-done.4.v1 = bf16[1024,256]{1,0:T(8,128)(2,1)S(1)} collective-permute-done((bf16[1024,256]{1,0:T(8,128)(2,1)S(1)}, bf16[1024,256]{1,0:T(8,128)(2,1)S(1)}, u32[]{:S(2)}, u32[]{:S(2)}) %collective-permute-start.4) | collective-permute-done | bytes 524320 | tf_op jit(solution)/shard_map/ppermute | solution.py:35
  32.4 3.7 %collective-permute-done.5.v3 = bf16[1024,256]{1,0:T(8,128)(2,1)S(1)} collective-permute-done((bf16[1024,256]{1,0:T(8,128)(2,1)S(1)}, bf16[1024,256]{1,0:T(8,128)(2,1)S(1)}, u32[]{:S(2)}, u32[]{:S(2)}) %collective-permute-start.5) | collective-permute-done | bytes 524320 | tf_op jit(solution)/shard_map/ppermute | solution.py:35
  36.0 0.0 collective-permute-start.9
  36.0 2.0 %collective-permute-start.10 = (bf16[1024,256]{1,0:T(8,128)(2,1)S(1)}, bf16[1024,256]{1,0:T(8,128)(2,1)S(1)}, u32[]{:S(2)}, u32[]{:S(2)}) collective-permute-start(bf16[1024,256]{1,0:T(8,128)(2,1)S(1)} %pad_maximum_fusion.1.v0), channel_id=1, source_target_pairs={{0,8},{1,3},{2,10},{3,5},{4,12},{5,7},{6,14},{7,1},{8,16},{9,11},{... | collective-permute-start | bytes 1572872 | tf_op jit(solution)/shard_map/ppermute | solution.py:35
  38.1 0.3 collective-permute-start.11
  38.4 1.4 %copy-done.1 = bf16[768,1024]{1,0:T(8,128)(2,1)S(1)} copy-done((bf16[768,1024]{1,0:T(8,128)(2,1)S(1)}, bf16[768,1024]{1,0:T(8,128)(2,1)}, u32[]{:S(2)}) %copy-start.1) | copy-done | bytes 1572888
  39.8 4.5 %project.2 = (bf16[256,768]{1,0:T(8,128)(2,1)S(1)}, bf16[256,768]{1,0:T(8,128)(2,1)S(1)}, bf16[256,1024]{1,0:T(8,128)(2,1)S(1)}) custom-call(bf16[1024,256]{1,0:T(8,128)(2,1)S(1)} %pad_maximum_fusion.v0, bf16[1024,256]{1,0:T(8,128)(2,1)S(1)} %collective-permute-done.4.v1, bf16[1024,256]{1,0:T(8,128)(2,1)S(1)} %collective-permute-done.5.v3, ...), custom_call_target="tpu_custom_call" | custom-call | tf_op jit(solution)/shard_map/project/pallas_call | solution.py:153
  44.3 3.5 %collective-permute-start.12 = (bf16[256,1024]{1,0:T(8,128)(2,1)S(1)}, bf16[256,1024]{1,0:T(8,128)(2,1)S(1)}, u32[]{:S(2)}, u32[]{:S(2)}) collective-permute-start(bf16[256,1024]{1,0:T(8,128)(2,1)S(1)} %get-tuple-element.33), channel_id=1, source_target_pairs={{0,16},{1,5},{2,18},{3,7},{4,20},{5,1},{6,22},{7,3},{8,24},{9,13},... | collective-permute-start | bytes 1572872 | tf_op jit(solution)/shard_map/ppermute | solution.py:35
  47.8 1.9 %sides.2 = (bf16[256,1024]{1,0:T(8,128)(2,1)S(1)}, bf16[256,1024]{1,0:T(8,128)(2,1)S(1)}) custom-call(bf16[256,768]{1,0:T(8,128)(2,1)S(1)} %get-tuple-element.28.refs_0_.s, bf16[256,768]{1,0:T(8,128)(2,1)S(1)} %get-tuple-element.29.refs_1_.so, bf16[768,4096]{1,0:T(8,128)(2,1)S(1)} %copy-done, bf16[768,4096]{1,0:T(8,128)(2,1)S(1)} %collective-permute-done.7.xo.refs_5_), custom_call_target="tpu_custom_call" | custom-call | tf_op jit(solution)/shard_map/sides/pallas_call | solution.py:153
  49.7 0.1 collective-permute-start.13
  49.8 3.2 %collective-permute-start.14 = (bf16[256,1024]{1,0:T(8,128)(2,1)S(1)}, bf16[256,1024]{1,0:T(8,128)(2,1)S(1)}, u32[]{:S(2)}, u32[]{:S(2)}) collective-permute-start(bf16[256,1024]{1,0:T(8,128)(2,1)S(1)} %get-tuple-element.35), channel_id=1, source_target_pairs={{0,24},{1,7},{2,26},{3,1},{4,28},{5,3},{6,30},{7,5},{8,0},{9,15},{... | collective-permute-start | bytes 1572872 | tf_op jit(solution)/shard_map/ppermute | solution.py:35
  53.0 4.7 %collective-permute-done.10.v3 = bf16[1024,256]{1,0:T(8,128)(2,1)S(1)} collective-permute-done((bf16[1024,256]{1,0:T(8,128)(2,1)S(1)}, bf16[1024,256]{1,0:T(8,128)(2,1)S(1)}, u32[]{:S(2)}, u32[]{:S(2)}) %collective-permute-start.10) | collective-permute-done | bytes 524320 | tf_op jit(solution)/shard_map/ppermute | solution.py:35
  57.7 4.5 %project.3 = (bf16[256,768]{1,0:T(8,128)(2,1)S(1)}, bf16[256,768]{1,0:T(8,128)(2,1)S(1)}, bf16[256,1024]{1,0:T(8,128)(2,1)S(1)}) custom-call(bf16[1024,256]{1,0:T(8,128)(2,1)S(1)} %pad_maximum_fusion.1.v0, bf16[1024,256]{1,0:T(8,128)(2,1)S(1)} %collective-permute-done.9.v1, bf16[1024,256]{1,0:T(8,128)(2,1)S(1)} %collective-permute-done.10.v3, ...), custom_call_target="tpu_custom_call" | custom-call | tf_op jit(solution)/shard_map/project/pallas_call | solution.py:153
  62.2 0.1 collective-permute-start.15
  62.3 1.9 %sides.3 = (bf16[256,1024]{1,0:T(8,128)(2,1)S(1)}, bf16[256,1024]{1,0:T(8,128)(2,1)S(1)}) custom-call(bf16[256,768]{1,0:T(8,128)(2,1)S(1)} %get-tuple-element.31.refs_2_.s, bf16[256,768]{1,0:T(8,128)(2,1)S(1)} %get-tuple-element.32.refs_3_.so, bf16[768,4096]{1,0:T(8,128)(2,1)S(1)} %copy-done, bf16[768,4096]{1,0:T(8,128)(2,1)S(1)} %collective-permute-done.7.xo.refs_5_), custom_call_target="tpu_custom_call" | custom-call | tf_op jit(solution)/shard_map/sides/pallas_call | solution.py:153
  64.2 0.5 collective-permute-start.16
  64.7 2.8 %collective-permute-start.17 = (bf16[256,1024]{1,0:T(8,128)(2,1)S(1)}, bf16[256,1024]{1,0:T(8,128)(2,1)S(1)}, u32[]{:S(2)}, u32[]{:S(2)}) collective-permute-start(bf16[256,1024]{1,0:T(8,128)(2,1)S(1)} %get-tuple-element.38), channel_id=1, source_target_pairs={{0,24},{1,7},{2,26},{3,1},{4,28},{5,3},{6,30},{7,5},{8,0},{9,15},{... | collective-permute-start | bytes 1572872 | tf_op jit(solution)/shard_map/ppermute | solution.py:35
  67.5 1.8 %kept.1.refs_0_ = f32[512,1024]{1,0:T(8,128)S(1)} custom-call(bf16[256,768]{1,0:T(8,128)(2,1)S(1)} %get-tuple-element.28.refs_0_.s, bf16[256,768]{1,0:T(8,128)(2,1)S(1)} %get-tuple-element.29.refs_1_.so, bf16[256,768]{1,0:T(8,128)(2,1)S(1)} %get-tuple-element.31.refs_2_.s, bf16[256,768]{1,0:T(8,128)(2,1)S(1)} %get-tuple-element.32.refs_3_.so, ...), custom_call_target="tpu_custom_call" | custom-call | tf_op jit(solution)/shard_map/kept/pallas_call | solution.py:153
  69.3 0.0 copy-start.2
  69.4 3.7 %collective-permute-done.15.refs_4_ = bf16[256,1024]{1,0:T(8,128)(2,1)S(1)} collective-permute-done((bf16[256,1024]{1,0:T(8,128)(2,1)S(1)}, bf16[256,1024]{1,0:T(8,128)(2,1)S(1)}, u32[]{:S(2)}, u32[]{:S(2)}) %collective-permute-start.15) | collective-permute-done | bytes 524320 | tf_op jit(solution)/shard_map/ppermute | solution.py:35
  73.1 7.3 %collective-permute-done.16.refs_5_ = bf16[256,1024]{1,0:T(8,128)(2,1)S(1)} collective-permute-done((bf16[256,1024]{1,0:T(8,128)(2,1)S(1)}, bf16[256,1024]{1,0:T(8,128)(2,1)S(1)}, u32[]{:S(2)}, u32[]{:S(2)}) %collective-permute-start.16) | collective-permute-done | bytes 524320 | tf_op jit(solution)/shard_map/ppermute | solution.py:35
  80.4 0.5 fold.1
  80.9 0.9 collective-permute-start.18
  81.7 2.5 %collective-permute-start.20 = (bf16[512,256]{1,0:T(8,128)(2,1)S(1)}, bf16[512,256]{1,0:T(8,128)(2,1)S(1)}, u32[]{:S(2)}, u32[]{:S(2)}) collective-permute-start(bf16[512,256]{1,0:T(8,128)(2,1)S(1)} %get-tuple-element.42), channel_id=1, source_target_pairs={{0,6},{1,25},{2,0},{3,27},{4,2},{5,29},{6,4},{7,31},{8,14},{9,1},{... | collective-permute-start | bytes 786440 | tf_op jit(solution)/shard_map/ppermute | solution.py:35
  84.2 3.3 %collective-permute-done.18.a = bf16[512,256]{1,0:T(8,128)(2,1)S(1)} collective-permute-done((bf16[512,256]{1,0:T(8,128)(2,1)S(1)}, bf16[512,256]{1,0:T(8,128)(2,1)S(1)}, u32[]{:S(2)}, u32[]{:S(2)}) %collective-permute-start.18) | collective-permute-done | bytes 262176 | tf_op jit(solution)/shard_map/ppermute | solution.py:35
  87.5 2.2 %collective-permute-done.19.b = bf16[512,256]{1,0:T(8,128)(2,1)S(1)} collective-permute-done((bf16[512,256]{1,0:T(8,128)(2,1)S(1)}, bf16[512,256]{1,0:T(8,128)(2,1)S(1)}, u32[]{:S(2)}, u32[]{:S(2)}) %collective-permute-start.19) | collective-permute-done | bytes 262176 | tf_op jit(solution)/shard_map/ppermute | solution.py:35
  89.7 2.1 %collective-permute-done.20.c = bf16[512,256]{1,0:T(8,128)(2,1)S(1)} collective-permute-done((bf16[512,256]{1,0:T(8,128)(2,1)S(1)}, bf16[512,256]{1,0:T(8,128)(2,1)S(1)}, u32[]{:S(2)}, u32[]{:S(2)}) %collective-permute-start.20) | collective-permute-done | bytes 262176 | tf_op jit(solution)/shard_map/ppermute | solution.py:35
  91.8 0.1 split.1
  92.0 0.1 collective-permute-start.21
  92.9 0.1 pad_maximum_fusion.3.rate_ref
  93.0 0.4 collective-permute-done.21.theirs
  93.4 2.0 %inner_step.1 = (f32[128,1024]{1,0:T(8,128)}, f32[128,1024]{1,0:T(8,128)}, bf16[128,1024]{1,0:T(8,128)(2,1)S(1)}) custom-call(f32[3]{0:T(128)S(1)} %pad_maximum_fusion.3.rate_ref, f32[512,128]{1,0:T(8,128)S(1)} %get-tuple-element.43.mine, bf16[512,128]{1,0:T(8,128)(2,1)S(1)} %collective-permute-done.21.theirs, f32[128,1024]{1,0:T(8,128)S(1)} %bitcast.13, ...), custom_call_target="tpu_custom_call" | custom-call | tf_op jit(solution)/shard_map/inner_step/pallas_call | solution.py:153
  95.4 20.4 %all_to_all.10 = bf16[8,16,1024]{2,1,0:T(8,128)(2,1)S(1)} all-to-all(bf16[8,16,1024]{2,1,0:T(8,128)(2,1)S(1)} %bitcast.15), channel_id=1, replica_groups=mesh['island'=8,'fsdp'=8,'dp'=4] {'island'}, dimensions={0} | all-to-all | bytes 524288 | tf_op jit(solution)/shard_map/all_to_all | solution.py:233
  115.9 13.5 %all_to_all.11 = bf16[8,16,1024]{2,1,0:T(8,128)(2,1)S(1)} all-to-all(bf16[8,16,1024]{2,1,0:T(8,128)(2,1)S(1)} %broadcast_in_dim.12), channel_id=1, replica_groups=mesh['island'=8,'fsdp'=8,'dp'=4] {'island'}, dimensions={0} | all-to-all | bytes 524288 | tf_op jit(solution)/shard_map/all_to_all | solution.py:236
  129.4 1.1 fusion.1
  (33 shorter events, 0.3 us)
Async XLA Ops:
  1.8 1.4 %collective-permute-start = (bf16[128,512]{1,0:T(8,128)(2,1)S(1)}, bf16[128,512]{1,0:T(8,128)(2,1)S(1)}, u32[]{:S(2)}, u32[]{:S(2)}) collective-permute-start(bf16[128,512]{1,0:T(8,128)(2,1)S(1)} %get-tuple-element.59), channel_id=1, source_target_pairs={{0,1},{1,0},{2,3},{3,2},{4,5},{5,4},{6,7},{7,6},{8,9},{9,8},{10,11... | collective-permute-start | bytes 393224 | tf_op jit(solution)/shard_map/ppermute | solution.py:35
  3.2 35.2 %collective-permute-start.7 = (bf16[768,4096]{1,0:T(8,128)(2,1)}, bf16[768,4096]{1,0:T(8,128)(2,1)S(1)}, u32[]{:S(2)}, u32[]{:S(2)}) collective-permute-start(bf16[768,4096]{1,0:T(8,128)(2,1)} %x.7), channel_id=1, source_target_pairs={{0,1},{1,0},{2,3},{3,2},{4,5},{5,4},{6,7},{7,6},{8,9},{9,8},{10,11... | collective-permute-start | bytes 18874376 | tf_op jit(solution)/shard_map/ppermute | solution.py:35
  3.3 35.0 %copy-start = (bf16[768,4096]{1,0:T(8,128)(2,1)S(1)}, bf16[768,4096]{1,0:T(8,128)(2,1)}, u32[]{:S(2)}) copy-start(bf16[768,4096]{1,0:T(8,128)(2,1)} %x.7) | copy-start | bytes 18874372
  3.4 7.0 %collective-permute-start.3 = (bf16[256,512]{1,0:T(8,128)(2,1)S(1)}, bf16[256,512]{1,0:T(8,128)(2,1)S(1)}, u32[]{:S(2)}, u32[]{:S(2)}) collective-permute-start(bf16[256,512]{1,0:T(8,128)(2,1)S(1)} %pad_maximum_fusion.2), channel_id=1, source_target_pairs={{0,2},{1,9},{2,4},{3,11},{4,6},{5,13},{6,0},{7,15},{8,10},{9,17},{... | collective-permute-start | bytes 786440 | tf_op jit(solution)/shard_map/ppermute | solution.py:35
  6.3 32.0 %collective-permute-start.8 = (bf16[768,512]{1,0:T(8,128)(2,1)S(1)}, bf16[768,512]{1,0:T(8,128)(2,1)S(1)}, u32[]{:S(2)}, u32[]{:S(2)}) collective-permute-start(bf16[768,512]{1,0:T(8,128)(2,1)S(1)} %constant_dynamic-slice_fusion), channel_id=1, source_target_pairs={{0,1},{1,0},{2,3},{3,2},{4,5},{5,4},{6,7},{7,6},{8,9},{9,8},{10,11... | collective-permute-start | bytes 2359304 | tf_op jit(solution)/shard_map/ppermute | solution.py:35
  6.8 8.0 %collective-permute-start.2 = (bf16[256,512]{1,0:T(8,128)(2,1)S(1)}, bf16[256,512]{1,0:T(8,128)(2,1)S(1)}, u32[]{:S(2)}, u32[]{:S(2)}) collective-permute-start(bf16[256,512]{1,0:T(8,128)(2,1)S(1)} %pad_maximum_fusion.2), channel_id=1, source_target_pairs={{0,4},{1,17},{2,6},{3,19},{4,0},{5,21},{6,2},{7,23},{8,12},{9,25},... | collective-permute-start | bytes 786440 | tf_op jit(solution)/shard_map/ppermute | solution.py:35
  9.2 8.3 %collective-permute-start.1 = (bf16[256,512]{1,0:T(8,128)(2,1)S(1)}, bf16[256,512]{1,0:T(8,128)(2,1)S(1)}, u32[]{:S(2)}, u32[]{:S(2)}) collective-permute-start(bf16[256,512]{1,0:T(8,128)(2,1)S(1)} %pad_maximum_fusion.2), channel_id=1, source_target_pairs={{0,6},{1,25},{2,0},{3,27},{4,2},{5,29},{6,4},{7,31},{8,14},{9,1},{... | collective-permute-start | bytes 786440 | tf_op jit(solution)/shard_map/ppermute | solution.py:35
  17.5 14.8 %collective-permute-start.4 = (bf16[1024,256]{1,0:T(8,128)(2,1)S(1)}, bf16[1024,256]{1,0:T(8,128)(2,1)S(1)}, u32[]{:S(2)}, u32[]{:S(2)}) collective-permute-start(bf16[1024,256]{1,0:T(8,128)(2,1)S(1)} %pad_maximum_fusion.v0), channel_id=1, source_target_pairs={{0,24},{1,7},{2,26},{3,1},{4,28},{5,3},{6,30},{7,5},{8,0},{9,15},{... | collective-permute-start | bytes 1572872 | tf_op jit(solution)/shard_map/ppermute | solution.py:35
  20.0 16.0 %collective-permute-start.5 = (bf16[1024,256]{1,0:T(8,128)(2,1)S(1)}, bf16[1024,256]{1,0:T(8,128)(2,1)S(1)}, u32[]{:S(2)}, u32[]{:S(2)}) collective-permute-start(bf16[1024,256]{1,0:T(8,128)(2,1)S(1)} %pad_maximum_fusion.v0), channel_id=1, source_target_pairs={{0,8},{1,3},{2,10},{3,5},{4,12},{5,7},{6,14},{7,1},{8,16},{9,11},{... | collective-permute-start | bytes 1572872 | tf_op jit(solution)/shard_map/ppermute | solution.py:35
  20.0 16.0 %collective-permute-start.6 = (bf16[1024,256]{1,0:T(8,128)(2,1)S(1)}, bf16[1024,256]{1,0:T(8,128)(2,1)S(1)}, u32[]{:S(2)}, u32[]{:S(2)}) collective-permute-start(bf16[1024,256]{1,0:T(8,128)(2,1)S(1)} %pad_maximum_fusion.v0), channel_id=1, source_target_pairs={{0,16},{1,5},{2,18},{3,7},{4,20},{5,1},{6,22},{7,3},{8,24},{9,13},... | collective-permute-start | bytes 1572872 | tf_op jit(solution)/shard_map/ppermute | solution.py:35
  36.0 13.7 %collective-permute-start.9 = (bf16[1024,256]{1,0:T(8,128)(2,1)S(1)}, bf16[1024,256]{1,0:T(8,128)(2,1)S(1)}, u32[]{:S(2)}, u32[]{:S(2)}) collective-permute-start(bf16[1024,256]{1,0:T(8,128)(2,1)S(1)} %pad_maximum_fusion.1.v0), channel_id=1, source_target_pairs={{0,24},{1,7},{2,26},{3,1},{4,28},{5,3},{6,30},{7,5},{8,0},{9,15},{... | collective-permute-start | bytes 1572872 | tf_op jit(solution)/shard_map/ppermute | solution.py:35
  36.0 21.6 %collective-permute-start.10 = (bf16[1024,256]{1,0:T(8,128)(2,1)S(1)}, bf16[1024,256]{1,0:T(8,128)(2,1)S(1)}, u32[]{:S(2)}, u32[]{:S(2)}) collective-permute-start(bf16[1024,256]{1,0:T(8,128)(2,1)S(1)} %pad_maximum_fusion.1.v0), channel_id=1, source_target_pairs={{0,8},{1,3},{2,10},{3,5},{4,12},{5,7},{6,14},{7,1},{8,16},{9,11},{... | collective-permute-start | bytes 1572872 | tf_op jit(solution)/shard_map/ppermute | solution.py:35
  38.1 19.6 %collective-permute-start.11 = (bf16[1024,256]{1,0:T(8,128)(2,1)S(1)}, bf16[1024,256]{1,0:T(8,128)(2,1)S(1)}, u32[]{:S(2)}, u32[]{:S(2)}) collective-permute-start(bf16[1024,256]{1,0:T(8,128)(2,1)S(1)} %pad_maximum_fusion.1.v0), channel_id=1, source_target_pairs={{0,16},{1,5},{2,18},{3,7},{4,20},{5,1},{6,22},{7,3},{8,24},{9,13},... | collective-permute-start | bytes 1572872 | tf_op jit(solution)/shard_map/ppermute | solution.py:35
  38.4 1.4 %copy-start.1 = (bf16[768,1024]{1,0:T(8,128)(2,1)S(1)}, bf16[768,1024]{1,0:T(8,128)(2,1)}, u32[]{:S(2)}) copy-start(bf16[768,1024]{1,0:T(8,128)(2,1)} %t.3) | copy-start | bytes 4718596
  44.3 20.4 %collective-permute-start.12 = (bf16[256,1024]{1,0:T(8,128)(2,1)S(1)}, bf16[256,1024]{1,0:T(8,128)(2,1)S(1)}, u32[]{:S(2)}, u32[]{:S(2)}) collective-permute-start(bf16[256,1024]{1,0:T(8,128)(2,1)S(1)} %get-tuple-element.33), channel_id=1, source_target_pairs={{0,16},{1,5},{2,18},{3,7},{4,20},{5,1},{6,22},{7,3},{8,24},{9,13},... | collective-permute-start | bytes 1572872 | tf_op jit(solution)/shard_map/ppermute | solution.py:35
  49.7 19.7 %collective-permute-start.13 = (bf16[256,1024]{1,0:T(8,128)(2,1)S(1)}, bf16[256,1024]{1,0:T(8,128)(2,1)S(1)}, u32[]{:S(2)}, u32[]{:S(2)}) collective-permute-start(bf16[256,1024]{1,0:T(8,128)(2,1)S(1)} %get-tuple-element.34), channel_id=1, source_target_pairs={{0,8},{1,3},{2,10},{3,5},{4,12},{5,7},{6,14},{7,1},{8,16},{9,11},{... | collective-permute-start | bytes 1572872 | tf_op jit(solution)/shard_map/ppermute | solution.py:35
  49.8 19.6 %collective-permute-start.14 = (bf16[256,1024]{1,0:T(8,128)(2,1)S(1)}, bf16[256,1024]{1,0:T(8,128)(2,1)S(1)}, u32[]{:S(2)}, u32[]{:S(2)}) collective-permute-start(bf16[256,1024]{1,0:T(8,128)(2,1)S(1)} %get-tuple-element.35), channel_id=1, source_target_pairs={{0,24},{1,7},{2,26},{3,1},{4,28},{5,3},{6,30},{7,5},{8,0},{9,15},{... | collective-permute-start | bytes 1572872 | tf_op jit(solution)/shard_map/ppermute | solution.py:35
  62.2 10.9 %collective-permute-start.15 = (bf16[256,1024]{1,0:T(8,128)(2,1)S(1)}, bf16[256,1024]{1,0:T(8,128)(2,1)S(1)}, u32[]{:S(2)}, u32[]{:S(2)}) collective-permute-start(bf16[256,1024]{1,0:T(8,128)(2,1)S(1)} %get-tuple-element.36), channel_id=1, source_target_pairs={{0,16},{1,5},{2,18},{3,7},{4,20},{5,1},{6,22},{7,3},{8,24},{9,13},... | collective-permute-start | bytes 1572872 | tf_op jit(solution)/shard_map/ppermute | solution.py:35
  64.2 16.2 %collective-permute-start.16 = (bf16[256,1024]{1,0:T(8,128)(2,1)S(1)}, bf16[256,1024]{1,0:T(8,128)(2,1)S(1)}, u32[]{:S(2)}, u32[]{:S(2)}) collective-permute-start(bf16[256,1024]{1,0:T(8,128)(2,1)S(1)} %get-tuple-element.37), channel_id=1, source_target_pairs={{0,8},{1,3},{2,10},{3,5},{4,12},{5,7},{6,14},{7,1},{8,16},{9,11},{... | collective-permute-start | bytes 1572872 | tf_op jit(solution)/shard_map/ppermute | solution.py:35
  64.7 15.7 %collective-permute-start.17 = (bf16[256,1024]{1,0:T(8,128)(2,1)S(1)}, bf16[256,1024]{1,0:T(8,128)(2,1)S(1)}, u32[]{:S(2)}, u32[]{:S(2)}) collective-permute-start(bf16[256,1024]{1,0:T(8,128)(2,1)S(1)} %get-tuple-element.38), channel_id=1, source_target_pairs={{0,24},{1,7},{2,26},{3,1},{4,28},{5,3},{6,30},{7,5},{8,0},{9,15},{... | collective-permute-start | bytes 1572872 | tf_op jit(solution)/shard_map/ppermute | solution.py:35
  69.3 24.1 %copy-start.2 = (f32[128,1024]{1,0:T(8,128)S(1)}, f32[128,1024]{1,0:T(8,128)}, u32[]{:S(2)}) copy-start(f32[128,1024]{1,0:T(8,128)} %weight.1) | copy-start | bytes 1572868
  69.4 24.1 %copy-start.3 = (f32[1,128,1024]{2,1,0:T(8,128)S(1)}, f32[1,128,1024]{2,1,0:T(8,128)}, u32[]{:S(2)}) copy-start(f32[1,128,1024]{2,1,0:T(8,128)} %param.11) | copy-start | bytes 1572868
  69.4 24.0 %copy-start.4 = (f32[1,128,1024]{2,1,0:T(8,128)S(1)}, f32[1,128,1024]{2,1,0:T(8,128)}, u32[]{:S(2)}) copy-start(f32[1,128,1024]{2,1,0:T(8,128)} %param.12) | copy-start | bytes 1572868
  80.9 6.7 %collective-permute-start.18 = (bf16[512,256]{1,0:T(8,128)(2,1)S(1)}, bf16[512,256]{1,0:T(8,128)(2,1)S(1)}, u32[]{:S(2)}, u32[]{:S(2)}) collective-permute-start(bf16[512,256]{1,0:T(8,128)(2,1)S(1)} %get-tuple-element.40), channel_id=1, source_target_pairs={{0,2},{1,9},{2,4},{3,11},{4,6},{5,13},{6,0},{7,15},{8,10},{9,17},{... | collective-permute-start | bytes 786440 | tf_op jit(solution)/shard_map/ppermute | solution.py:35
  81.7 8.0 %collective-permute-start.19 = (bf16[512,256]{1,0:T(8,128)(2,1)S(1)}, bf16[512,256]{1,0:T(8,128)(2,1)S(1)}, u32[]{:S(2)}, u32[]{:S(2)}) collective-permute-start(bf16[512,256]{1,0:T(8,128)(2,1)S(1)} %get-tuple-element.41), channel_id=1, source_target_pairs={{0,4},{1,17},{2,6},{3,19},{4,0},{5,21},{6,2},{7,23},{8,12},{9,25},... | collective-permute-start | bytes 786440 | tf_op jit(solution)/shard_map/ppermute | solution.py:35
  81.7 10.1 %collective-permute-start.20 = (bf16[512,256]{1,0:T(8,128)(2,1)S(1)}, bf16[512,256]{1,0:T(8,128)(2,1)S(1)}, u32[]{:S(2)}, u32[]{:S(2)}) collective-permute-start(bf16[512,256]{1,0:T(8,128)(2,1)S(1)} %get-tuple-element.42), channel_id=1, source_target_pairs={{0,6},{1,25},{2,0},{3,27},{4,2},{5,29},{6,4},{7,31},{8,14},{9,1},{... | collective-permute-start | bytes 786440 | tf_op jit(solution)/shard_map/ppermute | solution.py:35
  92.0 37.5 %copy-start.5 = (f32[128,1024]{1,0:T(8,128)S(1)}, f32[128,1024]{1,0:T(8,128)}, u32[]{:S(2)}) copy-start(f32[128,1024]{1,0:T(8,128)} %param.10) | copy-start | bytes 1572868
  92.0 1.4 %collective-permute-start.21 = (bf16[512,128]{1,0:T(8,128)(2,1)S(1)}, bf16[512,128]{1,0:T(8,128)(2,1)S(1)}, u32[]{:S(2)}, u32[]{:S(2)}) collective-permute-start(bf16[512,128]{1,0:T(8,128)(2,1)S(1)} %get-tuple-element.44), channel_id=1, source_target_pairs={{0,1},{1,0},{2,3},{3,2},{4,5},{5,4},{6,7},{7,6},{8,9},{9,8},{10,11... | collective-permute-start | bytes 393224 | tf_op jit(solution)/shard_map/ppermute | solution.py:35

commit v3 on v2

v3 whole, which is shorter than its diff:
```python
import functools
import jax
import jax.numpy as jnp
from jax import lax
from jax.experimental import pallas as pl
from jax.experimental.pallas import tpu as pltpu
from jax.sharding import PartitionSpec as P

WARM = 32
NX = NY = 4
NZ = 8
BIG = (768, 4096)
SIDE = 256
STEPS = 3
LOW, HIGH = (0, 1), (2, 3)
LIMIT_A = 10
LIMIT_B = 8
AXES = ("island", "fsdp", "dp")
MIB = 1024 * 1024
GIGA = 10**9
VM = pl.BlockSpec(memory_space=pltpu.VMEM)
SM = pl.BlockSpec(memory_space=pltpu.SMEM)


def flat(z, y, x, c):
    return (z % NZ) * 32 + (y % NY) * 8 + (x % NX) * 2 + c


def send(value, where):
    pairs = [
        (flat(z, y, x, c), flat(*where(z, y, x, c)))
        for z in range(NZ)
        for y in range(NY)
        for x in range(NX)
        for c in range(2)
    ]
    return lax.ppermute(value, AXES, pairs)


def near(k):
    return lambda z, y, x, c: (z, y, x + k, c) if c == 0 else (z, y + k, x, c)


def far(k):
    return lambda z, y, x, c: (z, y + k, x, c) if c == 0 else (z, y, x + k, c)


def partner(z, y, x, c):
    return (z, y, x, 1 - c)


def params(limit):
    return pltpu.CompilerParams(vmem_limit_bytes=limit * MIB)


def here():
    fsdp, dp = lax.axis_index("fsdp"), lax.axis_index("dp")
    return lax.div(fsdp, 2), lax.rem(fsdp, 2) * 2 + lax.div(dp, 2), lax.rem(dp, 2)


def chip(place, g, m):
    y, x, core = place
    outer = lax.rem(jnp.where(core == 0, y, x) + g, 4)
    inner = lax.rem(jnp.where(core == 0, x, y) + m, 4)
    return jnp.where(core == 0, outer * NX + inner, inner * NX + outer)


def columns_of(place, g, m):
    return pl.ds(pl.multiple_of(chip(place, g, m) * SIDE, SIDE), SIDE)


def term(place, g, m, s, so, x, xo):
    columns = columns_of(place, g, m)
    total = jnp.dot(s[...], x[:, columns], preferred_element_type=jnp.float32)
    return total + jnp.dot(so[...], xo[:, columns], preferred_element_type=jnp.float32)


def product(place, tokens, g, members, block, span=slice(None)):
    rows = [tokens[span, columns_of(place, g, m)] for m in members]
    return jnp.dot(jnp.concatenate(rows, axis=1), block, preferred_element_type=jnp.float32)


def first_kernel(a, b, c, d, x, xo, out, out_other, held, held_other, sems):
    place = here()
    rows = x.shape[0] // STEPS
    copies = []
    for i, (source, into) in enumerate(((x, held), (xo, held_other))):
        for k in range(STEPS):
            span = pl.ds(k * rows, rows)
            copies.append(pltpu.make_async_copy(source.at[span], into.at[span], sems.at[i, k]))
    for copy in copies:
        copy.start()
    block = jnp.concatenate([a[...], b[...], c[...], d[...]], axis=0)
    for i, (tokens, ref) in enumerate(((held, out), (held_other, out_other))):
        for k in range(STEPS):
            copies[i * STEPS + k].wait()
            span = slice(k * rows, (k + 1) * rows)
            ref[span, :] = product(place, tokens, 0, range(4), block, span).astype(ref.dtype)


def more_kernel(acc, acc_other, low_1, high_1, low_3, high_3, x, xo, out, out_other):
    place = here()
    blocks = ((1, (low_1, high_1)), (3, (low_3, high_3)))
    blocks = [(g, jnp.concatenate([ref[...] for ref in refs], axis=0)) for g, refs in blocks]
    for tokens, start, ref in ((x, acc, out), (xo, acc_other, out_other)):
        total = start[...].astype(jnp.float32)
        for g, block in blocks:
            total += product(place, tokens, g, range(4), block)
        ref[...] = total.astype(ref.dtype)


def late_kernel(scales, acc, acc_other, va, vb, x, xo, rates, t, to, s_ref, so_ref, relay_a, relay_b, rates_out, aims, sems):
    place = here()
    copies = [pltpu.make_async_copy(ref, aims.at[i], sems.at[i]) for i, ref in enumerate((t, to))]
    for copy in copies:
        copy.start()
    inv_width, inv_count = scales
    rates_out[...] = rates[...]
    for i, (tokens, total, out) in enumerate(((x, acc, s_ref), (xo, acc_other, so_ref))):
        proj = total[...].astype(jnp.float32) + product(place, tokens, 2, LOW, va[...]) + product(place, tokens, 2, HIGH, vb[...])
        copies[i].wait()
        scaled = (proj * inv_width - aims[i].astype(jnp.float32)) * inv_count
        out[...] = scaled.T.astype(jnp.bfloat16)
    for out, members in ((relay_a, LOW), (relay_b, HIGH)):
        for k, m in enumerate(members):
            out[:, k * SIDE : (k + 1) * SIDE] = term(place, 2, m, s_ref, so_ref, x, xo).astype(out.dtype)


def sides_kernel(members, s, so, x, xo, up, down):
    place = here()
    for g, out, chosen in ((1, up, members[0]), (3, down, members[1])):
        for k, m in enumerate(chosen):
            out[:, k * SIDE : (k + 1) * SIDE] = term(place, g, m, s, so, x, xo).astype(out.dtype)


def kept_kernel(s, so, x, xo, out):
    place = here()
    for m in range(4):
        out[:, m * SIDE : (m + 1) * SIDE] = term(place, 0, m, s, so, x, xo)


def fold_kernel(kept, up_a, down_a, up_b, down_b, *outs):
    for m in range(4):
        part = slice(m % 2 * SIDE, (m % 2 + 1) * SIDE)
        total = kept[:, m * SIDE : (m + 1) * SIDE]
        for ref in (up_a, down_a) if m < 2 else (up_b, down_b):
            total += ref[:, part].astype(jnp.float32)
        outs[m][...] = total.astype(outs[m].dtype)


def split_kernel(own, a, b, c, mine, theirs):
    total = own[...] + a[...].astype(jnp.float32) + b[...].astype(jnp.float32) + c[...].astype(jnp.float32)
    core = here()[2]
    low, high = total[:, : SIDE // 2], total[:, SIDE // 2 :]
    mine[...] = jnp.where(core == 0, low, high)
    theirs[...] = jnp.where(core == 0, high, low).astype(theirs.dtype)


def inner_kernel(rates, first, second, weight, *refs):
    grads, (new_first, new_second, pseudo) = refs[:-3], refs[-3:]
    core = here()[2]
    width = grads[0].shape[0]
    rate, first_scale, second_scale = rates[0:1, :], rates[1:2, :], rates[2:3, :]
    for k, ref in enumerate(grads):
        side = core if k % 2 == 0 else 1 - core
        columns = pl.ds(pl.multiple_of(side * width, width), width)
        grad = ref[...].astype(jnp.float32).T
        one = 0.9 * first[:, columns] + 0.1 * grad
        two = 0.95 * second[:, columns] + 0.05 * grad * grad
        update = (one * first_scale) / (jnp.sqrt(two * second_scale) + 1e-08)
        new_first[:, columns] = one
        new_second[:, columns] = two
        pseudo[:, columns] = (rate * (update + 0.1 * weight[:, columns])).astype(pseudo.dtype)


def local(kernel, shapes, limit, name, *operands, cost=1, alias={}):
    operands = [
        pltpu.with_memory_space_constraint(o, pltpu.VMEM) if o.shape == BIG else o for o in operands
    ]
    return pl.pallas_call(
        kernel,
        out_shape=[jax.ShapeDtypeStruct(*s) for s in shapes],
        in_specs=[VM] * len(operands),
        out_specs=[VM] * len(shapes),
        compiler_params=params(limit),
        input_output_aliases=alias,
        cost_estimate=pl.CostEstimate(flops=cost * GIGA, bytes_accessed=MIB, transcendentals=0),
        name=name,
    )(*operands)


def per_device(tokens, targets, kv_weight, momentum, first_moment, second_moment, step):
    f32, bf16 = jnp.float32, jnp.bfloat16
    count, features = tokens.shape
    rows, columns = kv_weight.shape
    half = columns // 2
    core = here()[2]
    scales = (1.0 / float(features) ** 0.5, 1.0 / float(count * 32) ** 0.5)

    whole = kv_weight.astype(bf16)
    own_half = lax.dynamic_slice_in_dim(whole, core * half, half, 1)
    other_half = lax.dynamic_slice_in_dim(whole, (1 - core) * half, half, 1)
    crossed = send(other_half, partner)
    crossed, tokens_now = lax.optimization_barrier((crossed, tokens))
    tokens_other = send(tokens_now, partner)
    shard = jnp.where(
        core == 0,
        jnp.concatenate([own_half, crossed], axis=0),
        jnp.concatenate([crossed, own_half], axis=0),
    )
    inner = [shard] + [send(shard, near(-k)) for k in (1, 2, 3)]
    tally = step.astype(f32)
    rate = 0.1 * jnp.minimum(tally, f32(WARM)) / f32(WARM)
    first_scale = 1.0 / (1.0 - jnp.power(f32(0.9), tally))
    second_scale = 1.0 / (1.0 - jnp.power(f32(0.95), tally))
    rates = jnp.stack([rate, first_scale, second_scale] + [rate] * 5)
    rates = jnp.broadcast_to(rates[:, None], (8, half))

    inner[3], targets = lax.optimization_barrier((inner[3], targets))
    goals = lax.dynamic_slice_in_dim(targets, core * half, half, 1)
    goals_other = lax.dynamic_slice_in_dim(targets, (1 - core) * half, half, 1)
    inner[2], goals, goals_other = lax.optimization_barrier((inner[2], goals, goals_other))
    goals_other = send(goals_other, partner)
    low, high = jnp.concatenate(inner[:2], axis=0), jnp.concatenate(inner[2:], axis=0)
    low, tokens_other = lax.optimization_barrier((low, tokens_other))
    low_1, high_3 = send(low, far(-1)), send(high, far(1))
    high_1, low_3 = send(high, far(-1)), send(low, far(1))
    low_2, high_2 = send(low_1, far(-1)), send(high_3, far(1))
    hbm = pl.BlockSpec(memory_space=pltpu.HBM)
    *acc, tokens, tokens_other = pl.pallas_call(
        first_kernel,
        out_shape=[jax.ShapeDtypeStruct((count, half), bf16)] * 2 + [pltpu.VMEM(tokens.shape, bf16)] * 2,
        in_specs=[VM] * 4 + [hbm] * 2,
        out_specs=[VM] * 4,
        scratch_shapes=[pltpu.SemaphoreType.DMA((2, STEPS))],
        compiler_params=params(LIMIT_A),
        name="first",
    )(
        *inner,
        pltpu.with_memory_space_constraint(tokens, pltpu.HBM),
        pltpu.with_memory_space_constraint(tokens_other, pltpu.HBM),
    )
    pair = (tokens, tokens_other)
    acc = local(
        more_kernel, [((count, half), bf16)] * 2, LIMIT_A, "more", *acc, low_1, high_1, low_3, high_3, *pair, cost=4
    )
    mid = ((half, 2 * SIDE), bf16)
    s, so, relay_a, relay_b, rates = pl.pallas_call(
        functools.partial(late_kernel, scales),
        out_shape=[
            jax.ShapeDtypeStruct(*k) for k in [((half, count), bf16)] * 2 + [mid] * 2 + [(rates.shape, f32)]
        ],
        in_specs=[VM] * 7 + [pl.BlockSpec(memory_space=pltpu.HBM)] * 2,
        out_specs=[VM] * 5,
        scratch_shapes=[pltpu.VMEM((2, count, half), bf16), pltpu.SemaphoreType.DMA((2,))],
        compiler_params=params(LIMIT_A),
        name="late",
    )(
        *acc,
        low_2, high_2,
        *[pltpu.with_memory_space_constraint(k, pltpu.VMEM) for k in pair],
        rates,
        *[pltpu.with_memory_space_constraint(k, pltpu.HBM) for k in (goals, goals_other)],
    )
    sides = functools.partial(sides_kernel, (HIGH, LOW))
    up_b, down_a = local(sides, [mid] * 2, LIMIT_B, "sides_near", s, so, *pair, cost=2)
    sides = functools.partial(sides_kernel, (LOW, HIGH))
    up_a, down_b = local(sides, [mid] * 2, LIMIT_B, "sides_rest", s, so, *pair, cost=2)
    (kept,) = local(kept_kernel, [((half, 4 * SIDE), f32)], LIMIT_B, "kept", s, so, *pair, cost=2)
    from_low, from_high = send(relay_a, far(1)), send(relay_b, far(-1))
    up_b, down_a = send(up_b, far(1)), send(down_a, far(-1))
    up_a = send((up_a.astype(f32) + from_low.astype(f32)).astype(bf16), far(1))
    down_b = send((down_b.astype(f32) + from_high.astype(f32)).astype(bf16), far(-1))
    parts = local(
        fold_kernel,
        [((half, SIDE), f32)] + [((half, SIDE), bf16)] * 3,
        LIMIT_B,
        "fold",
        kept, up_a, down_a, up_b, down_b,
    )
    mine, theirs = local(
        split_kernel,
        [((half, SIDE // 2), f32), ((half, SIDE // 2), bf16)],
        LIMIT_B,
        "split",
        parts[0], *[send(parts[k], near(k)) for k in (1, 2, 3)],
    )
    grads = [mine, send(theirs, partner)]

    state = (kv_weight.shape, f32)
    new_first, new_second, pseudo = local(
        inner_kernel,
        [state, state, (kv_weight.shape, bf16)],
        LIMIT_B,
        "inner_step",
        rates, first_moment[0], second_moment[0], kv_weight, *grads,
    )

    split = lax.all_to_all(pseudo.reshape(NZ, rows // NZ, columns), "island", 0, 0, tiled=True)
    share = jnp.sum(split.astype(f32), axis=0) / f32(NZ)
    spread = jnp.broadcast_to(share.astype(bf16)[None], (NZ, rows // NZ, columns))
    mean = lax.all_to_all(spread, "island", 0, 0, tiled=True).reshape(rows, columns).astype(f32)
    new_momentum = 0.9 * momentum + mean
    new_weight = kv_weight - 0.7 * (mean + 0.9 * new_momentum)
    return (new_weight, new_momentum, new_first[None], new_second[None])


def solution(mesh):
    placed = (
        P(("island", "fsdp", "dp"), None),
        P(("island", "fsdp", "dp"), None),
        P(("fsdp", "dp"), None),
        P(("fsdp", "dp"), None),
        P("island", ("fsdp", "dp"), None),
        P("island", ("fsdp", "dp"), None),
        P(),
    )
    return jax.shard_map(
        per_device,
        mesh=mesh,
        in_specs=placed,
        out_specs=(
            P(("fsdp", "dp"), None),
            P(("fsdp", "dp"), None),
            P("island", ("fsdp", "dp"), None),
            P("island", ("fsdp", "dp"), None),
        ),
        check_vma=False,
    )
```

time: 131 us -> 118 us (0.901)
  waiting for transfers between devices: 45.4 us -> 24.8 us
  Pallas kernels: 17.2 us -> 21.3 us
  starting transfers between devices: 26.8 us -> 30.5 us
  blocking collectives: 33.9 us -> 31.2 us
  local copies, waits for them, and re-layouts: 2.94 us -> 4.29 us
    ppermute x22, waiting for transfers between devices: 45.4 us -> 24.8 us  [send(): return lax.ppermute(value, AXES, pairs)]
    pallas_call x0 -> x2, Pallas kernels: none -> 9.32 us  [the longest x1 5.16 us: per_device(): pl.pallas_call(first_kernel, out_shape=[jax.ShapeDtypeStruct((count, half...]
    pallas_call x8 -> x7, Pallas kernels: 17.2 us -> 12 us  [local(): pl.pallas_call(kernel, out_shape=[jax.ShapeDtypeStruct(*s) for s in shape...]
    ppermute x22, starting transfers between devices: 26.8 us -> 30.5 us  [send(): return lax.ppermute(value, AXES, pairs)]
    all_to_all x1, blocking collectives: 20.4 us -> 17.7 us  [per_device(): lax.all_to_all(pseudo.reshape(NZ, rows // NZ, columns), 'island', 0, 0, t...]
  transfers between devices with their start and end apart: 22 -> 22, of which waited for: 12 -> 14; matrix products, arithmetic and copies ran while one was open for 1% -> 5% of each run, Pallas kernels for 11% -> 13%
where the time goes in v3:
time: 118 us; the launch traced here: 117 us
  blocking collectives  31.2 us (26%)
  starting transfers between devices  30.5 us (26%)
  waiting for transfers between devices  24.8 us (21%)
  Pallas kernels  21.3 us (18%)
  local copies, waits for them, and re-layouts  4.29 us (4%)
  other arithmetic  3.4 us (3%)
  between operations  1.67 us (1%)
    ppermute x22, starting transfers between devices, send(): return lax.ppermute(value, AXES, pairs)  30.5 us
    ppermute x22, waiting for transfers between devices, send(): return lax.ppermute(value, AXES, pairs)  24.8 us
    all_to_all x1, blocking collectives, per_device(): lax.all_to_all(pseudo.reshape(NZ, rows // NZ, columns), 'island', 0, 0, t...  17.7 us
    all_to_all x1, blocking collectives, per_device(): lax.all_to_all(spread, 'island', 0, 0, tiled=True).reshape(rows, columns)  13.5 us
    pallas_call x7, Pallas kernels, local(): pl.pallas_call(kernel, out_shape=[jax.ShapeDtypeStruct(*s) for s in shape...  12 us
    pallas_call x1, Pallas kernels, per_device(): pl.pallas_call(first_kernel, out_shape=[jax.ShapeDtypeStruct((count, half...  5.16 us
    pallas_call x1, Pallas kernels, per_device(): pl.pallas_call(functools.partial(late_kernel, scales), out_shape=[jax.Sha...  4.16 us
    dynamic_slice x1, local copies, waits for them, and re-layouts, per_device(): goals_other = lax.dynamic_slice_in_dim(targets, (1 - core) * half, half, 1)  2.62 us
  transfers between devices with their start and end apart: 22, of which 14 were waited for; matrix products, arithmetic and copies ran while one was open for 5% of the time, Pallas kernels for 13%

profile of v3, /device:TPU:2, one launch (start us, length us, event | category | flops | bytes accessed | tf_op | source)
XLA Modules:
  0.0 117.1 jit_solution(11130949168160136379)
XLA Ops:
  0.6 1.1 convert_element_type.40
  1.9 1.3 %collective-permute-done = bf16[128,512]{1,0:T(8,128)(2,1)S(1)} collective-permute-done((bf16[128,512]{1,0:T(8,128)(2,1)S(1)}, bf16[128,512]{1,0:T(8,128)(2,1)S(1)}, u32[]{:S(2)}, u32[]{:S(2)}) %collective-permute-start) | collective-permute-done | bytes 131104 | tf_op jit(solution)/shard_map/ppermute | solution.py:37
  3.4 1.6 %collective-permute-start.3 = (bf16[256,512]{1,0:T(8,128)(2,1)S(1)}, bf16[256,512]{1,0:T(8,128)(2,1)S(1)}, u32[]{:S(2)}, u32[]{:S(2)}) collective-permute-start(bf16[256,512]{1,0:T(8,128)(2,1)S(1)} %maximum_select_fusion.a), channel_id=1, source_target_pairs={{0,2},{1,9},{2,4},{3,11},{4,6},{5,13},{6,0},{7,15},{8,10},{9,17},{... | collective-permute-start | bytes 786440 | tf_op jit(solution)/shard_map/ppermute | solution.py:37
  5.0 2.8 %collective-permute-start.2 = (bf16[256,512]{1,0:T(8,128)(2,1)S(1)}, bf16[256,512]{1,0:T(8,128)(2,1)S(1)}, u32[]{:S(2)}, u32[]{:S(2)}) collective-permute-start(bf16[256,512]{1,0:T(8,128)(2,1)S(1)} %maximum_select_fusion.a), channel_id=1, source_target_pairs={{0,4},{1,17},{2,6},{3,19},{4,0},{5,21},{6,2},{7,23},{8,12},{9,25},... | collective-permute-start | bytes 786440 | tf_op jit(solution)/shard_map/ppermute | solution.py:37
  7.8 0.4 collective-permute-start.1
  8.2 1.9 %collective-permute-done.3.d = bf16[256,512]{1,0:T(8,128)(2,1)S(1)} collective-permute-done((bf16[256,512]{1,0:T(8,128)(2,1)S(1)}, bf16[256,512]{1,0:T(8,128)(2,1)S(1)}, u32[]{:S(2)}, u32[]{:S(2)}) %collective-permute-start.3) | collective-permute-done | bytes 262176 | tf_op jit(solution)/shard_map/ppermute | solution.py:37
  10.1 2.6 %constant_dynamic-slice_fusion = (bf16[768,512]{1,0:T(8,128)(2,1)}, bf16[768,512]{1,0:T(8,128)(2,1)}) fusion(bf16[768,1024]{1,0:T(8,128)(2,1)} %param.8, s32[]{:T(128)S(6)} %select_n.18, s32[]{:T(128)S(6)} %select_n.17), kind=kLoop, calls=%fused_computation.12 | loop fusion | bytes 3145736 | tf_op jit(solution)/shard_map/dynamic_slice | solution.py:221
  12.7 0.2 collective-permute-done.2.c
  13.0 0.7 constant_dynamic-update-slice_fusion.1
  13.7 0.7 constant_dynamic-update-slice_fusion
  14.4 1.6 %collective-permute-start.8 = (bf16[512,512]{1,0:T(8,128)(2,1)}, bf16[512,512]{1,0:T(8,128)(2,1)S(1)}, u32[]{:S(2)}, u32[]{:S(2)}) collective-permute-start(bf16[512,512]{1,0:T(8,128)(2,1)} %constant_dynamic-update-slice_fusion), channel_id=1, source_target_pairs={{0,8},{1,3},{2,10},{3,5},{4,12},{5,7},{6,14},{7,1},{8,16},{9,11},{... | collective-permute-start | bytes 1572872 | tf_op jit(solution)/shard_map/ppermute | solution.py:37
  16.0 0.8 pad_maximum_fusion
  16.8 2.3 %collective-permute-start.5 = (bf16[512,512]{1,0:T(8,128)(2,1)}, bf16[512,512]{1,0:T(8,128)(2,1)S(1)}, u32[]{:S(2)}, u32[]{:S(2)}) collective-permute-start(bf16[512,512]{1,0:T(8,128)(2,1)} %pad_maximum_fusion), channel_id=1, source_target_pairs={{0,24},{1,7},{2,26},{3,1},{4,28},{5,3},{6,30},{7,5},{8,0},{9,15},{... | collective-permute-start | bytes 1572872 | tf_op jit(solution)/shard_map/ppermute | solution.py:37
  19.1 1.2 collective-permute-start.6
  20.3 0.9 collective-permute-start.7
  21.1 1.8 %collective-permute-start.11 = (bf16[768,512]{1,0:T(8,128)(2,1)}, bf16[768,512]{1,0:T(8,128)(2,1)}, u32[]{:S(2)}, u32[]{:S(2)}) collective-permute-start(bf16[768,512]{1,0:T(8,128)(2,1)} %get-tuple-element.51), channel_id=1, source_target_pairs={{0,1},{1,0},{2,3},{3,2},{4,5},{5,4},{6,7},{7,6},{8,9},{9,8},{10,11... | collective-permute-start | bytes 2359304 | tf_op jit(solution)/shard_map/ppermute | solution.py:37
  23.0 2.0 %collective-permute-done.8.high_3 = bf16[512,512]{1,0:T(8,128)(2,1)S(1)} collective-permute-done((bf16[512,512]{1,0:T(8,128)(2,1)}, bf16[512,512]{1,0:T(8,128)(2,1)S(1)}, u32[]{:S(2)}, u32[]{:S(2)}) %collective-permute-start.8) | collective-permute-done | bytes 524320 | tf_op jit(solution)/shard_map/ppermute | solution.py:37
  25.0 0.4 collective-permute-start.10
  25.4 0.8 collective-permute-done.5.low_1
  26.2 3.5 %collective-permute-start.9 = (bf16[512,512]{1,0:T(8,128)(2,1)S(1)}, bf16[512,512]{1,0:T(8,128)(2,1)S(1)}, u32[]{:S(2)}, u32[]{:S(2)}) collective-permute-start(bf16[512,512]{1,0:T(8,128)(2,1)S(1)} %collective-permute-done.5.low_1), channel_id=1, source_target_pairs={{0,24},{1,7},{2,26},{3,1},{4,28},{5,3},{6,30},{7,5},{8,0},{9,15},{... | collective-permute-start | bytes 1572872 | tf_op jit(solution)/shard_map/ppermute | solution.py:37
  30.6 5.2 %first.1 = (bf16[768,512]{1,0:T(8,128)(2,1)S(1)}, bf16[768,512]{1,0:T(8,128)(2,1)S(1)}, bf16[768,4096]{1,0:T(8,128)(2,1)S(1)}, bf16[768,4096]{1,0:T(8,128)(2,1)S(1)}) custom-call(bf16[256,512]{1,0:T(8,128)(2,1)S(1)} %maximum_select_fusion.a, bf16[256,512]{1,0:T(8,128)(2,1)S(1)} %collective-permute-done.1.b, bf16[256,512]{1,0:T(8,128)(2,1)S(1)} %collective-permute-done.2.c, ...), custom_call_target="tpu_custom_call" | custom-call | tf_op jit(solution)/shard_map/first/pallas_call | solution.py:230
  35.8 4.6 %more.1 = (bf16[768,512]{1,0:T(8,128)(2,1)S(1)}, bf16[768,512]{1,0:T(8,128)(2,1)S(1)}) custom-call(bf16[768,512]{1,0:T(8,128)(2,1)S(1)} %get-tuple-element.43.acc, bf16[768,512]{1,0:T(8,128)(2,1)S(1)} %get-tuple-element.44.acc_other, bf16[512,512]{1,0:T(8,128)(2,1)S(1)} %collective-permute-done.5.low_1, bf16[512,512]{1,0:T(8,128)(2,1)} %collective-permute-done.6.high_1, ...), custom_call_target="tpu_custom_call" | custom-call | flops 4000000000 | bytes 1048576 | tf_op jit(solution)/shard_map/more/pallas_call | solution.py:180
  40.6 4.2 %late.1 = (bf16[512,768]{1,0:T(8,128)(2,1)S(1)}, bf16[512,768]{1,0:T(8,128)(2,1)S(1)}, bf16[512,512]{1,0:T(8,128)(2,1)S(1)}, bf16[512,512]{1,0:T(8,128)(2,1)S(1)}, f32[8,512]{1,0:T(8,128)S(1)}) custom-call(bf16[768,512]{1,0:T(8,128)(2,1)S(1)} %get-tuple-element.48.acc, bf16[768,512]{1,0:T(8,128)(2,1)S(1)} %get-tuple-element.49.acc_other, ...), custom_call_target="tpu_custom_call" | custom-call | tf_op jit(solution)/shard_map/late/pallas_call | solution.py:248
  44.7 0.6 collective-permute-start.16
  45.3 1.5 %collective-permute-start.12 = (bf16[512,512]{1,0:T(8,128)(2,1)S(1)}, bf16[512,512]{1,0:T(8,128)(2,1)S(1)}, u32[]{:S(2)}, u32[]{:S(2)}) collective-permute-start(bf16[512,512]{1,0:T(8,128)(2,1)S(1)} %get-tuple-element.56), channel_id=1, source_target_pairs={{0,8},{1,3},{2,10},{3,5},{4,12},{5,7},{6,14},{7,1},{8,16},{9,11},{... | collective-permute-start | bytes 1572872 | tf_op jit(solution)/shard_map/ppermute | solution.py:37
  46.8 1.8 %sides_near.1 = (bf16[512,512]{1,0:T(8,128)(2,1)S(1)}, bf16[512,512]{1,0:T(8,128)(2,1)S(1)}) custom-call(bf16[512,768]{1,0:T(8,128)(2,1)S(1)} %get-tuple-element.53.s, bf16[512,768]{1,0:T(8,128)(2,1)S(1)} %get-tuple-element.54.so, bf16[768,4096]{1,0:T(8,128)(2,1)S(1)} %get-tuple-element.46.x, bf16[768,4096]{1,0:T(8,128)(2,1)S(1)} %get-tuple-element.47.xo), custom_call_target="tpu_custom_call" | custom-call | flops 2000000000 | bytes 1048576 | tf_op jit(solution)/shard_map/sides_near/pallas_call | solution.py:180
  48.7 1.8 %collective-permute-start.14 = (bf16[512,512]{1,0:T(8,128)(2,1)S(1)}, bf16[512,512]{1,0:T(8,128)(2,1)S(1)}, u32[]{:S(2)}, u32[]{:S(2)}) collective-permute-start(bf16[512,512]{1,0:T(8,128)(2,1)S(1)} %get-tuple-element.57), channel_id=1, source_target_pairs={{0,24},{1,7},{2,26},{3,1},{4,28},{5,3},{6,30},{7,5},{8,0},{9,15},{... | collective-permute-start | bytes 1572872 | tf_op jit(solution)/shard_map/ppermute | solution.py:37
  50.4 0.3 collective-permute-start.15
  50.8 1.8 %sides_rest.1 = (bf16[512,512]{1,0:T(8,128)(2,1)S(1)}, bf16[512,512]{1,0:T(8,128)(2,1)S(1)}) custom-call(bf16[512,768]{1,0:T(8,128)(2,1)S(1)} %get-tuple-element.53.s, bf16[512,768]{1,0:T(8,128)(2,1)S(1)} %get-tuple-element.54.so, bf16[768,4096]{1,0:T(8,128)(2,1)S(1)} %get-tuple-element.46.x, bf16[768,4096]{1,0:T(8,128)(2,1)S(1)} %get-tuple-element.47.xo), custom_call_target="tpu_custom_call" | custom-call | flops 2000000000 | bytes 1048576 | tf_op jit(solution)/shard_map/sides_rest/pallas_call | solution.py:180
  52.6 1.4 %collective-permute-done.16 = bf16[512,512]{1,0:T(8,128)(2,1)S(1)} collective-permute-done((bf16[512,512]{1,0:T(8,128)(2,1)S(1)}, bf16[512,512]{1,0:T(8,128)(2,1)S(1)}, u32[]{:S(2)}, u32[]{:S(2)}) %collective-permute-start.16) | collective-permute-done | bytes 524320 | tf_op jit(solution)/shard_map/ppermute | solution.py:37
  54.1 1.8 %collective-permute-start.17 = (bf16[512,512]{1,0:T(8,128)(2,1)S(1)}, bf16[512,512]{1,0:T(8,128)(2,1)S(1)}, u32[]{:S(2)}, u32[]{:S(2)}) collective-permute-start(bf16[512,512]{1,0:T(8,128)(2,1)S(1)} %add_convert_fusion), channel_id=1, source_target_pairs={{0,24},{1,7},{2,26},{3,1},{4,28},{5,3},{6,30},{7,5},{8,0},{9,15},{... | collective-permute-start | bytes 1572872 | tf_op jit(solution)/shard_map/ppermute | solution.py:37
  56.0 0.4 collective-permute-start.13
  56.4 1.8 %kept.1 = f32[512,1024]{1,0:T(8,128)S(1)} custom-call(bf16[512,768]{1,0:T(8,128)(2,1)S(1)} %get-tuple-element.53.s, bf16[512,768]{1,0:T(8,128)(2,1)S(1)} %get-tuple-element.54.so, bf16[768,4096]{1,0:T(8,128)(2,1)S(1)} %get-tuple-element.46.x, bf16[768,4096]{1,0:T(8,128)(2,1)S(1)} %get-tuple-element.47.xo), custom_call_target="tpu_custom_call" | custom-call | flops 2000000000 | bytes 1048576 | tf_op jit(solution)/shard_map/kept/pallas_call | solution.py:180
  58.3 1.3 %collective-permute-done.14.down_a = bf16[512,512]{1,0:T(8,128)(2,1)S(1)} collective-permute-done((bf16[512,512]{1,0:T(8,128)(2,1)S(1)}, bf16[512,512]{1,0:T(8,128)(2,1)S(1)}, u32[]{:S(2)}, u32[]{:S(2)}) %collective-permute-start.14) | collective-permute-done | bytes 524320 | tf_op jit(solution)/shard_map/ppermute | solution.py:37
  59.6 1.7 %collective-permute-done.15.up_b = bf16[512,512]{1,0:T(8,128)(2,1)S(1)} collective-permute-done((bf16[512,512]{1,0:T(8,128)(2,1)S(1)}, bf16[512,512]{1,0:T(8,128)(2,1)S(1)}, u32[]{:S(2)}, u32[]{:S(2)}) %collective-permute-start.15) | collective-permute-done | bytes 524320 | tf_op jit(solution)/shard_map/ppermute | solution.py:37
  61.3 3.9 %collective-permute-done.17.down_b = bf16[512,512]{1,0:T(8,128)(2,1)S(1)} collective-permute-done((bf16[512,512]{1,0:T(8,128)(2,1)S(1)}, bf16[512,512]{1,0:T(8,128)(2,1)S(1)}, u32[]{:S(2)}, u32[]{:S(2)}) %collective-permute-start.17) | collective-permute-done | bytes 524320 | tf_op jit(solution)/shard_map/ppermute | solution.py:37
  65.2 1.7 %collective-permute-done.13.up_a = bf16[512,512]{1,0:T(8,128)(2,1)S(1)} collective-permute-done((bf16[512,512]{1,0:T(8,128)(2,1)S(1)}, bf16[512,512]{1,0:T(8,128)(2,1)S(1)}, u32[]{:S(2)}, u32[]{:S(2)}) %collective-permute-start.13) | collective-permute-done | bytes 524320 | tf_op jit(solution)/shard_map/ppermute | solution.py:37
  66.9 0.3 fold.1
  67.2 1.1 collective-permute-start.18
  68.3 6.2 %collective-permute-start.19 = (bf16[512,256]{1,0:T(8,128)(2,1)S(1)}, bf16[512,256]{1,0:T(8,128)(2,1)S(1)}, u32[]{:S(2)}, u32[]{:S(2)}) collective-permute-start(bf16[512,256]{1,0:T(8,128)(2,1)S(1)} %get-tuple-element.63), channel_id=1, source_target_pairs={{0,4},{1,17},{2,6},{3,19},{4,0},{5,21},{6,2},{7,23},{8,12},{9,25},... | collective-permute-start | bytes 786440 | tf_op jit(solution)/shard_map/ppermute | solution.py:37
  74.5 2.3 %collective-permute-done.18.a = bf16[512,256]{1,0:T(8,128)(2,1)S(1)} collective-permute-done((bf16[512,256]{1,0:T(8,128)(2,1)S(1)}, bf16[512,256]{1,0:T(8,128)(2,1)S(1)}, u32[]{:S(2)}, u32[]{:S(2)}) %collective-permute-start.18) | collective-permute-done | bytes 262176 | tf_op jit(solution)/shard_map/ppermute | solution.py:37
  76.8 2.1 %collective-permute-done.19.b = bf16[512,256]{1,0:T(8,128)(2,1)S(1)} collective-permute-done((bf16[512,256]{1,0:T(8,128)(2,1)S(1)}, bf16[512,256]{1,0:T(8,128)(2,1)S(1)}, u32[]{:S(2)}, u32[]{:S(2)}) %collective-permute-start.19) | collective-permute-done | bytes 262176 | tf_op jit(solution)/shard_map/ppermute | solution.py:37
  79.0 2.7 %collective-permute-done.20.c = bf16[512,256]{1,0:T(8,128)(2,1)S(1)} collective-permute-done((bf16[512,256]{1,0:T(8,128)(2,1)S(1)}, bf16[512,256]{1,0:T(8,128)(2,1)S(1)}, u32[]{:S(2)}, u32[]{:S(2)}) %collective-permute-start.20) | collective-permute-done | bytes 262176 | tf_op jit(solution)/shard_map/ppermute | solution.py:37
  81.9 1.3 %collective-permute-done.21.refs_1_ = bf16[512,128]{1,0:T(8,128)(2,1)S(1)} collective-permute-done((bf16[512,128]{1,0:T(8,128)(2,1)S(1)}, bf16[512,128]{1,0:T(8,128)(2,1)S(1)}, u32[]{:S(2)}, u32[]{:S(2)}) %collective-permute-start.21) | collective-permute-done | bytes 131104 | tf_op jit(solution)/shard_map/ppermute | solution.py:37
  83.3 1.4 %inner_step.1 = (f32[128,1024]{1,0:T(8,128)}, f32[128,1024]{1,0:T(8,128)}, bf16[128,1024]{1,0:T(8,128)(2,1)S(1)}) custom-call(f32[8,512]{1,0:T(8,128)S(1)} %get-tuple-element.52.rates, f32[128,1024]{1,0:T(8,128)S(1)} %bitcast.14, f32[128,1024]{1,0:T(8,128)S(1)} %bitcast.15, f32[128,1024]{1,0:T(8,128)S(1)} %copy-done, ...), custom_call_target="tpu_custom_call" | custom-call | flops 1000000000 | bytes 1048576 | tf_op jit(solution)/shard_map/inner_step/pallas_call | solution.py:180
  84.7 17.7 %all_to_all.10 = bf16[8,16,1024]{2,1,0:T(8,128)(2,1)S(1)} all-to-all(bf16[8,16,1024]{2,1,0:T(8,128)(2,1)S(1)} %bitcast.13), channel_id=1, replica_groups=mesh['island'=8,'fsdp'=8,'dp'=4] {'island'}, dimensions={0} | all-to-all | bytes 524288 | tf_op jit(solution)/shard_map/all_to_all | solution.py:299
  102.5 13.5 %all_to_all.11 = bf16[8,16,1024]{2,1,0:T(8,128)(2,1)S(1)} all-to-all(bf16[8,16,1024]{2,1,0:T(8,128)(2,1)S(1)} %broadcast_in_dim.9), channel_id=1, replica_groups=mesh['island'=8,'fsdp'=8,'dp'=4] {'island'}, dimensions={0} | all-to-all | bytes 524288 | tf_op jit(solution)/shard_map/all_to_all | solution.py:302
  116.0 1.1 fusion.1
  (30 shorter events, 1.1 us)
Async XLA Ops:
  1.8 1.4 %collective-permute-start = (bf16[128,512]{1,0:T(8,128)(2,1)S(1)}, bf16[128,512]{1,0:T(8,128)(2,1)S(1)}, u32[]{:S(2)}, u32[]{:S(2)}) collective-permute-start(bf16[128,512]{1,0:T(8,128)(2,1)S(1)} %get-tuple-element.75), channel_id=1, source_target_pairs={{0,1},{1,0},{2,3},{3,2},{4,5},{5,4},{6,7},{7,6},{8,9},{9,8},{10,11... | collective-permute-start | bytes 393224 | tf_op jit(solution)/shard_map/ppermute | solution.py:37
  3.2 13.6 %collective-permute-start.4 = (bf16[768,4096]{1,0:T(8,128)(2,1)}, bf16[768,4096]{1,0:T(8,128)(2,1)}, u32[]{:S(2)}, u32[]{:S(2)}) collective-permute-start(bf16[768,4096]{1,0:T(8,128)(2,1)} %x.1), channel_id=1, source_target_pairs={{0,1},{1,0},{2,3},{3,2},{4,5},{5,4},{6,7},{7,6},{8,9},{9,8},{10,11... | collective-permute-start | bytes 18874376 | tf_op jit(solution)/shard_map/ppermute | solution.py:37
  3.4 6.7 %collective-permute-start.3 = (bf16[256,512]{1,0:T(8,128)(2,1)S(1)}, bf16[256,512]{1,0:T(8,128)(2,1)S(1)}, u32[]{:S(2)}, u32[]{:S(2)}) collective-permute-start(bf16[256,512]{1,0:T(8,128)(2,1)S(1)} %maximum_select_fusion.a), channel_id=1, source_target_pairs={{0,2},{1,9},{2,4},{3,11},{4,6},{5,13},{6,0},{7,15},{8,10},{9,17},{... | collective-permute-start | bytes 786440 | tf_op jit(solution)/shard_map/ppermute | solution.py:37
  5.0 8.0 %collective-permute-start.2 = (bf16[256,512]{1,0:T(8,128)(2,1)S(1)}, bf16[256,512]{1,0:T(8,128)(2,1)S(1)}, u32[]{:S(2)}, u32[]{:S(2)}) collective-permute-start(bf16[256,512]{1,0:T(8,128)(2,1)S(1)} %maximum_select_fusion.a), channel_id=1, source_target_pairs={{0,4},{1,17},{2,6},{3,19},{4,0},{5,21},{6,2},{7,23},{8,12},{9,25},... | collective-permute-start | bytes 786440 | tf_op jit(solution)/shard_map/ppermute | solution.py:37
  7.8 8.2 %collective-permute-start.1 = (bf16[256,512]{1,0:T(8,128)(2,1)S(1)}, bf16[256,512]{1,0:T(8,128)(2,1)S(1)}, u32[]{:S(2)}, u32[]{:S(2)}) collective-permute-start(bf16[256,512]{1,0:T(8,128)(2,1)S(1)} %maximum_select_fusion.a), channel_id=1, source_target_pairs={{0,6},{1,25},{2,0},{3,27},{4,2},{5,29},{6,4},{7,31},{8,14},{9,1},{... | collective-permute-start | bytes 786440 | tf_op jit(solution)/shard_map/ppermute | solution.py:37
  14.4 10.6 %collective-permute-start.8 = (bf16[512,512]{1,0:T(8,128)(2,1)}, bf16[512,512]{1,0:T(8,128)(2,1)S(1)}, u32[]{:S(2)}, u32[]{:S(2)}) collective-permute-start(bf16[512,512]{1,0:T(8,128)(2,1)} %constant_dynamic-update-slice_fusion), channel_id=1, source_target_pairs={{0,8},{1,3},{2,10},{3,5},{4,12},{5,7},{6,14},{7,1},{8,16},{9,11},{... | collective-permute-start | bytes 1572872 | tf_op jit(solution)/shard_map/ppermute | solution.py:37
  16.8 9.4 %collective-permute-start.5 = (bf16[512,512]{1,0:T(8,128)(2,1)}, bf16[512,512]{1,0:T(8,128)(2,1)S(1)}, u32[]{:S(2)}, u32[]{:S(2)}) collective-permute-start(bf16[512,512]{1,0:T(8,128)(2,1)} %pad_maximum_fusion), channel_id=1, source_target_pairs={{0,24},{1,7},{2,26},{3,1},{4,28},{5,3},{6,30},{7,5},{8,0},{9,15},{... | collective-permute-start | bytes 1572872 | tf_op jit(solution)/shard_map/ppermute | solution.py:37
  19.1 16.7 %collective-permute-start.6 = (bf16[512,512]{1,0:T(8,128)(2,1)}, bf16[512,512]{1,0:T(8,128)(2,1)}, u32[]{:S(2)}, u32[]{:S(2)}) collective-permute-start(bf16[512,512]{1,0:T(8,128)(2,1)} %constant_dynamic-update-slice_fusion), channel_id=1, source_target_pairs={{0,24},{1,7},{2,26},{3,1},{4,28},{5,3},{6,30},{7,5},{8,0},{9,15},{... | collective-permute-start | bytes 1572872 | tf_op jit(solution)/shard_map/ppermute | solution.py:37
  20.3 15.5 %collective-permute-start.7 = (bf16[512,512]{1,0:T(8,128)(2,1)}, bf16[512,512]{1,0:T(8,128)(2,1)}, u32[]{:S(2)}, u32[]{:S(2)}) collective-permute-start(bf16[512,512]{1,0:T(8,128)(2,1)} %pad_maximum_fusion), channel_id=1, source_target_pairs={{0,8},{1,3},{2,10},{3,5},{4,12},{5,7},{6,14},{7,1},{8,16},{9,11},{... | collective-permute-start | bytes 1572872 | tf_op jit(solution)/shard_map/ppermute | solution.py:37
  21.1 19.3 %collective-permute-start.11 = (bf16[768,512]{1,0:T(8,128)(2,1)}, bf16[768,512]{1,0:T(8,128)(2,1)}, u32[]{:S(2)}, u32[]{:S(2)}) collective-permute-start(bf16[768,512]{1,0:T(8,128)(2,1)} %get-tuple-element.51), channel_id=1, source_target_pairs={{0,1},{1,0},{2,3},{3,2},{4,5},{5,4},{6,7},{7,6},{8,9},{9,8},{10,11... | collective-permute-start | bytes 2359304 | tf_op jit(solution)/shard_map/ppermute | solution.py:37
  25.0 15.5 %collective-permute-start.10 = (bf16[512,512]{1,0:T(8,128)(2,1)S(1)}, bf16[512,512]{1,0:T(8,128)(2,1)S(1)}, u32[]{:S(2)}, u32[]{:S(2)}) collective-permute-start(bf16[512,512]{1,0:T(8,128)(2,1)S(1)} %collective-permute-done.8.high_3), channel_id=1, source_target_pairs={{0,8},{1,3},{2,10},{3,5},{4,12},{5,7},{6,14},{7,1},{8,16},{9,11},{... | collective-permute-start | bytes 1572872 | tf_op jit(solution)/shard_map/ppermute | solution.py:37
  26.2 14.3 %collective-permute-start.9 = (bf16[512,512]{1,0:T(8,128)(2,1)S(1)}, bf16[512,512]{1,0:T(8,128)(2,1)S(1)}, u32[]{:S(2)}, u32[]{:S(2)}) collective-permute-start(bf16[512,512]{1,0:T(8,128)(2,1)S(1)} %collective-permute-done.5.low_1), channel_id=1, source_target_pairs={{0,24},{1,7},{2,26},{3,1},{4,28},{5,3},{6,30},{7,5},{8,0},{9,15},{... | collective-permute-start | bytes 1572872 | tf_op jit(solution)/shard_map/ppermute | solution.py:37
  44.7 9.3 %collective-permute-start.16 = (bf16[512,512]{1,0:T(8,128)(2,1)S(1)}, bf16[512,512]{1,0:T(8,128)(2,1)S(1)}, u32[]{:S(2)}, u32[]{:S(2)}) collective-permute-start(bf16[512,512]{1,0:T(8,128)(2,1)S(1)} %get-tuple-element.60), channel_id=1, source_target_pairs={{0,24},{1,7},{2,26},{3,1},{4,28},{5,3},{6,30},{7,5},{8,0},{9,15},{... | collective-permute-start | bytes 1572872 | tf_op jit(solution)/shard_map/ppermute | solution.py:37
  45.3 10.6 %collective-permute-start.12 = (bf16[512,512]{1,0:T(8,128)(2,1)S(1)}, bf16[512,512]{1,0:T(8,128)(2,1)S(1)}, u32[]{:S(2)}, u32[]{:S(2)}) collective-permute-start(bf16[512,512]{1,0:T(8,128)(2,1)S(1)} %get-tuple-element.56), channel_id=1, source_target_pairs={{0,8},{1,3},{2,10},{3,5},{4,12},{5,7},{6,14},{7,1},{8,16},{9,11},{... | collective-permute-start | bytes 1572872 | tf_op jit(solution)/shard_map/ppermute | solution.py:37
  48.7 11.0 %collective-permute-start.14 = (bf16[512,512]{1,0:T(8,128)(2,1)S(1)}, bf16[512,512]{1,0:T(8,128)(2,1)S(1)}, u32[]{:S(2)}, u32[]{:S(2)}) collective-permute-start(bf16[512,512]{1,0:T(8,128)(2,1)S(1)} %get-tuple-element.57), channel_id=1, source_target_pairs={{0,24},{1,7},{2,26},{3,1},{4,28},{5,3},{6,30},{7,5},{8,0},{9,15},{... | collective-permute-start | bytes 1572872 | tf_op jit(solution)/shard_map/ppermute | solution.py:37
  50.4 10.9 %collective-permute-start.15 = (bf16[512,512]{1,0:T(8,128)(2,1)S(1)}, bf16[512,512]{1,0:T(8,128)(2,1)S(1)}, u32[]{:S(2)}, u32[]{:S(2)}) collective-permute-start(bf16[512,512]{1,0:T(8,128)(2,1)S(1)} %get-tuple-element.58), channel_id=1, source_target_pairs={{0,8},{1,3},{2,10},{3,5},{4,12},{5,7},{6,14},{7,1},{8,16},{9,11},{... | collective-permute-start | bytes 1572872 | tf_op jit(solution)/shard_map/ppermute | solution.py:37
  54.1 11.1 %collective-permute-start.17 = (bf16[512,512]{1,0:T(8,128)(2,1)S(1)}, bf16[512,512]{1,0:T(8,128)(2,1)S(1)}, u32[]{:S(2)}, u32[]{:S(2)}) collective-permute-start(bf16[512,512]{1,0:T(8,128)(2,1)S(1)} %add_convert_fusion), channel_id=1, source_target_pairs={{0,24},{1,7},{2,26},{3,1},{4,28},{5,3},{6,30},{7,5},{8,0},{9,15},{... | collective-permute-start | bytes 1572872 | tf_op jit(solution)/shard_map/ppermute | solution.py:37
  56.0 10.9 %collective-permute-start.13 = (bf16[512,512]{1,0:T(8,128)(2,1)S(1)}, bf16[512,512]{1,0:T(8,128)(2,1)S(1)}, u32[]{:S(2)}, u32[]{:S(2)}) collective-permute-start(bf16[512,512]{1,0:T(8,128)(2,1)S(1)} %add_convert_fusion.1), channel_id=1, source_target_pairs={{0,8},{1,3},{2,10},{3,5},{4,12},{5,7},{6,14},{7,1},{8,16},{9,11},{... | collective-permute-start | bytes 1572872 | tf_op jit(solution)/shard_map/ppermute | solution.py:37
  58.3 25.0 %copy-start = (f32[128,1024]{1,0:T(8,128)S(1)}, f32[128,1024]{1,0:T(8,128)}, u32[]{:S(2)}) copy-start(f32[128,1024]{1,0:T(8,128)} %weight.1) | copy-start | bytes 1572868
  58.3 25.0 %copy-start.1 = (f32[1,128,1024]{2,1,0:T(8,128)S(1)}, f32[1,128,1024]{2,1,0:T(8,128)}, u32[]{:S(2)}) copy-start(f32[1,128,1024]{2,1,0:T(8,128)} %param.11) | copy-start | bytes 1572868
  58.3 25.0 %copy-start.2 = (f32[1,128,1024]{2,1,0:T(8,128)S(1)}, f32[1,128,1024]{2,1,0:T(8,128)}, u32[]{:S(2)}) copy-start(f32[1,128,1024]{2,1,0:T(8,128)} %param.12) | copy-start | bytes 1572868
  58.3 57.7 %copy-start.3 = (f32[128,1024]{1,0:T(8,128)S(1)}, f32[128,1024]{1,0:T(8,128)}, u32[]{:S(2)}) copy-start(f32[128,1024]{1,0:T(8,128)} %param.10) | copy-start | bytes 1572868
  67.2 9.6 %collective-permute-start.18 = (bf16[512,256]{1,0:T(8,128)(2,1)S(1)}, bf16[512,256]{1,0:T(8,128)(2,1)S(1)}, u32[]{:S(2)}, u32[]{:S(2)}) collective-permute-start(bf16[512,256]{1,0:T(8,128)(2,1)S(1)} %get-tuple-element.62), channel_id=1, source_target_pairs={{0,2},{1,9},{2,4},{3,11},{4,6},{5,13},{6,0},{7,15},{8,10},{9,17},{... | collective-permute-start | bytes 786440 | tf_op jit(solution)/shard_map/ppermute | solution.py:37
  68.3 10.7 %collective-permute-start.19 = (bf16[512,256]{1,0:T(8,128)(2,1)S(1)}, bf16[512,256]{1,0:T(8,128)(2,1)S(1)}, u32[]{:S(2)}, u32[]{:S(2)}) collective-permute-start(bf16[512,256]{1,0:T(8,128)(2,1)S(1)} %get-tuple-element.63), channel_id=1, source_target_pairs={{0,4},{1,17},{2,6},{3,19},{4,0},{5,21},{6,2},{7,23},{8,12},{9,25},... | collective-permute-start | bytes 786440 | tf_op jit(solution)/shard_map/ppermute | solution.py:37
  74.5 7.2 %collective-permute-start.20 = (bf16[512,256]{1,0:T(8,128)(2,1)S(1)}, bf16[512,256]{1,0:T(8,128)(2,1)S(1)}, u32[]{:S(2)}, u32[]{:S(2)}) collective-permute-start(bf16[512,256]{1,0:T(8,128)(2,1)S(1)} %get-tuple-element.64), channel_id=1, source_target_pairs={{0,6},{1,25},{2,0},{3,27},{4,2},{5,29},{6,4},{7,31},{8,14},{9,1},{... | collective-permute-start | bytes 786440 | tf_op jit(solution)/shard_map/ppermute | solution.py:37
  81.8 1.4 %collective-permute-start.21 = (bf16[512,128]{1,0:T(8,128)(2,1)S(1)}, bf16[512,128]{1,0:T(8,128)(2,1)S(1)}, u32[]{:S(2)}, u32[]{:S(2)}) collective-permute-start(bf16[512,128]{1,0:T(8,128)(2,1)S(1)} %get-tuple-element.66), channel_id=1, source_target_pairs={{0,1},{1,0},{2,3},{3,2},{4,5},{5,4},{6,7},{7,6},{8,9},{9,8},{10,11... | collective-permute-start | bytes 393224 | tf_op jit(solution)/shard_map/ppermute | solution.py:37

commit v4 on v3

--- a/solution.py
+++ b/solution.py
@@ -109,17 +109,22 @@
         ref[...] = total.astype(ref.dtype)
 
 
-def late_kernel(scales, acc, acc_other, va, vb, x, xo, rates, t, to, s_ref, so_ref, relay_a, relay_b, rates_out, aims, sems):
-    place = here()
-    copies = [pltpu.make_async_copy(ref, aims.at[i], sems.at[i]) for i, ref in enumerate((t, to))]
-    for copy in copies:
-        copy.start()
+def stack_kernel(a, b, out):
+    rows = a.shape[0]
+    out[:rows, :] = a[...]
+    out[rows:, :] = b[...]
+
+
+def late_kernel(scales, acc, acc_other, va, vb, x, xo, to, t, s_ref, so_ref, relay_a, relay_b, aims, sem):
+    place = here()
+    fetch = pltpu.make_async_copy(t, aims, sem)
+    fetch.start()
     inv_width, inv_count = scales
-    rates_out[...] = rates[...]
-    for i, (tokens, total, out) in enumerate(((x, acc, s_ref), (xo, acc_other, so_ref))):
+    for tokens, total, goals, out in ((xo, acc_other, to, so_ref), (x, acc, aims, s_ref)):
         proj = total[...].astype(jnp.float32) + product(place, tokens, 2, LOW, va[...]) + product(place, tokens, 2, HIGH, vb[...])
-        copies[i].wait()
-        scaled = (proj * inv_width - aims[i].astype(jnp.float32)) * inv_count
+        if goals is aims:
+            fetch.wait()
+        scaled = (proj * inv_width - goals[...].astype(jnp.float32)) * inv_count
         out[...] = scaled.T.astype(jnp.bfloat16)
     for out, members in ((relay_a, LOW), (relay_b, HIGH)):
         for k, m in enumerate(members):
@@ -148,7 +153,8 @@
         outs[m][...] = total.astype(outs[m].dtype)
 
 
-def split_kernel(own, a, b, c, mine, theirs):
+def split_kernel(own, a, b, c, rates, mine, theirs, rates_out):
+    rates_out[...] = rates[...]
     total = own[...] + a[...].astype(jnp.float32) + b[...].astype(jnp.float32) + c[...].astype(jnp.float32)
     core = here()[2]
     low, high = total[:, : SIDE // 2], total[:, SIDE // 2 :]
@@ -221,10 +227,13 @@
     goals_other = lax.dynamic_slice_in_dim(targets, (1 - core) * half, half, 1)
     inner[2], goals, goals_other = lax.optimization_barrier((inner[2], goals, goals_other))
     goals_other = send(goals_other, partner)
-    low, high = jnp.concatenate(inner[:2], axis=0), jnp.concatenate(inner[2:], axis=0)
+    both = [((2 * inner[0].shape[0], half), bf16)]
+    (high,) = local(stack_kernel, both, LIMIT_B, "stack", *inner[2:])
+    (low,) = local(stack_kernel, both, LIMIT_B, "stack", *inner[:2])
     low, tokens_other = lax.optimization_barrier((low, tokens_other))
     low_1, high_3 = send(low, far(-1)), send(high, far(1))
-    high_1, low_3 = send(high, far(-1)), send(low, far(1))
+    low_3 = send(low, far(1))
+    high_1 = send(high, far(-1))
     low_2, high_2 = send(low_1, far(-1)), send(high_3, far(1))
     hbm = pl.BlockSpec(memory_space=pltpu.HBM)
     *acc, tokens, tokens_other = pl.pallas_call(
@@ -245,22 +254,22 @@
         more_kernel, [((count, half), bf16)] * 2, LIMIT_A, "more", *acc, low_1, high_1, low_3, high_3, *pair, cost=4
     )
     mid = ((half, 2 * SIDE), bf16)
-    s, so, relay_a, relay_b, rates = pl.pallas_call(
+    s, so, relay_a, relay_b = pl.pallas_call(
         functools.partial(late_kernel, scales),
         out_shape=[
-            jax.ShapeDtypeStruct(*k) for k in [((half, count), bf16)] * 2 + [mid] * 2 + [(rates.shape, f32)]
+            jax.ShapeDtypeStruct(*k) for k in [((half, count), bf16)] * 2 + [mid] * 2
         ],
-        in_specs=[VM] * 7 + [pl.BlockSpec(memory_space=pltpu.HBM)] * 2,
-        out_specs=[VM] * 5,
-        scratch_shapes=[pltpu.VMEM((2, count, half), bf16), pltpu.SemaphoreType.DMA((2,))],
+        in_specs=[VM] * 7 + [hbm],
+        out_specs=[VM] * 4,
+        scratch_shapes=[pltpu.VMEM((count, half), bf16), pltpu.SemaphoreType.DMA],
         compiler_params=params(LIMIT_A),
         name="late",
     )(
         *acc,
         low_2, high_2,
         *[pltpu.with_memory_space_constraint(k, pltpu.VMEM) for k in pair],
-        rates,
-        *[pltpu.with_memory_space_constraint(k, pltpu.HBM) for k in (goals, goals_other)],
+        goals_other,
+        pltpu.with_memory_space_constraint(goals, pltpu.HBM),
     )
     sides = functools.partial(sides_kernel, (HIGH, LOW))
     up_b, down_a = local(sides, [mid] * 2, LIMIT_B, "sides_near", s, so, *pair, cost=2)
@@ -278,12 +287,12 @@
         "fold",
         kept, up_a, down_a, up_b, down_b,
     )
-    mine, theirs = local(
+    mine, theirs, rates = local(
         split_kernel,
-        [((half, SIDE // 2), f32), ((half, SIDE // 2), bf16)],
+        [((half, SIDE // 2), f32), ((half, SIDE // 2), bf16), (rates.shape, f32)],
         LIMIT_B,
         "split",
-        parts[0], *[send(parts[k], near(k)) for k in (1, 2, 3)],
+        parts[0], *[send(parts[k], near(k)) for k in (2, 1, 3)], rates,
     )
     grads = [mine, send(theirs, partner)]
 

time: 118 us -> 119 us (level)
  blocking collectives: 31.2 us -> 36.3 us
  local copies, waits for them, and re-layouts: 4.29 us -> 2.58 us
    all_to_all x1, blocking collectives: 17.7 us -> 22.8 us  [per_device(): lax.all_to_all(pseudo.reshape(NZ, rows // NZ, columns), 'island', 0, 0, t...]
    pallas_call x7 -> x9, Pallas kernels: 12 us -> 11.5 us  [local(): pl.pallas_call(kernel, out_shape=[jax.ShapeDtypeStruct(*s) for s in shape...]
  transfers between devices with their start and end apart: 22 -> 22, of which waited for: 14 -> 13; matrix products, arithmetic and copies ran while one was open for 5% -> 2% of each run, Pallas kernels for 13% -> 12%
where the time goes in v4:
time: 119 us
  blocking collectives  36.3 us (31%)
  starting transfers between devices  30.6 us (26%)
  waiting for transfers between devices  24.3 us (20%)
  Pallas kernels  20.8 us (17%)
  other arithmetic  2.58 us (2%)
  local copies, waits for them, and re-layouts  2.58 us (2%)
  between operations  1.7 us (1%)
    ppermute x22, starting transfers between devices, send(): return lax.ppermute(value, AXES, pairs)  30.6 us
    ppermute x22, waiting for transfers between devices, send(): return lax.ppermute(value, AXES, pairs)  24.3 us
    all_to_all x1, blocking collectives, per_device(): lax.all_to_all(pseudo.reshape(NZ, rows // NZ, columns), 'island', 0, 0, t...  22.8 us
    all_to_all x1, blocking collectives, per_device(): lax.all_to_all(spread, 'island', 0, 0, tiled=True).reshape(rows, columns)  13.5 us
    pallas_call x9, Pallas kernels, local(): pl.pallas_call(kernel, out_shape=[jax.ShapeDtypeStruct(*s) for s in shape...  11.5 us
    pallas_call x1, Pallas kernels, per_device(): pl.pallas_call(first_kernel, out_shape=[jax.ShapeDtypeStruct((count, half...  5.15 us
    pallas_call x1, Pallas kernels, per_device(): pl.pallas_call(functools.partial(late_kernel, scales), out_shape=[jax.Sha...  4.16 us
  transfers between devices with their start and end apart: 22, of which 13 were waited for; matrix products, arithmetic and copies ran while one was open for 2% of the time, Pallas kernels for 12%

profile of v4, /device:TPU:2, one launch (start us, length us, event | category | flops | bytes accessed | tf_op | source)
XLA Modules:
  0.0 118.8 jit_solution(12063156932212636911)
XLA Ops:
  0.6 1.1 convert_element_type.40
  1.8 0.1 collective-permute-start
  1.9 1.3 %collective-permute-done = bf16[128,512]{1,0:T(8,128)(2,1)S(1)} collective-permute-done((bf16[128,512]{1,0:T(8,128)(2,1)S(1)}, bf16[128,512]{1,0:T(8,128)(2,1)S(1)}, u32[]{:S(2)}, u32[]{:S(2)}) %collective-permute-start) | collective-permute-done | bytes 131104 | tf_op jit(solution)/shard_map/ppermute | solution.py:37
  3.2 0.1 collective-permute-start.4
  3.4 1.6 %collective-permute-start.3 = (bf16[256,512]{1,0:T(8,128)(2,1)S(1)}, bf16[256,512]{1,0:T(8,128)(2,1)S(1)}, u32[]{:S(2)}, u32[]{:S(2)}) collective-permute-start(bf16[256,512]{1,0:T(8,128)(2,1)S(1)} %maximum_select_fusion.a), channel_id=1, source_target_pairs={{0,2},{1,9},{2,4},{3,11},{4,6},{5,13},{6,0},{7,15},{8,10},{9,17},{... | collective-permute-start | bytes 786440 | tf_op jit(solution)/shard_map/ppermute | solution.py:37
  5.0 2.8 %collective-permute-start.2 = (bf16[256,512]{1,0:T(8,128)(2,1)S(1)}, bf16[256,512]{1,0:T(8,128)(2,1)S(1)}, u32[]{:S(2)}, u32[]{:S(2)}) collective-permute-start(bf16[256,512]{1,0:T(8,128)(2,1)S(1)} %maximum_select_fusion.a), channel_id=1, source_target_pairs={{0,4},{1,17},{2,6},{3,19},{4,0},{5,21},{6,2},{7,23},{8,12},{9,25},... | collective-permute-start | bytes 786440 | tf_op jit(solution)/shard_map/ppermute | solution.py:37
  7.8 0.4 collective-permute-start.1
  8.2 1.9 %collective-permute-done.3.d.b = bf16[256,512]{1,0:T(8,128)(2,1)S(1)} collective-permute-done((bf16[256,512]{1,0:T(8,128)(2,1)S(1)}, bf16[256,512]{1,0:T(8,128)(2,1)S(1)}, u32[]{:S(2)}, u32[]{:S(2)}) %collective-permute-start.3) | collective-permute-done | bytes 262176 | tf_op jit(solution)/shard_map/ppermute | solution.py:37
  10.1 2.4 %constant_dynamic-slice_fusion = (bf16[768,512]{1,0:T(8,128)(2,1)S(1)}, bf16[768,512]{1,0:T(8,128)(2,1)}) fusion(bf16[768,1024]{1,0:T(8,128)(2,1)} %param.8, s32[]{:T(128)S(6)} %select_n.18, s32[]{:T(128)S(6)} %select_n.17), kind=kLoop, calls=%fused_computation.9 | loop fusion | bytes 3145736 | tf_op jit(solution)/shard_map/dynamic_slice | solution.py:227
  12.5 0.5 collective-permute-done.2.c.a
  13.0 1.7 %collective-permute-start.8 = (bf16[512,512]{1,0:T(8,128)(2,1)S(1)}, bf16[512,512]{1,0:T(8,128)(2,1)S(1)}, u32[]{:S(2)}, u32[]{:S(2)}) collective-permute-start(bf16[512,512]{1,0:T(8,128)(2,1)S(1)} %stack.24), channel_id=1, source_target_pairs={{0,8},{1,3},{2,10},{3,5},{4,12},{5,7},{6,14},{7,1},{8,16},{9,11},{... | collective-permute-start | bytes 1572872 | tf_op jit(solution)/shard_map/ppermute | solution.py:37
  14.7 1.0 collective-permute-done.1.b
  15.7 2.7 %collective-permute-start.5 = (bf16[512,512]{1,0:T(8,128)(2,1)S(1)}, bf16[512,512]{1,0:T(8,128)(2,1)S(1)}, u32[]{:S(2)}, u32[]{:S(2)}) collective-permute-start(bf16[512,512]{1,0:T(8,128)(2,1)S(1)} %stack.23), channel_id=1, source_target_pairs={{0,24},{1,7},{2,26},{3,1},{4,28},{5,3},{6,30},{7,5},{8,0},{9,15},{... | collective-permute-start | bytes 1572872 | tf_op jit(solution)/shard_map/ppermute | solution.py:37
  18.4 0.7 collective-permute-start.6
  19.2 1.3 %collective-permute-start.7 = (bf16[512,512]{1,0:T(8,128)(2,1)S(1)}, bf16[512,512]{1,0:T(8,128)(2,1)S(1)}, u32[]{:S(2)}, u32[]{:S(2)}) collective-permute-start(bf16[512,512]{1,0:T(8,128)(2,1)S(1)} %stack.23), channel_id=1, source_target_pairs={{0,8},{1,3},{2,10},{3,5},{4,12},{5,7},{6,14},{7,1},{8,16},{9,11},{... | collective-permute-start | bytes 1572872 | tf_op jit(solution)/shard_map/ppermute | solution.py:37
  20.4 0.2 collective-permute-start.11
  20.7 2.8 %collective-permute-done.8.high_3 = bf16[512,512]{1,0:T(8,128)(2,1)S(1)} collective-permute-done((bf16[512,512]{1,0:T(8,128)(2,1)S(1)}, bf16[512,512]{1,0:T(8,128)(2,1)S(1)}, u32[]{:S(2)}, u32[]{:S(2)}) %collective-permute-start.8) | collective-permute-done | bytes 524320 | tf_op jit(solution)/shard_map/ppermute | solution.py:37
  23.5 0.4 collective-permute-start.10
  23.8 1.3 %collective-permute-done.5.low_1 = bf16[512,512]{1,0:T(8,128)(2,1)S(1)} collective-permute-done((bf16[512,512]{1,0:T(8,128)(2,1)S(1)}, bf16[512,512]{1,0:T(8,128)(2,1)S(1)}, u32[]{:S(2)}, u32[]{:S(2)}) %collective-permute-start.5) | collective-permute-done | bytes 524320 | tf_op jit(solution)/shard_map/ppermute | solution.py:37
  25.1 3.7 %collective-permute-start.9 = (bf16[512,512]{1,0:T(8,128)(2,1)S(1)}, bf16[512,512]{1,0:T(8,128)(2,1)S(1)}, u32[]{:S(2)}, u32[]{:S(2)}) collective-permute-start(bf16[512,512]{1,0:T(8,128)(2,1)S(1)} %collective-permute-done.5.low_1), channel_id=1, source_target_pairs={{0,24},{1,7},{2,26},{3,1},{4,28},{5,3},{6,30},{7,5},{8,0},{9,15},{... | collective-permute-start | bytes 1572872 | tf_op jit(solution)/shard_map/ppermute | solution.py:37
  28.8 5.2 %first.1 = (bf16[768,512]{1,0:T(8,128)(2,1)S(1)}, bf16[768,512]{1,0:T(8,128)(2,1)S(1)}, bf16[768,4096]{1,0:T(8,128)(2,1)S(1)}, bf16[768,4096]{1,0:T(8,128)(2,1)S(1)}) custom-call(bf16[256,512]{1,0:T(8,128)(2,1)S(1)} %maximum_select_fusion.a, bf16[256,512]{1,0:T(8,128)(2,1)S(1)} %collective-permute-done.1.b, bf16[256,512]{1,0:T(8,128)(2,1)S(1)} %collective-permute-done.2.c.a, ...), custom_call_target="tpu_custom_call" | custom-call | tf_op jit(solution)/shard_map/first/pallas_call | solution.py:239
  34.0 3.4 %more.1 = (bf16[768,512]{1,0:T(8,128)(2,1)S(1)}, bf16[768,512]{1,0:T(8,128)(2,1)S(1)}) custom-call(bf16[768,512]{1,0:T(8,128)(2,1)S(1)} %get-tuple-element.43.acc, bf16[768,512]{1,0:T(8,128)(2,1)S(1)} %get-tuple-element.44.acc_other, bf16[512,512]{1,0:T(8,128)(2,1)S(1)} %collective-permute-done.5.low_1, bf16[512,512]{1,0:T(8,128)(2,1)S(1)} %collective-permute-done.6.high_1, ...), custom_call_target="tpu_custom_call" | custom-call | flops 4000000000 | bytes 1048576 | tf_op jit(solution)/shard_map/more/pallas_call | solution.py:186
  37.5 4.2 %late.1 = (bf16[512,768]{1,0:T(8,128)(2,1)S(1)}, bf16[512,768]{1,0:T(8,128)(2,1)S(1)}, bf16[512,512]{1,0:T(8,128)(2,1)S(1)}, bf16[512,512]{1,0:T(8,128)(2,1)S(1)}) custom-call(bf16[768,512]{1,0:T(8,128)(2,1)S(1)} %get-tuple-element.48.acc, bf16[768,512]{1,0:T(8,128)(2,1)S(1)} %get-tuple-element.49.acc_other, bf16[512,512]{1,0:T(8,128)(2,1)S(1)} %collective-permute-done.9.va, ...), custom_call_target="tpu_custom_call" | custom-call | tf_op jit(solution)/shard_map/late/pallas_call | solution.py:257
  41.6 2.7 %collective-permute-start.16 = (bf16[512,512]{1,0:T(8,128)(2,1)S(1)}, bf16[512,512]{1,0:T(8,128)(2,1)S(1)}, u32[]{:S(2)}, u32[]{:S(2)}) collective-permute-start(bf16[512,512]{1,0:T(8,128)(2,1)S(1)} %get-tuple-element.59), channel_id=1, source_target_pairs={{0,24},{1,7},{2,26},{3,1},{4,28},{5,3},{6,30},{7,5},{8,0},{9,15},{... | collective-permute-start | bytes 1572872 | tf_op jit(solution)/shard_map/ppermute | solution.py:37
  44.3 1.8 %sides_near.1 = (bf16[512,512]{1,0:T(8,128)(2,1)S(1)}, bf16[512,512]{1,0:T(8,128)(2,1)S(1)}) custom-call(bf16[512,768]{1,0:T(8,128)(2,1)S(1)} %get-tuple-element.52.s, bf16[512,768]{1,0:T(8,128)(2,1)S(1)} %get-tuple-element.53.so, bf16[768,4096]{1,0:T(8,128)(2,1)S(1)} %get-tuple-element.46.x, bf16[768,4096]{1,0:T(8,128)(2,1)S(1)} %get-tuple-element.47.xo), custom_call_target="tpu_custom_call" | custom-call | flops 2000000000 | bytes 1048576 | tf_op jit(solution)/shard_map/sides_near/pallas_call | solution.py:186
  46.1 3.3 %collective-permute-start.14 = (bf16[512,512]{1,0:T(8,128)(2,1)S(1)}, bf16[512,512]{1,0:T(8,128)(2,1)S(1)}, u32[]{:S(2)}, u32[]{:S(2)}) collective-permute-start(bf16[512,512]{1,0:T(8,128)(2,1)S(1)} %get-tuple-element.56), channel_id=1, source_target_pairs={{0,24},{1,7},{2,26},{3,1},{4,28},{5,3},{6,30},{7,5},{8,0},{9,15},{... | collective-permute-start | bytes 1572872 | tf_op jit(solution)/shard_map/ppermute | solution.py:37
  49.4 1.8 %sides_rest.1 = (bf16[512,512]{1,0:T(8,128)(2,1)S(1)}, bf16[512,512]{1,0:T(8,128)(2,1)S(1)}) custom-call(bf16[512,768]{1,0:T(8,128)(2,1)S(1)} %get-tuple-element.52.s, bf16[512,768]{1,0:T(8,128)(2,1)S(1)} %get-tuple-element.53.so, bf16[768,4096]{1,0:T(8,128)(2,1)S(1)} %get-tuple-element.46.x, bf16[768,4096]{1,0:T(8,128)(2,1)S(1)} %get-tuple-element.47.xo), custom_call_target="tpu_custom_call" | custom-call | flops 2000000000 | bytes 1048576 | tf_op jit(solution)/shard_map/sides_rest/pallas_call | solution.py:186
  51.3 0.1 add_convert_fusion
  51.4 3.7 %collective-permute-start.17 = (bf16[512,512]{1,0:T(8,128)(2,1)S(1)}, bf16[512,512]{1,0:T(8,128)(2,1)S(1)}, u32[]{:S(2)}, u32[]{:S(2)}) collective-permute-start(bf16[512,512]{1,0:T(8,128)(2,1)S(1)} %add_convert_fusion), channel_id=1, source_target_pairs={{0,24},{1,7},{2,26},{3,1},{4,28},{5,3},{6,30},{7,5},{8,0},{9,15},{... | collective-permute-start | bytes 1572872 | tf_op jit(solution)/shard_map/ppermute | solution.py:37
  55.1 0.1 add_convert_fusion.1
  55.3 1.8 %kept.1 = f32[512,1024]{1,0:T(8,128)S(1)} custom-call(bf16[512,768]{1,0:T(8,128)(2,1)S(1)} %get-tuple-element.52.s, bf16[512,768]{1,0:T(8,128)(2,1)S(1)} %get-tuple-element.53.so, bf16[768,4096]{1,0:T(8,128)(2,1)S(1)} %get-tuple-element.46.x, bf16[768,4096]{1,0:T(8,128)(2,1)S(1)} %get-tuple-element.47.xo), custom_call_target="tpu_custom_call" | custom-call | flops 2000000000 | bytes 1048576 | tf_op jit(solution)/shard_map/kept/pallas_call | solution.py:186
  57.2 3.1 %collective-permute-done.15.up_b = bf16[512,512]{1,0:T(8,128)(2,1)S(1)} collective-permute-done((bf16[512,512]{1,0:T(8,128)(2,1)S(1)}, bf16[512,512]{1,0:T(8,128)(2,1)S(1)}, u32[]{:S(2)}, u32[]{:S(2)}) %collective-permute-start.15) | collective-permute-done | bytes 524320 | tf_op jit(solution)/shard_map/ppermute | solution.py:37
  60.3 1.9 %collective-permute-done.17.down_b = bf16[512,512]{1,0:T(8,128)(2,1)S(1)} collective-permute-done((bf16[512,512]{1,0:T(8,128)(2,1)S(1)}, bf16[512,512]{1,0:T(8,128)(2,1)S(1)}, u32[]{:S(2)}, u32[]{:S(2)}) %collective-permute-start.17) | collective-permute-done | bytes 524320 | tf_op jit(solution)/shard_map/ppermute | solution.py:37
  62.2 3.7 %collective-permute-done.13.up_a = bf16[512,512]{1,0:T(8,128)(2,1)S(1)} collective-permute-done((bf16[512,512]{1,0:T(8,128)(2,1)S(1)}, bf16[512,512]{1,0:T(8,128)(2,1)S(1)}, u32[]{:S(2)}, u32[]{:S(2)}) %collective-permute-start.13) | collective-permute-done | bytes 524320 | tf_op jit(solution)/shard_map/ppermute | solution.py:37
  65.9 0.9 fold.1
  66.8 2.0 %collective-permute-start.18 = (bf16[512,256]{1,0:T(8,128)(2,1)}, bf16[512,256]{1,0:T(8,128)(2,1)S(1)}, u32[]{:S(2)}, u32[]{:S(2)}) collective-permute-start(bf16[512,256]{1,0:T(8,128)(2,1)} %get-tuple-element.61), channel_id=1, source_target_pairs={{0,4},{1,17},{2,6},{3,19},{4,0},{5,21},{6,2},{7,23},{8,12},{9,25},... | collective-permute-start | bytes 786440 | tf_op jit(solution)/shard_map/ppermute | solution.py:37
  68.8 3.1 %collective-permute-start.19 = (bf16[512,256]{1,0:T(8,128)(2,1)S(1)}, bf16[512,256]{1,0:T(8,128)(2,1)S(1)}, u32[]{:S(2)}, u32[]{:S(2)}) collective-permute-start(bf16[512,256]{1,0:T(8,128)(2,1)S(1)} %get-tuple-element.62), channel_id=1, source_target_pairs={{0,2},{1,9},{2,4},{3,11},{4,6},{5,13},{6,0},{7,15},{8,10},{9,17},{... | collective-permute-start | bytes 786440 | tf_op jit(solution)/shard_map/ppermute | solution.py:37
  72.7 0.1 stack.22
  72.8 2.2 %collective-permute-done.18.a = bf16[512,256]{1,0:T(8,128)(2,1)S(1)} collective-permute-done((bf16[512,256]{1,0:T(8,128)(2,1)}, bf16[512,256]{1,0:T(8,128)(2,1)S(1)}, u32[]{:S(2)}, u32[]{:S(2)}) %collective-permute-start.18) | collective-permute-done | bytes 262176 | tf_op jit(solution)/shard_map/ppermute | solution.py:37
  74.9 2.8 %collective-permute-done.19.b = bf16[512,256]{1,0:T(8,128)(2,1)S(1)} collective-permute-done((bf16[512,256]{1,0:T(8,128)(2,1)S(1)}, bf16[512,256]{1,0:T(8,128)(2,1)S(1)}, u32[]{:S(2)}, u32[]{:S(2)}) %collective-permute-start.19) | collective-permute-done | bytes 262176 | tf_op jit(solution)/shard_map/ppermute | solution.py:37
  77.8 0.5 collective-permute-done.20.c
  78.3 0.1 split.1
  78.4 0.1 collective-permute-start.21
  78.5 1.3 %collective-permute-done.21.refs_1_ = bf16[512,128]{1,0:T(8,128)(2,1)S(1)} collective-permute-done((bf16[512,128]{1,0:T(8,128)(2,1)S(1)}, bf16[512,128]{1,0:T(8,128)(2,1)S(1)}, u32[]{:S(2)}, u32[]{:S(2)}) %collective-permute-start.21) | collective-permute-done | bytes 131104 | tf_op jit(solution)/shard_map/ppermute | solution.py:37
  79.9 1.4 %inner_step.1 = (f32[128,1024]{1,0:T(8,128)}, f32[128,1024]{1,0:T(8,128)}, bf16[128,1024]{1,0:T(8,128)(2,1)S(1)}) custom-call(f32[8,512]{1,0:T(8,128)S(1)} %get-tuple-element.64.rates, f32[128,1024]{1,0:T(8,128)S(1)} %bitcast.14, f32[128,1024]{1,0:T(8,128)S(1)} %bitcast.15, f32[128,1024]{1,0:T(8,128)S(1)} %copy-done, ...), custom_call_target="tpu_custom_call" | custom-call | flops 1000000000 | bytes 1048576 | tf_op jit(solution)/shard_map/inner_step/pallas_call | solution.py:186
  81.3 22.8 %all_to_all.10 = bf16[8,16,1024]{2,1,0:T(8,128)(2,1)S(1)} all-to-all(bf16[8,16,1024]{2,1,0:T(8,128)(2,1)S(1)} %bitcast.13), channel_id=1, replica_groups=mesh['island'=8,'fsdp'=8,'dp'=4] {'island'}, dimensions={0} | all-to-all | bytes 524288 | tf_op jit(solution)/shard_map/all_to_all | solution.py:308
  104.2 13.5 %all_to_all.11 = bf16[8,16,1024]{2,1,0:T(8,128)(2,1)S(1)} all-to-all(bf16[8,16,1024]{2,1,0:T(8,128)(2,1)S(1)} %broadcast_in_dim.9), channel_id=1, replica_groups=mesh['island'=8,'fsdp'=8,'dp'=4] {'island'}, dimensions={0} | all-to-all | bytes 524288 | tf_op jit(solution)/shard_map/all_to_all | solution.py:311
  117.7 1.1 fusion.1
  (29 shorter events, 0.4 us)
Async XLA Ops:
  1.8 1.4 %collective-permute-start = (bf16[128,512]{1,0:T(8,128)(2,1)S(1)}, bf16[128,512]{1,0:T(8,128)(2,1)S(1)}, u32[]{:S(2)}, u32[]{:S(2)}) collective-permute-start(bf16[128,512]{1,0:T(8,128)(2,1)S(1)} %get-tuple-element.75), channel_id=1, source_target_pairs={{0,1},{1,0},{2,3},{3,2},{4,5},{5,4},{6,7},{7,6},{8,9},{9,8},{10,11... | collective-permute-start | bytes 393224 | tf_op jit(solution)/shard_map/ppermute | solution.py:37
  3.2 12.5 %collective-permute-start.4 = (bf16[768,4096]{1,0:T(8,128)(2,1)}, bf16[768,4096]{1,0:T(8,128)(2,1)}, u32[]{:S(2)}, u32[]{:S(2)}) collective-permute-start(bf16[768,4096]{1,0:T(8,128)(2,1)} %x.1), channel_id=1, source_target_pairs={{0,1},{1,0},{2,3},{3,2},{4,5},{5,4},{6,7},{7,6},{8,9},{9,8},{10,11... | collective-permute-start | bytes 18874376 | tf_op jit(solution)/shard_map/ppermute | solution.py:37
  3.4 6.7 %collective-permute-start.3 = (bf16[256,512]{1,0:T(8,128)(2,1)S(1)}, bf16[256,512]{1,0:T(8,128)(2,1)S(1)}, u32[]{:S(2)}, u32[]{:S(2)}) collective-permute-start(bf16[256,512]{1,0:T(8,128)(2,1)S(1)} %maximum_select_fusion.a), channel_id=1, source_target_pairs={{0,2},{1,9},{2,4},{3,11},{4,6},{5,13},{6,0},{7,15},{8,10},{9,17},{... | collective-permute-start | bytes 786440 | tf_op jit(solution)/shard_map/ppermute | solution.py:37
  5.0 8.0 %collective-permute-start.2 = (bf16[256,512]{1,0:T(8,128)(2,1)S(1)}, bf16[256,512]{1,0:T(8,128)(2,1)S(1)}, u32[]{:S(2)}, u32[]{:S(2)}) collective-permute-start(bf16[256,512]{1,0:T(8,128)(2,1)S(1)} %maximum_select_fusion.a), channel_id=1, source_target_pairs={{0,4},{1,17},{2,6},{3,19},{4,0},{5,21},{6,2},{7,23},{8,12},{9,25},... | collective-permute-start | bytes 786440 | tf_op jit(solution)/shard_map/ppermute | solution.py:37
  7.8 7.8 %collective-permute-start.1 = (bf16[256,512]{1,0:T(8,128)(2,1)S(1)}, bf16[256,512]{1,0:T(8,128)(2,1)S(1)}, u32[]{:S(2)}, u32[]{:S(2)}) collective-permute-start(bf16[256,512]{1,0:T(8,128)(2,1)S(1)} %maximum_select_fusion.a), channel_id=1, source_target_pairs={{0,6},{1,25},{2,0},{3,27},{4,2},{5,29},{6,4},{7,31},{8,14},{9,1},{... | collective-permute-start | bytes 786440 | tf_op jit(solution)/shard_map/ppermute | solution.py:37
  13.0 10.5 %collective-permute-start.8 = (bf16[512,512]{1,0:T(8,128)(2,1)S(1)}, bf16[512,512]{1,0:T(8,128)(2,1)S(1)}, u32[]{:S(2)}, u32[]{:S(2)}) collective-permute-start(bf16[512,512]{1,0:T(8,128)(2,1)S(1)} %stack.24), channel_id=1, source_target_pairs={{0,8},{1,3},{2,10},{3,5},{4,12},{5,7},{6,14},{7,1},{8,16},{9,11},{... | collective-permute-start | bytes 1572872 | tf_op jit(solution)/shard_map/ppermute | solution.py:37
  15.7 9.4 %collective-permute-start.5 = (bf16[512,512]{1,0:T(8,128)(2,1)S(1)}, bf16[512,512]{1,0:T(8,128)(2,1)S(1)}, u32[]{:S(2)}, u32[]{:S(2)}) collective-permute-start(bf16[512,512]{1,0:T(8,128)(2,1)S(1)} %stack.23), channel_id=1, source_target_pairs={{0,24},{1,7},{2,26},{3,1},{4,28},{5,3},{6,30},{7,5},{8,0},{9,15},{... | collective-permute-start | bytes 1572872 | tf_op jit(solution)/shard_map/ppermute | solution.py:37
  18.4 15.6 %collective-permute-start.6 = (bf16[512,512]{1,0:T(8,128)(2,1)S(1)}, bf16[512,512]{1,0:T(8,128)(2,1)S(1)}, u32[]{:S(2)}, u32[]{:S(2)}) collective-permute-start(bf16[512,512]{1,0:T(8,128)(2,1)S(1)} %stack.24), channel_id=1, source_target_pairs={{0,24},{1,7},{2,26},{3,1},{4,28},{5,3},{6,30},{7,5},{8,0},{9,15},{... | collective-permute-start | bytes 1572872 | tf_op jit(solution)/shard_map/ppermute | solution.py:37
  19.2 14.8 %collective-permute-start.7 = (bf16[512,512]{1,0:T(8,128)(2,1)S(1)}, bf16[512,512]{1,0:T(8,128)(2,1)S(1)}, u32[]{:S(2)}, u32[]{:S(2)}) collective-permute-start(bf16[512,512]{1,0:T(8,128)(2,1)S(1)} %stack.23), channel_id=1, source_target_pairs={{0,8},{1,3},{2,10},{3,5},{4,12},{5,7},{6,14},{7,1},{8,16},{9,11},{... | collective-permute-start | bytes 1572872 | tf_op jit(solution)/shard_map/ppermute | solution.py:37
  20.4 17.0 %collective-permute-start.11 = (bf16[768,512]{1,0:T(8,128)(2,1)S(1)}, bf16[768,512]{1,0:T(8,128)(2,1)S(1)}, u32[]{:S(2)}, u32[]{:S(2)}) collective-permute-start(bf16[768,512]{1,0:T(8,128)(2,1)S(1)} %get-tuple-element.50), channel_id=1, source_target_pairs={{0,1},{1,0},{2,3},{3,2},{4,5},{5,4},{6,7},{7,6},{8,9},{9,8},{10,11... | collective-permute-start | bytes 2359304 | tf_op jit(solution)/shard_map/ppermute | solution.py:37
  23.5 14.0 %collective-permute-start.10 = (bf16[512,512]{1,0:T(8,128)(2,1)S(1)}, bf16[512,512]{1,0:T(8,128)(2,1)S(1)}, u32[]{:S(2)}, u32[]{:S(2)}) collective-permute-start(bf16[512,512]{1,0:T(8,128)(2,1)S(1)} %collective-permute-done.8.high_3), channel_id=1, source_target_pairs={{0,8},{1,3},{2,10},{3,5},{4,12},{5,7},{6,14},{7,1},{8,16},{9,11},{... | collective-permute-start | bytes 1572872 | tf_op jit(solution)/shard_map/ppermute | solution.py:37
  25.1 12.3 %collective-permute-start.9 = (bf16[512,512]{1,0:T(8,128)(2,1)S(1)}, bf16[512,512]{1,0:T(8,128)(2,1)S(1)}, u32[]{:S(2)}, u32[]{:S(2)}) collective-permute-start(bf16[512,512]{1,0:T(8,128)(2,1)S(1)} %collective-permute-done.5.low_1), channel_id=1, source_target_pairs={{0,24},{1,7},{2,26},{3,1},{4,28},{5,3},{6,30},{7,5},{8,0},{9,15},{... | collective-permute-start | bytes 1572872 | tf_op jit(solution)/shard_map/ppermute | solution.py:37
  41.6 9.6 %collective-permute-start.16 = (bf16[512,512]{1,0:T(8,128)(2,1)S(1)}, bf16[512,512]{1,0:T(8,128)(2,1)S(1)}, u32[]{:S(2)}, u32[]{:S(2)}) collective-permute-start(bf16[512,512]{1,0:T(8,128)(2,1)S(1)} %get-tuple-element.59), channel_id=1, source_target_pairs={{0,24},{1,7},{2,26},{3,1},{4,28},{5,3},{6,30},{7,5},{8,0},{9,15},{... | collective-permute-start | bytes 1572872 | tf_op jit(solution)/shard_map/ppermute | solution.py:37
  44.3 10.8 %collective-permute-start.12 = (bf16[512,512]{1,0:T(8,128)(2,1)S(1)}, bf16[512,512]{1,0:T(8,128)(2,1)S(1)}, u32[]{:S(2)}, u32[]{:S(2)}) collective-permute-start(bf16[512,512]{1,0:T(8,128)(2,1)S(1)} %get-tuple-element.55), channel_id=1, source_target_pairs={{0,8},{1,3},{2,10},{3,5},{4,12},{5,7},{6,14},{7,1},{8,16},{9,11},{... | collective-permute-start | bytes 1572872 | tf_op jit(solution)/shard_map/ppermute | solution.py:37
  46.1 11.1 %collective-permute-start.14 = (bf16[512,512]{1,0:T(8,128)(2,1)S(1)}, bf16[512,512]{1,0:T(8,128)(2,1)S(1)}, u32[]{:S(2)}, u32[]{:S(2)}) collective-permute-start(bf16[512,512]{1,0:T(8,128)(2,1)S(1)} %get-tuple-element.56), channel_id=1, source_target_pairs={{0,24},{1,7},{2,26},{3,1},{4,28},{5,3},{6,30},{7,5},{8,0},{9,15},{... | collective-permute-start | bytes 1572872 | tf_op jit(solution)/shard_map/ppermute | solution.py:37
  49.4 10.9 %collective-permute-start.15 = (bf16[512,512]{1,0:T(8,128)(2,1)S(1)}, bf16[512,512]{1,0:T(8,128)(2,1)S(1)}, u32[]{:S(2)}, u32[]{:S(2)}) collective-permute-start(bf16[512,512]{1,0:T(8,128)(2,1)S(1)} %get-tuple-element.57), channel_id=1, source_target_pairs={{0,8},{1,3},{2,10},{3,5},{4,12},{5,7},{6,14},{7,1},{8,16},{9,11},{... | collective-permute-start | bytes 1572872 | tf_op jit(solution)/shard_map/ppermute | solution.py:37
  51.4 10.8 %collective-permute-start.17 = (bf16[512,512]{1,0:T(8,128)(2,1)S(1)}, bf16[512,512]{1,0:T(8,128)(2,1)S(1)}, u32[]{:S(2)}, u32[]{:S(2)}) collective-permute-start(bf16[512,512]{1,0:T(8,128)(2,1)S(1)} %add_convert_fusion), channel_id=1, source_target_pairs={{0,24},{1,7},{2,26},{3,1},{4,28},{5,3},{6,30},{7,5},{8,0},{9,15},{... | collective-permute-start | bytes 1572872 | tf_op jit(solution)/shard_map/ppermute | solution.py:37
  55.2 10.7 %collective-permute-start.13 = (bf16[512,512]{1,0:T(8,128)(2,1)S(1)}, bf16[512,512]{1,0:T(8,128)(2,1)S(1)}, u32[]{:S(2)}, u32[]{:S(2)}) collective-permute-start(bf16[512,512]{1,0:T(8,128)(2,1)S(1)} %add_convert_fusion.1), channel_id=1, source_target_pairs={{0,8},{1,3},{2,10},{3,5},{4,12},{5,7},{6,14},{7,1},{8,16},{9,11},{... | collective-permute-start | bytes 1572872 | tf_op jit(solution)/shard_map/ppermute | solution.py:37
  57.2 22.7 %copy-start = (f32[128,1024]{1,0:T(8,128)S(1)}, f32[128,1024]{1,0:T(8,128)}, u32[]{:S(2)}) copy-start(f32[128,1024]{1,0:T(8,128)} %weight.1) | copy-start | bytes 1572868
  57.2 22.7 %copy-start.1 = (f32[1,128,1024]{2,1,0:T(8,128)S(1)}, f32[1,128,1024]{2,1,0:T(8,128)}, u32[]{:S(2)}) copy-start(f32[1,128,1024]{2,1,0:T(8,128)} %param.11) | copy-start | bytes 1572868
  57.2 22.7 %copy-start.2 = (f32[1,128,1024]{2,1,0:T(8,128)S(1)}, f32[1,128,1024]{2,1,0:T(8,128)}, u32[]{:S(2)}) copy-start(f32[1,128,1024]{2,1,0:T(8,128)} %param.12) | copy-start | bytes 1572868
  66.8 8.1 %collective-permute-start.18 = (bf16[512,256]{1,0:T(8,128)(2,1)}, bf16[512,256]{1,0:T(8,128)(2,1)S(1)}, u32[]{:S(2)}, u32[]{:S(2)}) collective-permute-start(bf16[512,256]{1,0:T(8,128)(2,1)} %get-tuple-element.61), channel_id=1, source_target_pairs={{0,4},{1,17},{2,6},{3,19},{4,0},{5,21},{6,2},{7,23},{8,12},{9,25},... | collective-permute-start | bytes 786440 | tf_op jit(solution)/shard_map/ppermute | solution.py:37
  68.8 9.0 %collective-permute-start.19 = (bf16[512,256]{1,0:T(8,128)(2,1)S(1)}, bf16[512,256]{1,0:T(8,128)(2,1)S(1)}, u32[]{:S(2)}, u32[]{:S(2)}) collective-permute-start(bf16[512,256]{1,0:T(8,128)(2,1)S(1)} %get-tuple-element.62), channel_id=1, source_target_pairs={{0,2},{1,9},{2,4},{3,11},{4,6},{5,13},{6,0},{7,15},{8,10},{9,17},{... | collective-permute-start | bytes 786440 | tf_op jit(solution)/shard_map/ppermute | solution.py:37
  71.9 6.4 %collective-permute-start.20 = (bf16[512,256]{1,0:T(8,128)(2,1)S(1)}, bf16[512,256]{1,0:T(8,128)(2,1)S(1)}, u32[]{:S(2)}, u32[]{:S(2)}) collective-permute-start(bf16[512,256]{1,0:T(8,128)(2,1)S(1)} %get-tuple-element.63), channel_id=1, source_target_pairs={{0,6},{1,25},{2,0},{3,27},{4,2},{5,29},{6,4},{7,31},{8,14},{9,1},{... | collective-permute-start | bytes 786440 | tf_op jit(solution)/shard_map/ppermute | solution.py:37
  72.8 44.9 %copy-start.3 = (f32[128,1024]{1,0:T(8,128)S(1)}, f32[128,1024]{1,0:T(8,128)}, u32[]{:S(2)}) copy-start(f32[128,1024]{1,0:T(8,128)} %param.10) | copy-start | bytes 1572868
  78.4 1.4 %collective-permute-start.21 = (bf16[512,128]{1,0:T(8,128)(2,1)S(1)}, bf16[512,128]{1,0:T(8,128)(2,1)S(1)}, u32[]{:S(2)}, u32[]{:S(2)}) collective-permute-start(bf16[512,128]{1,0:T(8,128)(2,1)S(1)} %get-tuple-element.66), channel_id=1, source_target_pairs={{0,1},{1,0},{2,3},{3,2},{4,5},{5,4},{6,7},{7,6},{8,9},{9,8},{10,11... | collective-permute-start | bytes 393224 | tf_op jit(solution)/shard_map/ppermute | solution.py:37

commit v5 on v4

--- a/solution.py
+++ b/solution.py
@@ -144,17 +144,16 @@
         out[:, m * SIDE : (m + 1) * SIDE] = term(place, 0, m, s, so, x, xo)
 
 
-def fold_kernel(kept, up_a, down_a, up_b, down_b, *outs):
-    for m in range(4):
-        part = slice(m % 2 * SIDE, (m % 2 + 1) * SIDE)
-        total = kept[:, m * SIDE : (m + 1) * SIDE]
-        for ref in (up_a, down_a) if m < 2 else (up_b, down_b):
+def fold_kernel(first, kept, up, down, *outs):
+    for k, out in enumerate(outs):
+        part = slice(k * SIDE, (k + 1) * SIDE)
+        total = kept[:, (first + k) * SIDE : (first + k + 1) * SIDE]
+        for ref in (up, down):
             total += ref[:, part].astype(jnp.float32)
-        outs[m][...] = total.astype(outs[m].dtype)
-
-
-def split_kernel(own, a, b, c, rates, mine, theirs, rates_out):
-    rates_out[...] = rates[...]
+        out[...] = total.astype(out.dtype)
+
+
+def split_kernel(own, a, b, c, mine, theirs):
     total = own[...] + a[...].astype(jnp.float32) + b[...].astype(jnp.float32) + c[...].astype(jnp.float32)
     core = here()[2]
     low, high = total[:, : SIDE // 2], total[:, SIDE // 2 :]
@@ -280,19 +279,17 @@
     up_b, down_a = send(up_b, far(1)), send(down_a, far(-1))
     up_a = send((up_a.astype(f32) + from_low.astype(f32)).astype(bf16), far(1))
     down_b = send((down_b.astype(f32) + from_high.astype(f32)).astype(bf16), far(-1))
-    parts = local(
-        fold_kernel,
-        [((half, SIDE), f32)] + [((half, SIDE), bf16)] * 3,
-        LIMIT_B,
-        "fold",
-        kept, up_a, down_a, up_b, down_b,
-    )
-    mine, theirs, rates = local(
+    part = (half, SIDE)
+    fold = functools.partial(fold_kernel, 2)
+    parts = local(fold, [(part, bf16)] * 2, LIMIT_B, "fold_high", kept, up_b, down_b)
+    fold = functools.partial(fold_kernel, 0)
+    parts = [*local(fold, [(part, f32), (part, bf16)], LIMIT_B, "fold_low", kept, up_a, down_a), *parts]
+    mine, theirs = local(
         split_kernel,
-        [((half, SIDE // 2), f32), ((half, SIDE // 2), bf16), (rates.shape, f32)],
+        [((half, SIDE // 2), f32), ((half, SIDE // 2), bf16)],
         LIMIT_B,
         "split",
-        parts[0], *[send(parts[k], near(k)) for k in (2, 1, 3)], rates,
+        parts[0], *[send(parts[k], near(k)) for k in (2, 1, 3)],
     )
     grads = [mine, send(theirs, partner)]
 

time: 119 us -> 117 us (0.983); the launches traced: 119 us -> 115 us
  starting transfers between devices: 30.6 us -> 35.6 us
  waiting for transfers between devices: 24.3 us -> 20.1 us
  blocking collectives: 36.3 us -> 32.4 us
    ppermute x22, starting transfers between devices: 30.6 us -> 35.6 us  [send(): return lax.ppermute(value, AXES, pairs)]
    ppermute x22, waiting for transfers between devices: 24.3 us -> 20.1 us  [send(): return lax.ppermute(value, AXES, pairs)]
    all_to_all x1, blocking collectives: 22.8 us -> 18.9 us  [per_device(): lax.all_to_all(pseudo.reshape(NZ, rows // NZ, columns), 'island', 0, 0, t...]
    pallas_call x9 -> x10, Pallas kernels: 11.5 us -> 10.8 us  [local(): pl.pallas_call(kernel, out_shape=[jax.ShapeDtypeStruct(*s) for s in shape...]
  transfers between devices with their start and end apart: 22 -> 22, of which waited for: 13 -> 11; matrix products, arithmetic and copies ran while one was open for 2% -> 2% of each run, Pallas kernels for 12% -> 13%
where the time goes in v5:
time: 117 us; the launch traced here: 115 us
  starting transfers between devices  35.6 us (30%)
  blocking collectives  32.4 us (28%)
  Pallas kernels  20.2 us (17%)
  waiting for transfers between devices  20.1 us (17%)
  other arithmetic  2.57 us (2%)
  local copies, waits for them, and re-layouts  2.57 us (2%)
  between operations  1.7 us (1%)
    ppermute x22, starting transfers between devices, send(): return lax.ppermute(value, AXES, pairs)  35.6 us
    ppermute x22, waiting for transfers between devices, send(): return lax.ppermute(value, AXES, pairs)  20.1 us
    all_to_all x1, blocking collectives, per_device(): lax.all_to_all(pseudo.reshape(NZ, rows // NZ, columns), 'island', 0, 0, t...  18.9 us
    all_to_all x1, blocking collectives, per_device(): lax.all_to_all(spread, 'island', 0, 0, tiled=True).reshape(rows, columns)  13.5 us
    pallas_call x10, Pallas kernels, local(): pl.pallas_call(kernel, out_shape=[jax.ShapeDtypeStruct(*s) for s in shape...  10.8 us
    pallas_call x1, Pallas kernels, per_device(): pl.pallas_call(first_kernel, out_shape=[jax.ShapeDtypeStruct((count, half...  5.15 us
    pallas_call x1, Pallas kernels, per_device(): pl.pallas_call(functools.partial(late_kernel, scales), out_shape=[jax.Sha...  4.16 us
    dynamic_slice x1, local copies, waits for them, and re-layouts, per_device(): goals_other = lax.dynamic_slice_in_dim(targets, (1 - core) * half, half, 1)  2.35 us
  transfers between devices with their start and end apart: 22, of which 11 were waited for; matrix products, arithmetic and copies ran while one was open for 2% of the time, Pallas kernels for 13%

profile of v5, /device:TPU:2, one launch (start us, length us, event | category | flops | bytes accessed | tf_op | source)
XLA Modules:
  0.0 115.1 jit_solution(9412562287275796123)
XLA Ops:
  0.6 1.1 convert_element_type.41
  1.8 0.1 collective-permute-start
  1.9 1.3 %collective-permute-done = bf16[128,512]{1,0:T(8,128)(2,1)S(1)} collective-permute-done((bf16[128,512]{1,0:T(8,128)(2,1)S(1)}, bf16[128,512]{1,0:T(8,128)(2,1)S(1)}, u32[]{:S(2)}, u32[]{:S(2)}) %collective-permute-start) | collective-permute-done | bytes 131104 | tf_op jit(solution)/shard_map/ppermute | solution.py:37
  3.2 0.1 collective-permute-start.4
  3.4 1.6 %collective-permute-start.3 = (bf16[256,512]{1,0:T(8,128)(2,1)S(1)}, bf16[256,512]{1,0:T(8,128)(2,1)S(1)}, u32[]{:S(2)}, u32[]{:S(2)}) collective-permute-start(bf16[256,512]{1,0:T(8,128)(2,1)S(1)} %maximum_select_fusion.a), channel_id=1, source_target_pairs={{0,2},{1,9},{2,4},{3,11},{4,6},{5,13},{6,0},{7,15},{8,10},{9,17},{... | collective-permute-start | bytes 786440 | tf_op jit(solution)/shard_map/ppermute | solution.py:37
  5.0 2.8 %collective-permute-start.2 = (bf16[256,512]{1,0:T(8,128)(2,1)S(1)}, bf16[256,512]{1,0:T(8,128)(2,1)S(1)}, u32[]{:S(2)}, u32[]{:S(2)}) collective-permute-start(bf16[256,512]{1,0:T(8,128)(2,1)S(1)} %maximum_select_fusion.a), channel_id=1, source_target_pairs={{0,4},{1,17},{2,6},{3,19},{4,0},{5,21},{6,2},{7,23},{8,12},{9,25},... | collective-permute-start | bytes 786440 | tf_op jit(solution)/shard_map/ppermute | solution.py:37
  7.8 0.4 collective-permute-start.1
  8.2 1.9 %collective-permute-done.3.d.b = bf16[256,512]{1,0:T(8,128)(2,1)S(1)} collective-permute-done((bf16[256,512]{1,0:T(8,128)(2,1)S(1)}, bf16[256,512]{1,0:T(8,128)(2,1)S(1)}, u32[]{:S(2)}, u32[]{:S(2)}) %collective-permute-start.3) | collective-permute-done | bytes 262176 | tf_op jit(solution)/shard_map/ppermute | solution.py:37
  10.1 2.3 %constant_dynamic-slice_fusion = (bf16[768,512]{1,0:T(8,128)(2,1)S(1)}, bf16[768,512]{1,0:T(8,128)(2,1)}) fusion(bf16[768,1024]{1,0:T(8,128)(2,1)} %param.8, s32[]{:T(128)S(6)} %select_n.18, s32[]{:T(128)S(6)} %select_n.17), kind=kLoop, calls=%fused_computation.9 | loop fusion | bytes 3145736 | tf_op jit(solution)/shard_map/dynamic_slice | solution.py:226
  12.5 0.5 collective-permute-done.2.c.a
  13.0 1.7 %collective-permute-start.8 = (bf16[512,512]{1,0:T(8,128)(2,1)S(1)}, bf16[512,512]{1,0:T(8,128)(2,1)S(1)}, u32[]{:S(2)}, u32[]{:S(2)}) collective-permute-start(bf16[512,512]{1,0:T(8,128)(2,1)S(1)} %stack.24), channel_id=1, source_target_pairs={{0,8},{1,3},{2,10},{3,5},{4,12},{5,7},{6,14},{7,1},{8,16},{9,11},{... | collective-permute-start | bytes 1572872 | tf_op jit(solution)/shard_map/ppermute | solution.py:37
  14.7 1.0 collective-permute-done.1.b
  15.7 2.7 %collective-permute-start.5 = (bf16[512,512]{1,0:T(8,128)(2,1)S(1)}, bf16[512,512]{1,0:T(8,128)(2,1)S(1)}, u32[]{:S(2)}, u32[]{:S(2)}) collective-permute-start(bf16[512,512]{1,0:T(8,128)(2,1)S(1)} %stack.23), channel_id=1, source_target_pairs={{0,24},{1,7},{2,26},{3,1},{4,28},{5,3},{6,30},{7,5},{8,0},{9,15},{... | collective-permute-start | bytes 1572872 | tf_op jit(solution)/shard_map/ppermute | solution.py:37
  18.4 0.7 collective-permute-start.6
  19.2 1.3 %collective-permute-start.7 = (bf16[512,512]{1,0:T(8,128)(2,1)S(1)}, bf16[512,512]{1,0:T(8,128)(2,1)S(1)}, u32[]{:S(2)}, u32[]{:S(2)}) collective-permute-start(bf16[512,512]{1,0:T(8,128)(2,1)S(1)} %stack.23), channel_id=1, source_target_pairs={{0,8},{1,3},{2,10},{3,5},{4,12},{5,7},{6,14},{7,1},{8,16},{9,11},{... | collective-permute-start | bytes 1572872 | tf_op jit(solution)/shard_map/ppermute | solution.py:37
  20.4 0.2 collective-permute-start.11
  20.6 2.8 %collective-permute-done.8.high_3 = bf16[512,512]{1,0:T(8,128)(2,1)S(1)} collective-permute-done((bf16[512,512]{1,0:T(8,128)(2,1)S(1)}, bf16[512,512]{1,0:T(8,128)(2,1)S(1)}, u32[]{:S(2)}, u32[]{:S(2)}) %collective-permute-start.8) | collective-permute-done | bytes 524320 | tf_op jit(solution)/shard_map/ppermute | solution.py:37
  23.5 0.4 collective-permute-start.10
  23.8 1.3 %collective-permute-done.5.low_1 = bf16[512,512]{1,0:T(8,128)(2,1)S(1)} collective-permute-done((bf16[512,512]{1,0:T(8,128)(2,1)S(1)}, bf16[512,512]{1,0:T(8,128)(2,1)S(1)}, u32[]{:S(2)}, u32[]{:S(2)}) %collective-permute-start.5) | collective-permute-done | bytes 524320 | tf_op jit(solution)/shard_map/ppermute | solution.py:37
  25.1 3.7 %collective-permute-start.9 = (bf16[512,512]{1,0:T(8,128)(2,1)S(1)}, bf16[512,512]{1,0:T(8,128)(2,1)S(1)}, u32[]{:S(2)}, u32[]{:S(2)}) collective-permute-start(bf16[512,512]{1,0:T(8,128)(2,1)S(1)} %collective-permute-done.5.low_1), channel_id=1, source_target_pairs={{0,24},{1,7},{2,26},{3,1},{4,28},{5,3},{6,30},{7,5},{8,0},{9,15},{... | collective-permute-start | bytes 1572872 | tf_op jit(solution)/shard_map/ppermute | solution.py:37
  28.8 5.2 %first.1 = (bf16[768,512]{1,0:T(8,128)(2,1)S(1)}, bf16[768,512]{1,0:T(8,128)(2,1)S(1)}, bf16[768,4096]{1,0:T(8,128)(2,1)S(1)}, bf16[768,4096]{1,0:T(8,128)(2,1)S(1)}) custom-call(bf16[256,512]{1,0:T(8,128)(2,1)S(1)} %maximum_select_fusion.a, bf16[256,512]{1,0:T(8,128)(2,1)S(1)} %collective-permute-done.1.b, bf16[256,512]{1,0:T(8,128)(2,1)S(1)} %collective-permute-done.2.c.a, ...), custom_call_target="tpu_custom_call" | custom-call | tf_op jit(solution)/shard_map/first/pallas_call | solution.py:238
  34.0 3.4 %more.1 = (bf16[768,512]{1,0:T(8,128)(2,1)S(1)}, bf16[768,512]{1,0:T(8,128)(2,1)S(1)}) custom-call(bf16[768,512]{1,0:T(8,128)(2,1)S(1)} %get-tuple-element.42.acc, bf16[768,512]{1,0:T(8,128)(2,1)S(1)} %get-tuple-element.43.acc_other, bf16[512,512]{1,0:T(8,128)(2,1)S(1)} %collective-permute-done.5.low_1, bf16[512,512]{1,0:T(8,128)(2,1)S(1)} %collective-permute-done.6.high_1, ...), custom_call_target="tpu_custom_call" | custom-call | flops 4000000000 | bytes 1048576 | tf_op jit(solution)/shard_map/more/pallas_call | solution.py:185
  37.5 4.2 %late.1 = (bf16[512,768]{1,0:T(8,128)(2,1)S(1)}, bf16[512,768]{1,0:T(8,128)(2,1)S(1)}, bf16[512,512]{1,0:T(8,128)(2,1)S(1)}, bf16[512,512]{1,0:T(8,128)(2,1)S(1)}) custom-call(bf16[768,512]{1,0:T(8,128)(2,1)S(1)} %get-tuple-element.47.acc, bf16[768,512]{1,0:T(8,128)(2,1)S(1)} %get-tuple-element.48.acc_other, bf16[512,512]{1,0:T(8,128)(2,1)S(1)} %collective-permute-done.9.va, ...), custom_call_target="tpu_custom_call" | custom-call | tf_op jit(solution)/shard_map/late/pallas_call | solution.py:256
  41.6 2.7 %collective-permute-start.16 = (bf16[512,512]{1,0:T(8,128)(2,1)S(1)}, bf16[512,512]{1,0:T(8,128)(2,1)S(1)}, u32[]{:S(2)}, u32[]{:S(2)}) collective-permute-start(bf16[512,512]{1,0:T(8,128)(2,1)S(1)} %get-tuple-element.59), channel_id=1, source_target_pairs={{0,24},{1,7},{2,26},{3,1},{4,28},{5,3},{6,30},{7,5},{8,0},{9,15},{... | collective-permute-start | bytes 1572872 | tf_op jit(solution)/shard_map/ppermute | solution.py:37
  44.3 1.8 %sides_near.1 = (bf16[512,512]{1,0:T(8,128)(2,1)S(1)}, bf16[512,512]{1,0:T(8,128)(2,1)S(1)}) custom-call(bf16[512,768]{1,0:T(8,128)(2,1)S(1)} %get-tuple-element.51.s, bf16[512,768]{1,0:T(8,128)(2,1)S(1)} %get-tuple-element.52.so, bf16[768,4096]{1,0:T(8,128)(2,1)S(1)} %get-tuple-element.45.x, bf16[768,4096]{1,0:T(8,128)(2,1)S(1)} %get-tuple-element.46.xo), custom_call_target="tpu_custom_call" | custom-call | flops 2000000000 | bytes 1048576 | tf_op jit(solution)/shard_map/sides_near/pallas_call | solution.py:185
  46.2 3.3 %collective-permute-start.14 = (bf16[512,512]{1,0:T(8,128)(2,1)S(1)}, bf16[512,512]{1,0:T(8,128)(2,1)S(1)}, u32[]{:S(2)}, u32[]{:S(2)}) collective-permute-start(bf16[512,512]{1,0:T(8,128)(2,1)S(1)} %get-tuple-element.55), channel_id=1, source_target_pairs={{0,24},{1,7},{2,26},{3,1},{4,28},{5,3},{6,30},{7,5},{8,0},{9,15},{... | collective-permute-start | bytes 1572872 | tf_op jit(solution)/shard_map/ppermute | solution.py:37
  49.5 1.8 %sides_rest.1 = (bf16[512,512]{1,0:T(8,128)(2,1)S(1)}, bf16[512,512]{1,0:T(8,128)(2,1)S(1)}) custom-call(bf16[512,768]{1,0:T(8,128)(2,1)S(1)} %get-tuple-element.51.s, bf16[512,768]{1,0:T(8,128)(2,1)S(1)} %get-tuple-element.52.so, bf16[768,4096]{1,0:T(8,128)(2,1)S(1)} %get-tuple-element.45.x, bf16[768,4096]{1,0:T(8,128)(2,1)S(1)} %get-tuple-element.46.xo), custom_call_target="tpu_custom_call" | custom-call | flops 2000000000 | bytes 1048576 | tf_op jit(solution)/shard_map/sides_rest/pallas_call | solution.py:185
  51.3 0.1 add_convert_fusion
  51.5 3.6 %collective-permute-start.17 = (bf16[512,512]{1,0:T(8,128)(2,1)S(1)}, bf16[512,512]{1,0:T(8,128)(2,1)S(1)}, u32[]{:S(2)}, u32[]{:S(2)}) collective-permute-start(bf16[512,512]{1,0:T(8,128)(2,1)S(1)} %add_convert_fusion), channel_id=1, source_target_pairs={{0,24},{1,7},{2,26},{3,1},{4,28},{5,3},{6,30},{7,5},{8,0},{9,15},{... | collective-permute-start | bytes 1572872 | tf_op jit(solution)/shard_map/ppermute | solution.py:37
  55.1 0.1 add_convert_fusion.1
  55.3 1.8 %kept.1 = f32[512,1024]{1,0:T(8,128)S(1)} custom-call(bf16[512,768]{1,0:T(8,128)(2,1)S(1)} %get-tuple-element.51.s, bf16[512,768]{1,0:T(8,128)(2,1)S(1)} %get-tuple-element.52.so, bf16[768,4096]{1,0:T(8,128)(2,1)S(1)} %get-tuple-element.45.x, bf16[768,4096]{1,0:T(8,128)(2,1)S(1)} %get-tuple-element.46.xo), custom_call_target="tpu_custom_call" | custom-call | flops 2000000000 | bytes 1048576 | tf_op jit(solution)/shard_map/kept/pallas_call | solution.py:185
  57.2 3.1 %collective-permute-done.15.up = bf16[512,512]{1,0:T(8,128)(2,1)S(1)} collective-permute-done((bf16[512,512]{1,0:T(8,128)(2,1)S(1)}, bf16[512,512]{1,0:T(8,128)(2,1)S(1)}, u32[]{:S(2)}, u32[]{:S(2)}) %collective-permute-start.15) | collective-permute-done | bytes 524320 | tf_op jit(solution)/shard_map/ppermute | solution.py:37
  60.3 1.9 %collective-permute-done.17.down = bf16[512,512]{1,0:T(8,128)(2,1)S(1)} collective-permute-done((bf16[512,512]{1,0:T(8,128)(2,1)S(1)}, bf16[512,512]{1,0:T(8,128)(2,1)S(1)}, u32[]{:S(2)}, u32[]{:S(2)}) %collective-permute-start.17) | collective-permute-done | bytes 524320 | tf_op jit(solution)/shard_map/ppermute | solution.py:37
  62.2 0.2 fold_high.1
  62.4 2.1 %collective-permute-start.18 = (bf16[512,256]{1,0:T(8,128)(2,1)S(1)}, bf16[512,256]{1,0:T(8,128)(2,1)S(1)}, u32[]{:S(2)}, u32[]{:S(2)}) collective-permute-start(bf16[512,256]{1,0:T(8,128)(2,1)S(1)} %get-tuple-element.60), channel_id=1, source_target_pairs={{0,4},{1,17},{2,6},{3,19},{4,0},{5,21},{6,2},{7,23},{8,12},{9,25},... | collective-permute-start | bytes 786440 | tf_op jit(solution)/shard_map/ppermute | solution.py:37
  64.4 6.5 %collective-permute-start.20 = (bf16[512,256]{1,0:T(8,128)(2,1)S(1)}, bf16[512,256]{1,0:T(8,128)(2,1)S(1)}, u32[]{:S(2)}, u32[]{:S(2)}) collective-permute-start(bf16[512,256]{1,0:T(8,128)(2,1)S(1)} %get-tuple-element.62), channel_id=1, source_target_pairs={{0,6},{1,25},{2,0},{3,27},{4,2},{5,29},{6,4},{7,31},{8,14},{9,1},{... | collective-permute-start | bytes 786440 | tf_op jit(solution)/shard_map/ppermute | solution.py:37
  70.9 0.1 fold_low.1
  71.1 1.5 %collective-permute-start.19 = (bf16[512,256]{1,0:T(8,128)(2,1)S(1)}, bf16[512,256]{1,0:T(8,128)(2,1)S(1)}, u32[]{:S(2)}, u32[]{:S(2)}) collective-permute-start(bf16[512,256]{1,0:T(8,128)(2,1)S(1)} %get-tuple-element.61), channel_id=1, source_target_pairs={{0,2},{1,9},{2,4},{3,11},{4,6},{5,13},{6,0},{7,15},{8,10},{9,17},{... | collective-permute-start | bytes 786440 | tf_op jit(solution)/shard_map/ppermute | solution.py:37
  72.5 4.1 %collective-permute-done.20.c = bf16[512,256]{1,0:T(8,128)(2,1)S(1)} collective-permute-done((bf16[512,256]{1,0:T(8,128)(2,1)S(1)}, bf16[512,256]{1,0:T(8,128)(2,1)S(1)}, u32[]{:S(2)}, u32[]{:S(2)}) %collective-permute-start.20) | collective-permute-done | bytes 262176 | tf_op jit(solution)/shard_map/ppermute | solution.py:37
  76.6 1.7 %collective-permute-done.19.b = bf16[512,256]{1,0:T(8,128)(2,1)S(1)} collective-permute-done((bf16[512,256]{1,0:T(8,128)(2,1)S(1)}, bf16[512,256]{1,0:T(8,128)(2,1)S(1)}, u32[]{:S(2)}, u32[]{:S(2)}) %collective-permute-start.19) | collective-permute-done | bytes 262176 | tf_op jit(solution)/shard_map/ppermute | solution.py:37
  78.4 0.1 split.1
  78.5 0.1 collective-permute-start.21
  79.4 0.1 stack.22
  79.5 0.4 collective-permute-done.21.refs_1_
  80.0 1.4 %inner_step.1 = (f32[128,1024]{1,0:T(8,128)}, f32[128,1024]{1,0:T(8,128)}, bf16[128,1024]{1,0:T(8,128)(2,1)S(1)}) custom-call(f32[8,512]{1,0:T(8,128)S(1)} %broadcast_in_dim.8.rates, f32[128,1024]{1,0:T(8,128)S(1)} %bitcast.14, f32[128,1024]{1,0:T(8,128)S(1)} %bitcast.15, f32[128,1024]{1,0:T(8,128)S(1)} %copy-done, ...), custom_call_target="tpu_custom_call" | custom-call | flops 1000000000 | bytes 1048576 | tf_op jit(solution)/shard_map/inner_step/pallas_call | solution.py:185
  81.4 18.9 %all_to_all.10 = bf16[8,16,1024]{2,1,0:T(8,128)(2,1)S(1)} all-to-all(bf16[8,16,1024]{2,1,0:T(8,128)(2,1)S(1)} %bitcast.13), channel_id=1, replica_groups=mesh['island'=8,'fsdp'=8,'dp'=4] {'island'}, dimensions={0} | all-to-all | bytes 524288 | tf_op jit(solution)/shard_map/all_to_all | solution.py:305
  100.4 13.5 %all_to_all.11 = bf16[8,16,1024]{2,1,0:T(8,128)(2,1)S(1)} all-to-all(bf16[8,16,1024]{2,1,0:T(8,128)(2,1)S(1)} %broadcast_in_dim.9), channel_id=1, replica_groups=mesh['island'=8,'fsdp'=8,'dp'=4] {'island'}, dimensions={0} | all-to-all | bytes 524288 | tf_op jit(solution)/shard_map/all_to_all | solution.py:308
  114.0 1.1 fusion.1
  (30 shorter events, 0.5 us)
Async XLA Ops:
  1.8 1.4 %collective-permute-start = (bf16[128,512]{1,0:T(8,128)(2,1)S(1)}, bf16[128,512]{1,0:T(8,128)(2,1)S(1)}, u32[]{:S(2)}, u32[]{:S(2)}) collective-permute-start(bf16[128,512]{1,0:T(8,128)(2,1)S(1)} %get-tuple-element.73), channel_id=1, source_target_pairs={{0,1},{1,0},{2,3},{3,2},{4,5},{5,4},{6,7},{7,6},{8,9},{9,8},{10,11... | collective-permute-start | bytes 393224 | tf_op jit(solution)/shard_map/ppermute | solution.py:37
  3.2 12.5 %collective-permute-start.4 = (bf16[768,4096]{1,0:T(8,128)(2,1)}, bf16[768,4096]{1,0:T(8,128)(2,1)}, u32[]{:S(2)}, u32[]{:S(2)}) collective-permute-start(bf16[768,4096]{1,0:T(8,128)(2,1)} %x.1), channel_id=1, source_target_pairs={{0,1},{1,0},{2,3},{3,2},{4,5},{5,4},{6,7},{7,6},{8,9},{9,8},{10,11... | collective-permute-start | bytes 18874376 | tf_op jit(solution)/shard_map/ppermute | solution.py:37
  3.4 6.7 %collective-permute-start.3 = (bf16[256,512]{1,0:T(8,128)(2,1)S(1)}, bf16[256,512]{1,0:T(8,128)(2,1)S(1)}, u32[]{:S(2)}, u32[]{:S(2)}) collective-permute-start(bf16[256,512]{1,0:T(8,128)(2,1)S(1)} %maximum_select_fusion.a), channel_id=1, source_target_pairs={{0,2},{1,9},{2,4},{3,11},{4,6},{5,13},{6,0},{7,15},{8,10},{9,17},{... | collective-permute-start | bytes 786440 | tf_op jit(solution)/shard_map/ppermute | solution.py:37
  5.0 8.0 %collective-permute-start.2 = (bf16[256,512]{1,0:T(8,128)(2,1)S(1)}, bf16[256,512]{1,0:T(8,128)(2,1)S(1)}, u32[]{:S(2)}, u32[]{:S(2)}) collective-permute-start(bf16[256,512]{1,0:T(8,128)(2,1)S(1)} %maximum_select_fusion.a), channel_id=1, source_target_pairs={{0,4},{1,17},{2,6},{3,19},{4,0},{5,21},{6,2},{7,23},{8,12},{9,25},... | collective-permute-start | bytes 786440 | tf_op jit(solution)/shard_map/ppermute | solution.py:37
  7.8 7.8 %collective-permute-start.1 = (bf16[256,512]{1,0:T(8,128)(2,1)S(1)}, bf16[256,512]{1,0:T(8,128)(2,1)S(1)}, u32[]{:S(2)}, u32[]{:S(2)}) collective-permute-start(bf16[256,512]{1,0:T(8,128)(2,1)S(1)} %maximum_select_fusion.a), channel_id=1, source_target_pairs={{0,6},{1,25},{2,0},{3,27},{4,2},{5,29},{6,4},{7,31},{8,14},{9,1},{... | collective-permute-start | bytes 786440 | tf_op jit(solution)/shard_map/ppermute | solution.py:37
  13.0 10.5 %collective-permute-start.8 = (bf16[512,512]{1,0:T(8,128)(2,1)S(1)}, bf16[512,512]{1,0:T(8,128)(2,1)S(1)}, u32[]{:S(2)}, u32[]{:S(2)}) collective-permute-start(bf16[512,512]{1,0:T(8,128)(2,1)S(1)} %stack.24), channel_id=1, source_target_pairs={{0,8},{1,3},{2,10},{3,5},{4,12},{5,7},{6,14},{7,1},{8,16},{9,11},{... | collective-permute-start | bytes 1572872 | tf_op jit(solution)/shard_map/ppermute | solution.py:37
  15.7 9.4 %collective-permute-start.5 = (bf16[512,512]{1,0:T(8,128)(2,1)S(1)}, bf16[512,512]{1,0:T(8,128)(2,1)S(1)}, u32[]{:S(2)}, u32[]{:S(2)}) collective-permute-start(bf16[512,512]{1,0:T(8,128)(2,1)S(1)} %stack.23), channel_id=1, source_target_pairs={{0,24},{1,7},{2,26},{3,1},{4,28},{5,3},{6,30},{7,5},{8,0},{9,15},{... | collective-permute-start | bytes 1572872 | tf_op jit(solution)/shard_map/ppermute | solution.py:37
  18.4 15.6 %collective-permute-start.6 = (bf16[512,512]{1,0:T(8,128)(2,1)S(1)}, bf16[512,512]{1,0:T(8,128)(2,1)S(1)}, u32[]{:S(2)}, u32[]{:S(2)}) collective-permute-start(bf16[512,512]{1,0:T(8,128)(2,1)S(1)} %stack.24), channel_id=1, source_target_pairs={{0,24},{1,7},{2,26},{3,1},{4,28},{5,3},{6,30},{7,5},{8,0},{9,15},{... | collective-permute-start | bytes 1572872 | tf_op jit(solution)/shard_map/ppermute | solution.py:37
  19.2 14.8 %collective-permute-start.7 = (bf16[512,512]{1,0:T(8,128)(2,1)S(1)}, bf16[512,512]{1,0:T(8,128)(2,1)S(1)}, u32[]{:S(2)}, u32[]{:S(2)}) collective-permute-start(bf16[512,512]{1,0:T(8,128)(2,1)S(1)} %stack.23), channel_id=1, source_target_pairs={{0,8},{1,3},{2,10},{3,5},{4,12},{5,7},{6,14},{7,1},{8,16},{9,11},{... | collective-permute-start | bytes 1572872 | tf_op jit(solution)/shard_map/ppermute | solution.py:37
  20.4 17.0 %collective-permute-start.11 = (bf16[768,512]{1,0:T(8,128)(2,1)S(1)}, bf16[768,512]{1,0:T(8,128)(2,1)S(1)}, u32[]{:S(2)}, u32[]{:S(2)}) collective-permute-start(bf16[768,512]{1,0:T(8,128)(2,1)S(1)} %get-tuple-element.49), channel_id=1, source_target_pairs={{0,1},{1,0},{2,3},{3,2},{4,5},{5,4},{6,7},{7,6},{8,9},{9,8},{10,11... | collective-permute-start | bytes 2359304 | tf_op jit(solution)/shard_map/ppermute | solution.py:37
  23.5 14.0 %collective-permute-start.10 = (bf16[512,512]{1,0:T(8,128)(2,1)S(1)}, bf16[512,512]{1,0:T(8,128)(2,1)S(1)}, u32[]{:S(2)}, u32[]{:S(2)}) collective-permute-start(bf16[512,512]{1,0:T(8,128)(2,1)S(1)} %collective-permute-done.8.high_3), channel_id=1, source_target_pairs={{0,8},{1,3},{2,10},{3,5},{4,12},{5,7},{6,14},{7,1},{8,16},{9,11},{... | collective-permute-start | bytes 1572872 | tf_op jit(solution)/shard_map/ppermute | solution.py:37
  25.1 12.3 %collective-permute-start.9 = (bf16[512,512]{1,0:T(8,128)(2,1)S(1)}, bf16[512,512]{1,0:T(8,128)(2,1)S(1)}, u32[]{:S(2)}, u32[]{:S(2)}) collective-permute-start(bf16[512,512]{1,0:T(8,128)(2,1)S(1)} %collective-permute-done.5.low_1), channel_id=1, source_target_pairs={{0,24},{1,7},{2,26},{3,1},{4,28},{5,3},{6,30},{7,5},{8,0},{9,15},{... | collective-permute-start | bytes 1572872 | tf_op jit(solution)/shard_map/ppermute | solution.py:37
  41.6 9.7 %collective-permute-start.16 = (bf16[512,512]{1,0:T(8,128)(2,1)S(1)}, bf16[512,512]{1,0:T(8,128)(2,1)S(1)}, u32[]{:S(2)}, u32[]{:S(2)}) collective-permute-start(bf16[512,512]{1,0:T(8,128)(2,1)S(1)} %get-tuple-element.59), channel_id=1, source_target_pairs={{0,24},{1,7},{2,26},{3,1},{4,28},{5,3},{6,30},{7,5},{8,0},{9,15},{... | collective-permute-start | bytes 1572872 | tf_op jit(solution)/shard_map/ppermute | solution.py:37
  44.3 10.8 %collective-permute-start.12 = (bf16[512,512]{1,0:T(8,128)(2,1)S(1)}, bf16[512,512]{1,0:T(8,128)(2,1)S(1)}, u32[]{:S(2)}, u32[]{:S(2)}) collective-permute-start(bf16[512,512]{1,0:T(8,128)(2,1)S(1)} %get-tuple-element.54), channel_id=1, source_target_pairs={{0,8},{1,3},{2,10},{3,5},{4,12},{5,7},{6,14},{7,1},{8,16},{9,11},{... | collective-permute-start | bytes 1572872 | tf_op jit(solution)/shard_map/ppermute | solution.py:37
  46.1 14.2 %collective-permute-start.15 = (bf16[512,512]{1,0:T(8,128)(2,1)S(1)}, bf16[512,512]{1,0:T(8,128)(2,1)S(1)}, u32[]{:S(2)}, u32[]{:S(2)}) collective-permute-start(bf16[512,512]{1,0:T(8,128)(2,1)S(1)} %get-tuple-element.57), channel_id=1, source_target_pairs={{0,8},{1,3},{2,10},{3,5},{4,12},{5,7},{6,14},{7,1},{8,16},{9,11},{... | collective-permute-start | bytes 1572872 | tf_op jit(solution)/shard_map/ppermute | solution.py:37
  46.2 24.7 %collective-permute-start.14 = (bf16[512,512]{1,0:T(8,128)(2,1)S(1)}, bf16[512,512]{1,0:T(8,128)(2,1)S(1)}, u32[]{:S(2)}, u32[]{:S(2)}) collective-permute-start(bf16[512,512]{1,0:T(8,128)(2,1)S(1)} %get-tuple-element.55), channel_id=1, source_target_pairs={{0,24},{1,7},{2,26},{3,1},{4,28},{5,3},{6,30},{7,5},{8,0},{9,15},{... | collective-permute-start | bytes 1572872 | tf_op jit(solution)/shard_map/ppermute | solution.py:37
  51.5 10.7 %collective-permute-start.17 = (bf16[512,512]{1,0:T(8,128)(2,1)S(1)}, bf16[512,512]{1,0:T(8,128)(2,1)S(1)}, u32[]{:S(2)}, u32[]{:S(2)}) collective-permute-start(bf16[512,512]{1,0:T(8,128)(2,1)S(1)} %add_convert_fusion), channel_id=1, source_target_pairs={{0,24},{1,7},{2,26},{3,1},{4,28},{5,3},{6,30},{7,5},{8,0},{9,15},{... | collective-permute-start | bytes 1572872 | tf_op jit(solution)/shard_map/ppermute | solution.py:37
  55.2 15.7 %collective-permute-start.13 = (bf16[512,512]{1,0:T(8,128)(2,1)S(1)}, bf16[512,512]{1,0:T(8,128)(2,1)S(1)}, u32[]{:S(2)}, u32[]{:S(2)}) collective-permute-start(bf16[512,512]{1,0:T(8,128)(2,1)S(1)} %add_convert_fusion.1), channel_id=1, source_target_pairs={{0,8},{1,3},{2,10},{3,5},{4,12},{5,7},{6,14},{7,1},{8,16},{9,11},{... | collective-permute-start | bytes 1572872 | tf_op jit(solution)/shard_map/ppermute | solution.py:37
  57.2 22.8 %copy-start = (f32[128,1024]{1,0:T(8,128)S(1)}, f32[128,1024]{1,0:T(8,128)}, u32[]{:S(2)}) copy-start(f32[128,1024]{1,0:T(8,128)} %weight.1) | copy-start | bytes 1572868
  57.2 22.8 %copy-start.1 = (f32[1,128,1024]{2,1,0:T(8,128)S(1)}, f32[1,128,1024]{2,1,0:T(8,128)}, u32[]{:S(2)}) copy-start(f32[1,128,1024]{2,1,0:T(8,128)} %param.11) | copy-start | bytes 1572868
  57.2 22.8 %copy-start.2 = (f32[1,128,1024]{2,1,0:T(8,128)S(1)}, f32[1,128,1024]{2,1,0:T(8,128)}, u32[]{:S(2)}) copy-start(f32[1,128,1024]{2,1,0:T(8,128)} %param.12) | copy-start | bytes 1572868
  62.4 10.2 %collective-permute-start.18 = (bf16[512,256]{1,0:T(8,128)(2,1)S(1)}, bf16[512,256]{1,0:T(8,128)(2,1)S(1)}, u32[]{:S(2)}, u32[]{:S(2)}) collective-permute-start(bf16[512,256]{1,0:T(8,128)(2,1)S(1)} %get-tuple-element.60), channel_id=1, source_target_pairs={{0,4},{1,17},{2,6},{3,19},{4,0},{5,21},{6,2},{7,23},{8,12},{9,25},... | collective-permute-start | bytes 786440 | tf_op jit(solution)/shard_map/ppermute | solution.py:37
  64.4 49.5 %copy-start.3 = (f32[128,1024]{1,0:T(8,128)S(1)}, f32[128,1024]{1,0:T(8,128)}, u32[]{:S(2)}) copy-start(f32[128,1024]{1,0:T(8,128)} %param.10) | copy-start | bytes 1572868
  64.4 12.2 %collective-permute-start.20 = (bf16[512,256]{1,0:T(8,128)(2,1)S(1)}, bf16[512,256]{1,0:T(8,128)(2,1)S(1)}, u32[]{:S(2)}, u32[]{:S(2)}) collective-permute-start(bf16[512,256]{1,0:T(8,128)(2,1)S(1)} %get-tuple-element.62), channel_id=1, source_target_pairs={{0,6},{1,25},{2,0},{3,27},{4,2},{5,29},{6,4},{7,31},{8,14},{9,1},{... | collective-permute-start | bytes 786440 | tf_op jit(solution)/shard_map/ppermute | solution.py:37
  71.1 7.3 %collective-permute-start.19 = (bf16[512,256]{1,0:T(8,128)(2,1)S(1)}, bf16[512,256]{1,0:T(8,128)(2,1)S(1)}, u32[]{:S(2)}, u32[]{:S(2)}) collective-permute-start(bf16[512,256]{1,0:T(8,128)(2,1)S(1)} %get-tuple-element.61), channel_id=1, source_target_pairs={{0,2},{1,9},{2,4},{3,11},{4,6},{5,13},{6,0},{7,15},{8,10},{9,17},{... | collective-permute-start | bytes 786440 | tf_op jit(solution)/shard_map/ppermute | solution.py:37
  78.5 1.4 %collective-permute-start.21 = (bf16[512,128]{1,0:T(8,128)(2,1)S(1)}, bf16[512,128]{1,0:T(8,128)(2,1)S(1)}, u32[]{:S(2)}, u32[]{:S(2)}) collective-permute-start(bf16[512,128]{1,0:T(8,128)(2,1)S(1)} %get-tuple-element.64), channel_id=1, source_target_pairs={{0,1},{1,0},{2,3},{3,2},{4,5},{5,4},{6,7},{7,6},{8,9},{9,8},{10,11... | collective-permute-start | bytes 393224 | tf_op jit(solution)/shard_map/ppermute | solution.py:37

commit v6 on v5

--- a/solution.py
+++ b/solution.py
@@ -98,8 +98,12 @@
             ref[span, :] = product(place, tokens, 0, range(4), block, span).astype(ref.dtype)
 
 
-def more_kernel(acc, acc_other, low_1, high_1, low_3, high_3, x, xo, out, out_other):
-    place = here()
+def more_kernel(acc, acc_other, low_1, high_1, low_3, high_3, x, xo, t, out, out_other, goals, sem):
+    place = here()
+    half = goals.shape[1]
+    columns = pl.ds(pl.multiple_of(place[2] * half, half), half)
+    fetch = pltpu.make_async_copy(t.at[:, columns], goals, sem)
+    fetch.start()
     blocks = ((1, (low_1, high_1)), (3, (low_3, high_3)))
     blocks = [(g, jnp.concatenate([ref[...] for ref in refs], axis=0)) for g, refs in blocks]
     for tokens, start, ref in ((x, acc, out), (xo, acc_other, out_other)):
@@ -107,6 +111,7 @@
         for g, block in blocks:
             total += product(place, tokens, g, range(4), block)
         ref[...] = total.astype(ref.dtype)
+    fetch.wait()
 
 
 def stack_kernel(a, b, out):
@@ -115,15 +120,11 @@
     out[rows:, :] = b[...]
 
 
-def late_kernel(scales, acc, acc_other, va, vb, x, xo, to, t, s_ref, so_ref, relay_a, relay_b, aims, sem):
-    place = here()
-    fetch = pltpu.make_async_copy(t, aims, sem)
-    fetch.start()
+def late_kernel(scales, acc, acc_other, va, vb, x, xo, to, t, s_ref, so_ref, relay_a, relay_b):
+    place = here()
     inv_width, inv_count = scales
-    for tokens, total, goals, out in ((xo, acc_other, to, so_ref), (x, acc, aims, s_ref)):
+    for tokens, total, goals, out in ((xo, acc_other, to, so_ref), (x, acc, t, s_ref)):
         proj = total[...].astype(jnp.float32) + product(place, tokens, 2, LOW, va[...]) + product(place, tokens, 2, HIGH, vb[...])
-        if goals is aims:
-            fetch.wait()
         scaled = (proj * inv_width - goals[...].astype(jnp.float32)) * inv_count
         out[...] = scaled.T.astype(jnp.bfloat16)
     for out, members in ((relay_a, LOW), (relay_b, HIGH)):
@@ -221,10 +222,9 @@
     rates = jnp.stack([rate, first_scale, second_scale] + [rate] * 5)
     rates = jnp.broadcast_to(rates[:, None], (8, half))
 
-    inner[3], targets = lax.optimization_barrier((inner[3], targets))
-    goals = lax.dynamic_slice_in_dim(targets, core * half, half, 1)
-    goals_other = lax.dynamic_slice_in_dim(targets, (1 - core) * half, half, 1)
-    inner[2], goals, goals_other = lax.optimization_barrier((inner[2], goals, goals_other))
+    inner[3], goals = lax.optimization_barrier((inner[3], targets))
+    goals_other = lax.dynamic_slice_in_dim(goals, (1 - core) * half, half, 1)
+    inner[2], goals_other = lax.optimization_barrier((inner[2], goals_other))
     goals_other = send(goals_other, partner)
     both = [((2 * inner[0].shape[0], half), bf16)]
     (high,) = local(stack_kernel, both, LIMIT_B, "stack", *inner[2:])
@@ -249,8 +249,20 @@
         pltpu.with_memory_space_constraint(tokens_other, pltpu.HBM),
     )
     pair = (tokens, tokens_other)
-    acc = local(
-        more_kernel, [((count, half), bf16)] * 2, LIMIT_A, "more", *acc, low_1, high_1, low_3, high_3, *pair, cost=4
+    *acc, goals = pl.pallas_call(
+        more_kernel,
+        out_shape=[jax.ShapeDtypeStruct((count, half), bf16)] * 3,
+        in_specs=[VM] * 8 + [hbm],
+        out_specs=[VM] * 3,
+        scratch_shapes=[pltpu.SemaphoreType.DMA],
+        compiler_params=params(LIMIT_A),
+        cost_estimate=pl.CostEstimate(flops=4 * GIGA, bytes_accessed=MIB, transcendentals=0),
+        name="more",
+    )(
+        *acc,
+        low_1, high_1, low_3, high_3,
+        *[pltpu.with_memory_space_constraint(k, pltpu.VMEM) for k in pair],
+        pltpu.with_memory_space_constraint(targets, pltpu.HBM),
     )
     mid = ((half, 2 * SIDE), bf16)
     s, so, relay_a, relay_b = pl.pallas_call(
@@ -258,9 +270,8 @@
         out_shape=[
             jax.ShapeDtypeStruct(*k) for k in [((half, count), bf16)] * 2 + [mid] * 2
         ],
-        in_specs=[VM] * 7 + [hbm],
+        in_specs=[VM] * 8,
         out_specs=[VM] * 4,
-        scratch_shapes=[pltpu.VMEM((count, half), bf16), pltpu.SemaphoreType.DMA],
         compiler_params=params(LIMIT_A),
         name="late",
     )(
@@ -268,7 +279,7 @@
         low_2, high_2,
         *[pltpu.with_memory_space_constraint(k, pltpu.VMEM) for k in pair],
         goals_other,
-        pltpu.with_memory_space_constraint(goals, pltpu.HBM),
+        goals,
     )
     sides = functools.partial(sides_kernel, (HIGH, LOW))
     up_b, down_a = local(sides, [mid] * 2, LIMIT_B, "sides_near", s, so, *pair, cost=2)

time: 117 us -> 116 us (level)
  starting transfers between devices: 35.6 us -> 28.1 us
  waiting for transfers between devices: 20.1 us -> 26.7 us
  blocking collectives: 32.4 us -> 33.8 us
    ppermute x22, starting transfers between devices: 35.6 us -> 28.1 us  [send(): return lax.ppermute(value, AXES, pairs)]
    ppermute x22, waiting for transfers between devices: 20.1 us -> 26.7 us  [send(): return lax.ppermute(value, AXES, pairs)]
    pallas_call x0 -> x1, Pallas kernels: none -> 4.12 us  [per_device(): pl.pallas_call(more_kernel, out_shape=[jax.ShapeDtypeStruct((count, half)...]
    pallas_call x10 -> x9, Pallas kernels: 10.8 us -> 7.41 us  [local(): pl.pallas_call(kernel, out_shape=[jax.ShapeDtypeStruct(*s) for s in shape...]
    all_to_all x1, blocking collectives: 18.9 us -> 20.3 us  [per_device(): lax.all_to_all(pseudo.reshape(NZ, rows // NZ, columns), 'island', 0, 0, t...]
  transfers between devices with their start and end apart: 22 -> 22, of which waited for: 11 -> 14; matrix products, arithmetic and copies ran while one was open for 2% -> 1% of each run, Pallas kernels for 13% -> 13%
where the time goes in v6:
time: 116 us; the launch traced here: 115 us
  blocking collectives  33.8 us (29%)
  starting transfers between devices  28.1 us (24%)
  waiting for transfers between devices  26.7 us (23%)
  Pallas kernels  20.5 us (18%)
  other arithmetic  2.57 us (2%)
  between operations  1.7 us (1%)
  local copies, waits for them, and re-layouts  1.41 us (1%)
    ppermute x22, starting transfers between devices, send(): return lax.ppermute(value, AXES, pairs)  28.1 us
    ppermute x22, waiting for transfers between devices, send(): return lax.ppermute(value, AXES, pairs)  26.7 us
    all_to_all x1, blocking collectives, per_device(): lax.all_to_all(pseudo.reshape(NZ, rows // NZ, columns), 'island', 0, 0, t...  20.3 us
    all_to_all x1, blocking collectives, per_device(): lax.all_to_all(spread, 'island', 0, 0, tiled=True).reshape(rows, columns)  13.5 us
    pallas_call x9, Pallas kernels, local(): pl.pallas_call(kernel, out_shape=[jax.ShapeDtypeStruct(*s) for s in shape...  7.41 us
    pallas_call x1, Pallas kernels, per_device(): pl.pallas_call(first_kernel, out_shape=[jax.ShapeDtypeStruct((count, half...  5.15 us
    pallas_call x1, Pallas kernels, per_device(): pl.pallas_call(more_kernel, out_shape=[jax.ShapeDtypeStruct((count, half)...  4.12 us
    pallas_call x1, Pallas kernels, per_device(): pl.pallas_call(functools.partial(late_kernel, scales), out_shape=[jax.Sha...  3.8 us
  transfers between devices with their start and end apart: 22, of which 14 were waited for; matrix products, arithmetic and copies ran while one was open for 1% of the time, Pallas kernels for 13%

profile of v6, /device:TPU:2, one launch (start us, length us, event | category | flops | bytes accessed | tf_op | source)
XLA Modules:
  0.0 114.7 jit_solution(9347367829491537478)
XLA Ops:
  0.6 1.1 convert_element_type.41
  1.8 0.1 collective-permute-start
  1.9 1.3 %collective-permute-done = bf16[128,512]{1,0:T(8,128)(2,1)S(1)} collective-permute-done((bf16[128,512]{1,0:T(8,128)(2,1)S(1)}, bf16[128,512]{1,0:T(8,128)(2,1)S(1)}, u32[]{:S(2)}, u32[]{:S(2)}) %collective-permute-start) | collective-permute-done | bytes 131104 | tf_op jit(solution)/shard_map/ppermute | solution.py:37
  3.2 0.1 collective-permute-start.4
  3.4 1.6 %collective-permute-start.3 = (bf16[256,512]{1,0:T(8,128)(2,1)S(1)}, bf16[256,512]{1,0:T(8,128)(2,1)S(1)}, u32[]{:S(2)}, u32[]{:S(2)}) collective-permute-start(bf16[256,512]{1,0:T(8,128)(2,1)S(1)} %maximum_select_fusion.a), channel_id=1, source_target_pairs={{0,2},{1,9},{2,4},{3,11},{4,6},{5,13},{6,0},{7,15},{8,10},{9,17},{... | collective-permute-start | bytes 786440 | tf_op jit(solution)/shard_map/ppermute | solution.py:37
  5.0 2.8 %collective-permute-start.2 = (bf16[256,512]{1,0:T(8,128)(2,1)S(1)}, bf16[256,512]{1,0:T(8,128)(2,1)S(1)}, u32[]{:S(2)}, u32[]{:S(2)}) collective-permute-start(bf16[256,512]{1,0:T(8,128)(2,1)S(1)} %maximum_select_fusion.a), channel_id=1, source_target_pairs={{0,4},{1,17},{2,6},{3,19},{4,0},{5,21},{6,2},{7,23},{8,12},{9,25},... | collective-permute-start | bytes 786440 | tf_op jit(solution)/shard_map/ppermute | solution.py:37
  7.8 0.4 collective-permute-start.1
  8.2 1.9 %collective-permute-done.3.d.b = bf16[256,512]{1,0:T(8,128)(2,1)S(1)} collective-permute-done((bf16[256,512]{1,0:T(8,128)(2,1)S(1)}, bf16[256,512]{1,0:T(8,128)(2,1)S(1)}, u32[]{:S(2)}, u32[]{:S(2)}) %collective-permute-start.3) | collective-permute-done | bytes 262176 | tf_op jit(solution)/shard_map/ppermute | solution.py:37
  10.1 1.2 %constant_dynamic-slice_fusion = bf16[768,512]{1,0:T(8,128)(2,1)S(1)} fusion(bf16[768,1024]{1,0:T(8,128)(2,1)} %t.1, s32[]{:T(128)S(6)} %select_n.17), kind=kLoop, calls=%fused_computation.9 | loop fusion | bytes 1572868 | tf_op jit(solution)/shard_map/dynamic_slice | solution.py:226
  11.3 1.7 %collective-permute-done.2.c.a = bf16[256,512]{1,0:T(8,128)(2,1)S(1)} collective-permute-done((bf16[256,512]{1,0:T(8,128)(2,1)S(1)}, bf16[256,512]{1,0:T(8,128)(2,1)S(1)}, u32[]{:S(2)}, u32[]{:S(2)}) %collective-permute-start.2) | collective-permute-done | bytes 262176 | tf_op jit(solution)/shard_map/ppermute | solution.py:37
  13.0 1.7 %collective-permute-start.8 = (bf16[512,512]{1,0:T(8,128)(2,1)S(1)}, bf16[512,512]{1,0:T(8,128)(2,1)S(1)}, u32[]{:S(2)}, u32[]{:S(2)}) collective-permute-start(bf16[512,512]{1,0:T(8,128)(2,1)S(1)} %stack.24), channel_id=1, source_target_pairs={{0,8},{1,3},{2,10},{3,5},{4,12},{5,7},{6,14},{7,1},{8,16},{9,11},{... | collective-permute-start | bytes 1572872 | tf_op jit(solution)/shard_map/ppermute | solution.py:37
  14.7 1.0 collective-permute-done.1.b
  15.7 2.7 %collective-permute-start.5 = (bf16[512,512]{1,0:T(8,128)(2,1)S(1)}, bf16[512,512]{1,0:T(8,128)(2,1)S(1)}, u32[]{:S(2)}, u32[]{:S(2)}) collective-permute-start(bf16[512,512]{1,0:T(8,128)(2,1)S(1)} %stack.23), channel_id=1, source_target_pairs={{0,24},{1,7},{2,26},{3,1},{4,28},{5,3},{6,30},{7,5},{8,0},{9,15},{... | collective-permute-start | bytes 1572872 | tf_op jit(solution)/shard_map/ppermute | solution.py:37
  18.4 0.7 collective-permute-start.6
  19.2 1.3 %collective-permute-start.7 = (bf16[512,512]{1,0:T(8,128)(2,1)S(1)}, bf16[512,512]{1,0:T(8,128)(2,1)S(1)}, u32[]{:S(2)}, u32[]{:S(2)}) collective-permute-start(bf16[512,512]{1,0:T(8,128)(2,1)S(1)} %stack.23), channel_id=1, source_target_pairs={{0,8},{1,3},{2,10},{3,5},{4,12},{5,7},{6,14},{7,1},{8,16},{9,11},{... | collective-permute-start | bytes 1572872 | tf_op jit(solution)/shard_map/ppermute | solution.py:37
  20.4 3.0 %collective-permute-done.8.high_3 = bf16[512,512]{1,0:T(8,128)(2,1)S(1)} collective-permute-done((bf16[512,512]{1,0:T(8,128)(2,1)S(1)}, bf16[512,512]{1,0:T(8,128)(2,1)S(1)}, u32[]{:S(2)}, u32[]{:S(2)}) %collective-permute-start.8) | collective-permute-done | bytes 524320 | tf_op jit(solution)/shard_map/ppermute | solution.py:37
  23.5 0.4 collective-permute-start.10
  23.8 1.3 %collective-permute-done.5.low_1 = bf16[512,512]{1,0:T(8,128)(2,1)S(1)} collective-permute-done((bf16[512,512]{1,0:T(8,128)(2,1)S(1)}, bf16[512,512]{1,0:T(8,128)(2,1)S(1)}, u32[]{:S(2)}, u32[]{:S(2)}) %collective-permute-start.5) | collective-permute-done | bytes 524320 | tf_op jit(solution)/shard_map/ppermute | solution.py:37
  25.1 3.7 %collective-permute-start.9 = (bf16[512,512]{1,0:T(8,128)(2,1)S(1)}, bf16[512,512]{1,0:T(8,128)(2,1)S(1)}, u32[]{:S(2)}, u32[]{:S(2)}) collective-permute-start(bf16[512,512]{1,0:T(8,128)(2,1)S(1)} %collective-permute-done.5.low_1), channel_id=1, source_target_pairs={{0,24},{1,7},{2,26},{3,1},{4,28},{5,3},{6,30},{7,5},{8,0},{9,15},{... | collective-permute-start | bytes 1572872 | tf_op jit(solution)/shard_map/ppermute | solution.py:37
  28.8 5.2 %first.1 = (bf16[768,512]{1,0:T(8,128)(2,1)S(1)}, bf16[768,512]{1,0:T(8,128)(2,1)S(1)}, bf16[768,4096]{1,0:T(8,128)(2,1)S(1)}, bf16[768,4096]{1,0:T(8,128)(2,1)S(1)}) custom-call(bf16[256,512]{1,0:T(8,128)(2,1)S(1)} %maximum_select_fusion.a, bf16[256,512]{1,0:T(8,128)(2,1)S(1)} %collective-permute-done.1.b, bf16[256,512]{1,0:T(8,128)(2,1)S(1)} %collective-permute-done.2.c.a, ...), custom_call_target="tpu_custom_call" | custom-call | tf_op jit(solution)/shard_map/first/pallas_call | solution.py:238
  34.0 4.1 %more.1 = (bf16[768,512]{1,0:T(8,128)(2,1)S(1)}, bf16[768,512]{1,0:T(8,128)(2,1)S(1)}, bf16[768,512]{1,0:T(8,128)(2,1)S(1)}) custom-call(bf16[768,512]{1,0:T(8,128)(2,1)S(1)} %get-tuple-element.42.acc, bf16[768,512]{1,0:T(8,128)(2,1)S(1)} %get-tuple-element.43.acc_other, bf16[512,512]{1,0:T(8,128)(2,1)S(1)} %collective-permute-done.5.low_1, ...), custom_call_target="tpu_custom_call" | custom-call | flops 4000000000 | bytes 1048576 | tf_op jit(solution)/shard_map/more/pallas_call | solution.py:252
  38.1 3.8 %late.1 = (bf16[512,768]{1,0:T(8,128)(2,1)S(1)}, bf16[512,768]{1,0:T(8,128)(2,1)S(1)}, bf16[512,512]{1,0:T(8,128)(2,1)S(1)}, bf16[512,512]{1,0:T(8,128)(2,1)S(1)}) custom-call(bf16[768,512]{1,0:T(8,128)(2,1)S(1)} %get-tuple-element.47.acc, bf16[768,512]{1,0:T(8,128)(2,1)S(1)} %get-tuple-element.48.acc_other, bf16[512,512]{1,0:T(8,128)(2,1)S(1)} %collective-permute-done.9.va, ...), custom_call_target="tpu_custom_call" | custom-call | tf_op jit(solution)/shard_map/late/pallas_call | solution.py:268
  42.0 2.0 %collective-permute-start.16 = (bf16[512,512]{1,0:T(8,128)(2,1)S(1)}, bf16[512,512]{1,0:T(8,128)(2,1)S(1)}, u32[]{:S(2)}, u32[]{:S(2)}) collective-permute-start(bf16[512,512]{1,0:T(8,128)(2,1)S(1)} %get-tuple-element.59), channel_id=1, source_target_pairs={{0,24},{1,7},{2,26},{3,1},{4,28},{5,3},{6,30},{7,5},{8,0},{9,15},{... | collective-permute-start | bytes 1572872 | tf_op jit(solution)/shard_map/ppermute | solution.py:37
  43.9 0.1 collective-permute-start.12
  44.1 1.8 %sides_near.1 = (bf16[512,512]{1,0:T(8,128)(2,1)S(1)}, bf16[512,512]{1,0:T(8,128)(2,1)S(1)}) custom-call(bf16[512,768]{1,0:T(8,128)(2,1)S(1)} %get-tuple-element.51.s, bf16[512,768]{1,0:T(8,128)(2,1)S(1)} %get-tuple-element.52.so, bf16[768,4096]{1,0:T(8,128)(2,1)S(1)} %get-tuple-element.45.x, bf16[768,4096]{1,0:T(8,128)(2,1)S(1)} %get-tuple-element.46.xo), custom_call_target="tpu_custom_call" | custom-call | flops 2000000000 | bytes 1048576 | tf_op jit(solution)/shard_map/sides_near/pallas_call | solution.py:186
  46.0 3.2 %collective-permute-start.14 = (bf16[512,512]{1,0:T(8,128)(2,1)S(1)}, bf16[512,512]{1,0:T(8,128)(2,1)S(1)}, u32[]{:S(2)}, u32[]{:S(2)}) collective-permute-start(bf16[512,512]{1,0:T(8,128)(2,1)S(1)} %get-tuple-element.55), channel_id=1, source_target_pairs={{0,24},{1,7},{2,26},{3,1},{4,28},{5,3},{6,30},{7,5},{8,0},{9,15},{... | collective-permute-start | bytes 1572872 | tf_op jit(solution)/shard_map/ppermute | solution.py:37
  49.2 1.8 %sides_rest.1 = (bf16[512,512]{1,0:T(8,128)(2,1)S(1)}, bf16[512,512]{1,0:T(8,128)(2,1)S(1)}) custom-call(bf16[512,768]{1,0:T(8,128)(2,1)S(1)} %get-tuple-element.51.s, bf16[512,768]{1,0:T(8,128)(2,1)S(1)} %get-tuple-element.52.so, bf16[768,4096]{1,0:T(8,128)(2,1)S(1)} %get-tuple-element.45.x, bf16[768,4096]{1,0:T(8,128)(2,1)S(1)} %get-tuple-element.46.xo), custom_call_target="tpu_custom_call" | custom-call | flops 2000000000 | bytes 1048576 | tf_op jit(solution)/shard_map/sides_rest/pallas_call | solution.py:186
  51.0 0.2 collective-permute-done.16
  51.2 0.1 add_convert_fusion
  51.4 3.4 %collective-permute-start.17 = (bf16[512,512]{1,0:T(8,128)(2,1)S(1)}, bf16[512,512]{1,0:T(8,128)(2,1)S(1)}, u32[]{:S(2)}, u32[]{:S(2)}) collective-permute-start(bf16[512,512]{1,0:T(8,128)(2,1)S(1)} %add_convert_fusion), channel_id=1, source_target_pairs={{0,24},{1,7},{2,26},{3,1},{4,28},{5,3},{6,30},{7,5},{8,0},{9,15},{... | collective-permute-start | bytes 1572872 | tf_op jit(solution)/shard_map/ppermute | solution.py:37
  54.7 0.1 add_convert_fusion.1
  55.0 1.8 %kept.1 = f32[512,1024]{1,0:T(8,128)S(1)} custom-call(bf16[512,768]{1,0:T(8,128)(2,1)S(1)} %get-tuple-element.51.s, bf16[512,768]{1,0:T(8,128)(2,1)S(1)} %get-tuple-element.52.so, bf16[768,4096]{1,0:T(8,128)(2,1)S(1)} %get-tuple-element.45.x, bf16[768,4096]{1,0:T(8,128)(2,1)S(1)} %get-tuple-element.46.xo), custom_call_target="tpu_custom_call" | custom-call | flops 2000000000 | bytes 1048576 | tf_op jit(solution)/shard_map/kept/pallas_call | solution.py:186
  56.9 3.1 %collective-permute-done.15.up = bf16[512,512]{1,0:T(8,128)(2,1)S(1)} collective-permute-done((bf16[512,512]{1,0:T(8,128)(2,1)S(1)}, bf16[512,512]{1,0:T(8,128)(2,1)S(1)}, u32[]{:S(2)}, u32[]{:S(2)}) %collective-permute-start.15) | collective-permute-done | bytes 524320 | tf_op jit(solution)/shard_map/ppermute | solution.py:37
  59.9 4.8 %collective-permute-done.17.down = bf16[512,512]{1,0:T(8,128)(2,1)S(1)} collective-permute-done((bf16[512,512]{1,0:T(8,128)(2,1)S(1)}, bf16[512,512]{1,0:T(8,128)(2,1)S(1)}, u32[]{:S(2)}, u32[]{:S(2)}) %collective-permute-start.17) | collective-permute-done | bytes 524320 | tf_op jit(solution)/shard_map/ppermute | solution.py:37
  64.8 0.2 fold_high.1
  65.0 3.0 %collective-permute-start.20 = (bf16[512,256]{1,0:T(8,128)(2,1)S(1)}, bf16[512,256]{1,0:T(8,128)(2,1)S(1)}, u32[]{:S(2)}, u32[]{:S(2)}) collective-permute-start(bf16[512,256]{1,0:T(8,128)(2,1)S(1)} %get-tuple-element.62), channel_id=1, source_target_pairs={{0,6},{1,25},{2,0},{3,27},{4,2},{5,29},{6,4},{7,31},{8,14},{9,1},{... | collective-permute-start | bytes 786440 | tf_op jit(solution)/shard_map/ppermute | solution.py:37
  68.1 1.0 collective-permute-done.13.up
  69.1 0.1 fold_low.1
  69.2 0.5 collective-permute-start.19
  69.7 3.3 %collective-permute-done.18.a = bf16[512,256]{1,0:T(8,128)(2,1)S(1)} collective-permute-done((bf16[512,256]{1,0:T(8,128)(2,1)S(1)}, bf16[512,256]{1,0:T(8,128)(2,1)S(1)}, u32[]{:S(2)}, u32[]{:S(2)}) %collective-permute-start.18) | collective-permute-done | bytes 262176 | tf_op jit(solution)/shard_map/ppermute | solution.py:37
  73.0 2.7 %collective-permute-done.20.c = bf16[512,256]{1,0:T(8,128)(2,1)S(1)} collective-permute-done((bf16[512,256]{1,0:T(8,128)(2,1)S(1)}, bf16[512,256]{1,0:T(8,128)(2,1)S(1)}, u32[]{:S(2)}, u32[]{:S(2)}) %collective-permute-start.20) | collective-permute-done | bytes 262176 | tf_op jit(solution)/shard_map/ppermute | solution.py:37
  75.7 0.9 collective-permute-done.19.b
  76.6 0.1 split.1
  77.8 0.4 collective-permute-done.21.refs_1_
  78.3 1.4 %inner_step.1 = (f32[128,1024]{1,0:T(8,128)}, f32[128,1024]{1,0:T(8,128)}, bf16[128,1024]{1,0:T(8,128)(2,1)S(1)}) custom-call(f32[8,512]{1,0:T(8,128)S(1)} %broadcast_in_dim.8.rates, f32[128,1024]{1,0:T(8,128)S(1)} %bitcast.14, f32[128,1024]{1,0:T(8,128)S(1)} %bitcast.15, f32[128,1024]{1,0:T(8,128)S(1)} %copy-done, ...), custom_call_target="tpu_custom_call" | custom-call | flops 1000000000 | bytes 1048576 | tf_op jit(solution)/shard_map/inner_step/pallas_call | solution.py:186
  79.7 20.3 %all_to_all.10 = bf16[8,16,1024]{2,1,0:T(8,128)(2,1)S(1)} all-to-all(bf16[8,16,1024]{2,1,0:T(8,128)(2,1)S(1)} %bitcast.13), channel_id=1, replica_groups=mesh['island'=8,'fsdp'=8,'dp'=4] {'island'}, dimensions={0} | all-to-all | bytes 524288 | tf_op jit(solution)/shard_map/all_to_all | solution.py:316
  100.1 13.5 %all_to_all.11 = bf16[8,16,1024]{2,1,0:T(8,128)(2,1)S(1)} all-to-all(bf16[8,16,1024]{2,1,0:T(8,128)(2,1)S(1)} %broadcast_in_dim.9), channel_id=1, replica_groups=mesh['island'=8,'fsdp'=8,'dp'=4] {'island'}, dimensions={0} | all-to-all | bytes 524288 | tf_op jit(solution)/shard_map/all_to_all | solution.py:319
  113.6 1.1 fusion.1
  (30 shorter events, 0.8 us)
Async XLA Ops:
  1.8 1.4 %collective-permute-start = (bf16[128,512]{1,0:T(8,128)(2,1)S(1)}, bf16[128,512]{1,0:T(8,128)(2,1)S(1)}, u32[]{:S(2)}, u32[]{:S(2)}) collective-permute-start(bf16[128,512]{1,0:T(8,128)(2,1)S(1)} %get-tuple-element.71), channel_id=1, source_target_pairs={{0,1},{1,0},{2,3},{3,2},{4,5},{5,4},{6,7},{7,6},{8,9},{9,8},{10,11... | collective-permute-start | bytes 393224 | tf_op jit(solution)/shard_map/ppermute | solution.py:37
  3.2 12.5 %collective-permute-start.4 = (bf16[768,4096]{1,0:T(8,128)(2,1)}, bf16[768,4096]{1,0:T(8,128)(2,1)}, u32[]{:S(2)}, u32[]{:S(2)}) collective-permute-start(bf16[768,4096]{1,0:T(8,128)(2,1)} %x.1), channel_id=1, source_target_pairs={{0,1},{1,0},{2,3},{3,2},{4,5},{5,4},{6,7},{7,6},{8,9},{9,8},{10,11... | collective-permute-start | bytes 18874376 | tf_op jit(solution)/shard_map/ppermute | solution.py:37
  3.4 6.7 %collective-permute-start.3 = (bf16[256,512]{1,0:T(8,128)(2,1)S(1)}, bf16[256,512]{1,0:T(8,128)(2,1)S(1)}, u32[]{:S(2)}, u32[]{:S(2)}) collective-permute-start(bf16[256,512]{1,0:T(8,128)(2,1)S(1)} %maximum_select_fusion.a), channel_id=1, source_target_pairs={{0,2},{1,9},{2,4},{3,11},{4,6},{5,13},{6,0},{7,15},{8,10},{9,17},{... | collective-permute-start | bytes 786440 | tf_op jit(solution)/shard_map/ppermute | solution.py:37
  5.0 8.0 %collective-permute-start.2 = (bf16[256,512]{1,0:T(8,128)(2,1)S(1)}, bf16[256,512]{1,0:T(8,128)(2,1)S(1)}, u32[]{:S(2)}, u32[]{:S(2)}) collective-permute-start(bf16[256,512]{1,0:T(8,128)(2,1)S(1)} %maximum_select_fusion.a), channel_id=1, source_target_pairs={{0,4},{1,17},{2,6},{3,19},{4,0},{5,21},{6,2},{7,23},{8,12},{9,25},... | collective-permute-start | bytes 786440 | tf_op jit(solution)/shard_map/ppermute | solution.py:37
  7.8 7.8 %collective-permute-start.1 = (bf16[256,512]{1,0:T(8,128)(2,1)S(1)}, bf16[256,512]{1,0:T(8,128)(2,1)S(1)}, u32[]{:S(2)}, u32[]{:S(2)}) collective-permute-start(bf16[256,512]{1,0:T(8,128)(2,1)S(1)} %maximum_select_fusion.a), channel_id=1, source_target_pairs={{0,6},{1,25},{2,0},{3,27},{4,2},{5,29},{6,4},{7,31},{8,14},{9,1},{... | collective-permute-start | bytes 786440 | tf_op jit(solution)/shard_map/ppermute | solution.py:37
  13.0 10.5 %collective-permute-start.8 = (bf16[512,512]{1,0:T(8,128)(2,1)S(1)}, bf16[512,512]{1,0:T(8,128)(2,1)S(1)}, u32[]{:S(2)}, u32[]{:S(2)}) collective-permute-start(bf16[512,512]{1,0:T(8,128)(2,1)S(1)} %stack.24), channel_id=1, source_target_pairs={{0,8},{1,3},{2,10},{3,5},{4,12},{5,7},{6,14},{7,1},{8,16},{9,11},{... | collective-permute-start | bytes 1572872 | tf_op jit(solution)/shard_map/ppermute | solution.py:37
  15.7 9.4 %collective-permute-start.5 = (bf16[512,512]{1,0:T(8,128)(2,1)S(1)}, bf16[512,512]{1,0:T(8,128)(2,1)S(1)}, u32[]{:S(2)}, u32[]{:S(2)}) collective-permute-start(bf16[512,512]{1,0:T(8,128)(2,1)S(1)} %stack.23), channel_id=1, source_target_pairs={{0,24},{1,7},{2,26},{3,1},{4,28},{5,3},{6,30},{7,5},{8,0},{9,15},{... | collective-permute-start | bytes 1572872 | tf_op jit(solution)/shard_map/ppermute | solution.py:37
  18.4 15.6 %collective-permute-start.6 = (bf16[512,512]{1,0:T(8,128)(2,1)S(1)}, bf16[512,512]{1,0:T(8,128)(2,1)S(1)}, u32[]{:S(2)}, u32[]{:S(2)}) collective-permute-start(bf16[512,512]{1,0:T(8,128)(2,1)S(1)} %stack.24), channel_id=1, source_target_pairs={{0,24},{1,7},{2,26},{3,1},{4,28},{5,3},{6,30},{7,5},{8,0},{9,15},{... | collective-permute-start | bytes 1572872 | tf_op jit(solution)/shard_map/ppermute | solution.py:37
  19.2 14.8 %collective-permute-start.7 = (bf16[512,512]{1,0:T(8,128)(2,1)S(1)}, bf16[512,512]{1,0:T(8,128)(2,1)S(1)}, u32[]{:S(2)}, u32[]{:S(2)}) collective-permute-start(bf16[512,512]{1,0:T(8,128)(2,1)S(1)} %stack.23), channel_id=1, source_target_pairs={{0,8},{1,3},{2,10},{3,5},{4,12},{5,7},{6,14},{7,1},{8,16},{9,11},{... | collective-permute-start | bytes 1572872 | tf_op jit(solution)/shard_map/ppermute | solution.py:37
  20.4 17.7 %collective-permute-start.11 = (bf16[768,512]{1,0:T(8,128)(2,1)S(1)}, bf16[768,512]{1,0:T(8,128)(2,1)S(1)}, u32[]{:S(2)}, u32[]{:S(2)}) collective-permute-start(bf16[768,512]{1,0:T(8,128)(2,1)S(1)} %constant_dynamic-slice_fusion), channel_id=1, source_target_pairs={{0,1},{1,0},{2,3},{3,2},{4,5},{5,4},{6,7},{7,6},{8,9},{9,8},{10,11... | collective-permute-start | bytes 2359304 | tf_op jit(solution)/shard_map/ppermute | solution.py:37
  23.5 14.7 %collective-permute-start.10 = (bf16[512,512]{1,0:T(8,128)(2,1)S(1)}, bf16[512,512]{1,0:T(8,128)(2,1)S(1)}, u32[]{:S(2)}, u32[]{:S(2)}) collective-permute-start(bf16[512,512]{1,0:T(8,128)(2,1)S(1)} %collective-permute-done.8.high_3), channel_id=1, source_target_pairs={{0,8},{1,3},{2,10},{3,5},{4,12},{5,7},{6,14},{7,1},{8,16},{9,11},{... | collective-permute-start | bytes 1572872 | tf_op jit(solution)/shard_map/ppermute | solution.py:37
  25.1 13.0 %collective-permute-start.9 = (bf16[512,512]{1,0:T(8,128)(2,1)S(1)}, bf16[512,512]{1,0:T(8,128)(2,1)S(1)}, u32[]{:S(2)}, u32[]{:S(2)}) collective-permute-start(bf16[512,512]{1,0:T(8,128)(2,1)S(1)} %collective-permute-done.5.low_1), channel_id=1, source_target_pairs={{0,24},{1,7},{2,26},{3,1},{4,28},{5,3},{6,30},{7,5},{8,0},{9,15},{... | collective-permute-start | bytes 1572872 | tf_op jit(solution)/shard_map/ppermute | solution.py:37
  42.0 9.3 %collective-permute-start.16 = (bf16[512,512]{1,0:T(8,128)(2,1)S(1)}, bf16[512,512]{1,0:T(8,128)(2,1)S(1)}, u32[]{:S(2)}, u32[]{:S(2)}) collective-permute-start(bf16[512,512]{1,0:T(8,128)(2,1)S(1)} %get-tuple-element.59), channel_id=1, source_target_pairs={{0,24},{1,7},{2,26},{3,1},{4,28},{5,3},{6,30},{7,5},{8,0},{9,15},{... | collective-permute-start | bytes 1572872 | tf_op jit(solution)/shard_map/ppermute | solution.py:37
  43.9 10.8 %collective-permute-start.12 = (bf16[512,512]{1,0:T(8,128)(2,1)S(1)}, bf16[512,512]{1,0:T(8,128)(2,1)S(1)}, u32[]{:S(2)}, u32[]{:S(2)}) collective-permute-start(bf16[512,512]{1,0:T(8,128)(2,1)S(1)} %get-tuple-element.54), channel_id=1, source_target_pairs={{0,8},{1,3},{2,10},{3,5},{4,12},{5,7},{6,14},{7,1},{8,16},{9,11},{... | collective-permute-start | bytes 1572872 | tf_op jit(solution)/shard_map/ppermute | solution.py:37
  45.9 14.0 %collective-permute-start.15 = (bf16[512,512]{1,0:T(8,128)(2,1)S(1)}, bf16[512,512]{1,0:T(8,128)(2,1)S(1)}, u32[]{:S(2)}, u32[]{:S(2)}) collective-permute-start(bf16[512,512]{1,0:T(8,128)(2,1)S(1)} %get-tuple-element.57), channel_id=1, source_target_pairs={{0,8},{1,3},{2,10},{3,5},{4,12},{5,7},{6,14},{7,1},{8,16},{9,11},{... | collective-permute-start | bytes 1572872 | tf_op jit(solution)/shard_map/ppermute | solution.py:37
  46.0 22.1 %collective-permute-start.14 = (bf16[512,512]{1,0:T(8,128)(2,1)S(1)}, bf16[512,512]{1,0:T(8,128)(2,1)S(1)}, u32[]{:S(2)}, u32[]{:S(2)}) collective-permute-start(bf16[512,512]{1,0:T(8,128)(2,1)S(1)} %get-tuple-element.55), channel_id=1, source_target_pairs={{0,24},{1,7},{2,26},{3,1},{4,28},{5,3},{6,30},{7,5},{8,0},{9,15},{... | collective-permute-start | bytes 1572872 | tf_op jit(solution)/shard_map/ppermute | solution.py:37
  51.4 13.4 %collective-permute-start.17 = (bf16[512,512]{1,0:T(8,128)(2,1)S(1)}, bf16[512,512]{1,0:T(8,128)(2,1)S(1)}, u32[]{:S(2)}, u32[]{:S(2)}) collective-permute-start(bf16[512,512]{1,0:T(8,128)(2,1)S(1)} %add_convert_fusion), channel_id=1, source_target_pairs={{0,24},{1,7},{2,26},{3,1},{4,28},{5,3},{6,30},{7,5},{8,0},{9,15},{... | collective-permute-start | bytes 1572872 | tf_op jit(solution)/shard_map/ppermute | solution.py:37
  54.9 14.2 %collective-permute-start.13 = (bf16[512,512]{1,0:T(8,128)(2,1)S(1)}, bf16[512,512]{1,0:T(8,128)(2,1)S(1)}, u32[]{:S(2)}, u32[]{:S(2)}) collective-permute-start(bf16[512,512]{1,0:T(8,128)(2,1)S(1)} %add_convert_fusion.1), channel_id=1, source_target_pairs={{0,8},{1,3},{2,10},{3,5},{4,12},{5,7},{6,14},{7,1},{8,16},{9,11},{... | collective-permute-start | bytes 1572872 | tf_op jit(solution)/shard_map/ppermute | solution.py:37
  56.8 21.5 %copy-start = (f32[128,1024]{1,0:T(8,128)S(1)}, f32[128,1024]{1,0:T(8,128)}, u32[]{:S(2)}) copy-start(f32[128,1024]{1,0:T(8,128)} %weight.1) | copy-start | bytes 1572868
  56.8 21.4 %copy-start.1 = (f32[1,128,1024]{2,1,0:T(8,128)S(1)}, f32[1,128,1024]{2,1,0:T(8,128)}, u32[]{:S(2)}) copy-start(f32[1,128,1024]{2,1,0:T(8,128)} %param.11) | copy-start | bytes 1572868
  56.9 21.4 %copy-start.2 = (f32[1,128,1024]{2,1,0:T(8,128)S(1)}, f32[1,128,1024]{2,1,0:T(8,128)}, u32[]{:S(2)}) copy-start(f32[1,128,1024]{2,1,0:T(8,128)} %param.12) | copy-start | bytes 1572868
  64.9 8.1 %collective-permute-start.18 = (bf16[512,256]{1,0:T(8,128)(2,1)S(1)}, bf16[512,256]{1,0:T(8,128)(2,1)S(1)}, u32[]{:S(2)}, u32[]{:S(2)}) collective-permute-start(bf16[512,256]{1,0:T(8,128)(2,1)S(1)} %get-tuple-element.60), channel_id=1, source_target_pairs={{0,4},{1,17},{2,6},{3,19},{4,0},{5,21},{6,2},{7,23},{8,12},{9,25},... | collective-permute-start | bytes 786440 | tf_op jit(solution)/shard_map/ppermute | solution.py:37
  65.0 48.6 %copy-start.3 = (f32[128,1024]{1,0:T(8,128)S(1)}, f32[128,1024]{1,0:T(8,128)}, u32[]{:S(2)}) copy-start(f32[128,1024]{1,0:T(8,128)} %param.10) | copy-start | bytes 1572868
  65.0 10.7 %collective-permute-start.20 = (bf16[512,256]{1,0:T(8,128)(2,1)S(1)}, bf16[512,256]{1,0:T(8,128)(2,1)S(1)}, u32[]{:S(2)}, u32[]{:S(2)}) collective-permute-start(bf16[512,256]{1,0:T(8,128)(2,1)S(1)} %get-tuple-element.62), channel_id=1, source_target_pairs={{0,6},{1,25},{2,0},{3,27},{4,2},{5,29},{6,4},{7,31},{8,14},{9,1},{... | collective-permute-start | bytes 786440 | tf_op jit(solution)/shard_map/ppermute | solution.py:37
  69.2 7.4 %collective-permute-start.19 = (bf16[512,256]{1,0:T(8,128)(2,1)S(1)}, bf16[512,256]{1,0:T(8,128)(2,1)S(1)}, u32[]{:S(2)}, u32[]{:S(2)}) collective-permute-start(bf16[512,256]{1,0:T(8,128)(2,1)S(1)} %get-tuple-element.61), channel_id=1, source_target_pairs={{0,2},{1,9},{2,4},{3,11},{4,6},{5,13},{6,0},{7,15},{8,10},{9,17},{... | collective-permute-start | bytes 786440 | tf_op jit(solution)/shard_map/ppermute | solution.py:37
  76.8 1.4 %collective-permute-start.21 = (bf16[512,128]{1,0:T(8,128)(2,1)S(1)}, bf16[512,128]{1,0:T(8,128)(2,1)S(1)}, u32[]{:S(2)}, u32[]{:S(2)}) collective-permute-start(bf16[512,128]{1,0:T(8,128)(2,1)S(1)} %get-tuple-element.64), channel_id=1, source_target_pairs={{0,1},{1,0},{2,3},{3,2},{4,5},{5,4},{6,7},{7,6},{8,9},{9,8},{10,11... | collective-permute-start | bytes 393224 | tf_op jit(solution)/shard_map/ppermute | solution.py:37
